TPU v7x, 128 devices: a whole 4x4x4 slice. The times are simulated.
128 devices in a mesh: expert: 32 (over y, x, core), mp: 4 (over z).
Axes of the slice: x: 4, y: 4, z: 4, core: 2. Of those that a mesh axis runs over, the one named last changes fastest.
Arguments:
- tokens: bfloat16 [16384, 768], P(('expert', 'mp')), may hold values from -6 to 6
- gain_attn: float32 [768], replicated, may hold values from 0.5 to 1.5
- gain_moe: float32 [768], replicated, may hold values from 0.5 to 1.5
- qkv_weight: bfloat16 [768, 3, 768], P('expert', None, 'mp'), may hold values from -0.21875 to 0.21875
- proj_weight: bfloat16 [768, 768], P('mp', 'expert'), may hold values from -0.875 to 0.875
- bias_table: float32 [32, 12], P(None, 'mp'), may hold values from -4 to 4
- expert_in: bfloat16 [64, 768, 3072], P('expert', None, 'mp'), may hold values from -0.21875 to 0.21875
- expert_out: bfloat16 [64, 3072, 768], P('expert', 'mp'), may hold values from -0.4375 to 0.4375
- expert_ids: int32 [16384, 2], P(('expert', 'mp')), may hold values from 0 to 63, all different within a row; in each aligned block of 128 rows (0 to 127, 128 to 255, ...) at most 5 rows name the same one
- gate_values: float32 [16384, 2], P(('expert', 'mp')), may hold values from 0.5 to 1
- bucket_table: int32 [512], replicated, may hold values from 0 to 31
- cotangent: bfloat16 [16384, 768], P(('expert', 'mp')), may hold values from -6 to 6
Outputs:
- out: bfloat16 [16384, 768], P(('expert', 'mp'))
- input_grad: float32 [16384, 768], P(('expert', 'mp'))
- gain_attn_grad: float32 [768], P(('expert', 'mp'))
- gain_moe_grad: float32 [768], P(('expert', 'mp'))
- qkv_grad: float32 [768, 3, 768], P('expert', None, 'mp')
- proj_grad: float32 [768, 768], P('mp', 'expert')
- table_grad: float32 [32, 12], P('expert', 'mp')
- expert_in_grad: float32 [64, 768, 3072], P('expert', None, 'mp')
- expert_out_grad: float32 [64, 3072, 768], P('expert', 'mp')
Inputs may be any that keep to these rules, and one draw needn't show every extreme that they name: `expert_ids`: each row names 2 different experts. Among the 128 rows of one device no expert is named more than 5 times, a bound that some block reaches.
All inputs are finite; a program needn't handle non-finite values.
Results may differ from a plain program's by a relative error of at most 0.035.
Values may be sent and summed in bfloat16 or wider, within the bound.
A program may use at most 128 MiB of HBM per device.

v0:
```python
import jax
import jax.numpy as jnp
from jax import lax
from jax.sharding import PartitionSpec as P

HEAD_DIM = 64
TOPK = 2


epsilon = 1e-06
masked_value = -1e30
inv_root_two = 0.7071067811865476
inv_root_tau = 0.3989422804014327
highest = lax.Precision.HIGHEST


def contract_rows(left, right):
    return lax.dot_general(
        left, right, (((0,), (0,)), ((), ())), preferred_element_type=jnp.float32
    )


def contract_cols(left, right):
    return lax.dot_general(
        left, right, (((1,), (1,)), ((), ())), preferred_element_type=jnp.float32
    )


def fold_window(window, seq_len):
    return jnp.concatenate([window[:, :seq_len][:, ::-1], window[:, seq_len:][:, ::-1]], axis=1)


def body(
    tokens,
    gain_attn,
    gain_moe,
    qkv_weight,
    proj_weight,
    bias_table,
    expert_in,
    expert_out,
    expert_ids,
    gate_values,
    bucket_table,
    cotangent,
):
    expert_count = lax.axis_size("expert")
    mp_count = lax.axis_size("mp")
    tok_rows, model_width = tokens.shape
    local_experts = expert_in.shape[0]
    all_experts = local_experts * expert_count
    capacity = max(2, 5 * tok_rows * TOPK // (4 * all_experts))
    score_scale = HEAD_DIM ** (-0.5)
    inputs = tokens.astype(jnp.float32)
    scale_first = lax.rsqrt(jnp.mean(inputs * inputs, axis=1, keepdims=True) + epsilon)
    normal_first = inputs * scale_first
    unit_first = normal_first.astype(jnp.bfloat16)
    seq_units = lax.all_gather(unit_first, "mp", axis=0, tiled=True)
    qkv_full, proj_full = (
        lax.all_gather(qkv_weight, "expert", axis=0, tiled=True),
        lax.all_gather(proj_weight, "expert", axis=1, tiled=True),
    )
    seq_len = seq_units.shape[0]
    local_width = qkv_full.shape[2]
    local_heads = local_width // HEAD_DIM
    normed_first = (seq_units.astype(jnp.float32) * gain_attn).astype(jnp.bfloat16)
    qkv_flat = qkv_full.reshape(model_width, 3 * local_width)
    projected = jnp.dot(normed_first, qkv_flat, preferred_element_type=jnp.float32).astype(
        jnp.bfloat16
    )
    projected = projected.reshape(seq_len, 3, local_heads, HEAD_DIM)
    queries = projected[:, 0]
    key_rows = projected[:, 1]
    values = projected[:, 2]
    bucket_count = bias_table.shape[0]
    bucket_hot = (
        bucket_table[:, None] == jnp.arange(bucket_count, dtype=jnp.int32)[None, :]
    ).astype(jnp.float32)
    rel_heads = lax.dot_general(bias_table, bucket_hot, (((0,), (1,)), ((), ())), precision=highest)
    block_rows = min(512, seq_len)
    block_count = seq_len // block_rows
    period = seq_len + block_rows
    block_starts = jnp.arange(block_count, dtype=jnp.int32) * block_rows
    key_pos = jnp.arange(seq_len, dtype=jnp.int32)
    rel_padded = jnp.concatenate(
        [
            jnp.zeros((local_heads, seq_len - 1), jnp.float32),
            rel_heads,
            jnp.zeros((local_heads, block_rows), jnp.float32),
        ],
        axis=1,
    )

    def block_bias(row_start):
        window = lax.dynamic_slice_in_dim(rel_padded, row_start, period, 1)
        folded = fold_window(window, seq_len)
        tiled = jnp.tile(folded, (1, block_rows))[:, : block_rows * (period - 1)]
        return tiled.reshape(local_heads, block_rows, period - 1)[:, :, :seq_len]

    def block_logits(row_start):
        query_pos = row_start + jnp.arange(block_rows, dtype=jnp.int32)
        scores = (
            jnp.einsum("qhd,khd->hqk", queries, key_rows, preferred_element_type=jnp.float32)
            * score_scale
        )
        scores = scores + block_bias(row_start)
        causal = key_pos[None, :] <= query_pos[:, None]
        return (jnp.where(causal[None], scores, masked_value), queries)

    def forward_block(row_start):
        scores, query_block = block_logits(row_start)
        top_score = jnp.max(scores, axis=2, keepdims=True)
        raised = jnp.exp(scores - top_score)
        row_total = jnp.sum(raised, axis=2, keepdims=True)
        weights_p = (raised / row_total).astype(jnp.bfloat16)
        attended_block = jnp.einsum(
            "hqk,khd->qhd", weights_p, values, preferred_element_type=jnp.float32
        )
        return (
            attended_block.astype(jnp.bfloat16),
            top_score[:, :, 0] + jnp.log(row_total[:, :, 0]),
        )

    attended_blocks, log_totals = lax.map(forward_block, block_starts)
    attended = attended_blocks.reshape(seq_len, local_width)
    attn_out = lax.psum_scatter(
        jnp.dot(attended, proj_full, preferred_element_type=jnp.float32),
        "mp",
        scatter_dimension=0,
        tiled=True,
    )
    resid = inputs + attn_out
    scale_second = lax.rsqrt(jnp.mean(resid * resid, axis=1, keepdims=True) + epsilon)
    normal_second = resid * scale_second
    normed_second = (normal_second * gain_moe).astype(jnp.bfloat16)
    flat_ids = expert_ids.reshape(-1)
    expert_range = jnp.arange(all_experts, dtype=jnp.int32)
    id_hot = (flat_ids[:, None] == expert_range[None, :]).astype(jnp.int32)
    slot_index = jnp.sum((jnp.cumsum(id_hot, axis=0) - id_hot) * id_hot, axis=1).reshape(
        tok_rows, TOPK
    )
    dest_rows = expert_ids * capacity + slot_index
    buffer_pos = jnp.arange(all_experts * capacity, dtype=jnp.int32)
    selectors = [
        (buffer_pos[:, None] == dest_rows[None, :, route_slot]).astype(jnp.bfloat16)
        for route_slot in range(TOPK)
    ]

    def spread_rows(buffer_rows):
        shaped = buffer_rows.reshape(expert_count, 1, local_experts, capacity, model_width)
        widened = jnp.broadcast_to(
            shaped, (expert_count, mp_count, local_experts, capacity, model_width)
        )
        return widened.reshape(expert_count * mp_count, local_experts, capacity, model_width)

    send_rows = sum(
        (
            jnp.dot(selector, normed_second, preferred_element_type=jnp.float32)
            for selector in selectors
        )
    ).astype(jnp.bfloat16)
    received = lax.all_to_all(
        spread_rows(send_rows), ("expert", "mp"), split_axis=0, concat_axis=0, tiled=True
    )
    pre_act = jnp.einsum("sjcd,jdf->sjcf", received, expert_in, preferred_element_type=jnp.float32)
    normal_cdf = 0.5 * (1.0 + lax.erf(pre_act * inv_root_two))
    hidden = (pre_act * normal_cdf).astype(jnp.bfloat16)
    partial_out = jnp.einsum(
        "sjcf,jfd->sjcd", hidden, expert_out, preferred_element_type=jnp.float32
    )
    arrived = lax.all_to_all(partial_out, ("expert", "mp"), split_axis=0, concat_axis=0, tiled=True)
    summed = jnp.sum(
        arrived.reshape(expert_count, mp_count, local_experts, capacity, model_width), axis=1
    )
    expert_rows = summed.astype(jnp.bfloat16).reshape(all_experts * capacity, model_width)
    mixture = sum(
        (
            gate_values[:, route_slot, None] * contract_rows(selectors[route_slot], expert_rows)
            for route_slot in range(TOPK)
        )
    )
    result = resid + mixture
    grad_out = cotangent.astype(jnp.float32)
    grad_send = sum(
        (
            jnp.dot(
                selectors[route_slot],
                (gate_values[:, route_slot, None] * grad_out).astype(jnp.bfloat16),
                preferred_element_type=jnp.float32,
            )
            for route_slot in range(TOPK)
        )
    ).astype(jnp.bfloat16)
    grad_recv = lax.all_to_all(
        spread_rows(grad_send), ("expert", "mp"), split_axis=0, concat_axis=0, tiled=True
    )
    grad_hidden = jnp.einsum(
        "sjcd,jfd->sjcf", grad_recv, expert_out, preferred_element_type=jnp.float32
    )
    expert_out_grad = jnp.einsum(
        "sjcf,sjcd->jfd", hidden, grad_recv, preferred_element_type=jnp.float32
    )
    gelu_slope = normal_cdf + pre_act * jnp.exp(-0.5 * pre_act * pre_act) * inv_root_tau
    grad_pre = (grad_hidden * gelu_slope).astype(jnp.bfloat16)
    expert_in_grad = jnp.einsum(
        "sjcd,sjcf->jdf", received, grad_pre, preferred_element_type=jnp.float32
    )
    grad_partial = jnp.einsum(
        "sjcf,jdf->sjcd", grad_pre, expert_in, preferred_element_type=jnp.float32
    )
    grad_arrived = lax.all_to_all(
        grad_partial, ("expert", "mp"), split_axis=0, concat_axis=0, tiled=True
    )
    grad_summed = jnp.sum(
        grad_arrived.reshape(expert_count, mp_count, local_experts, capacity, model_width), axis=1
    )
    grad_rows = grad_summed.astype(jnp.bfloat16).reshape(all_experts * capacity, model_width)
    grad_normed = sum((contract_rows(selector, grad_rows) for selector in selectors))
    gain_second_part = jnp.sum(grad_normed * normal_second, axis=0)
    grad_unit_second = grad_normed * gain_moe
    grad_resid = grad_out + scale_second * (
        grad_unit_second
        - normal_second * jnp.mean(grad_unit_second * normal_second, axis=1, keepdims=True)
    )
    seq_grad = lax.all_gather(grad_resid.astype(jnp.bfloat16), "mp", axis=0, tiled=True)
    proj_grad_part = contract_rows(attended, seq_grad)
    grad_attended = (
        contract_cols(seq_grad, proj_full)
        .astype(jnp.bfloat16)
        .reshape(seq_len, local_heads, HEAD_DIM)
    )

    def bias_gradient(rel_acc, grad_scores, row_start):
        padded = jnp.concatenate(
            [grad_scores, jnp.zeros((local_heads, block_rows, period - 1 - seq_len), jnp.float32)],
            axis=2,
        )
        flat = jnp.concatenate(
            [
                padded.reshape(local_heads, block_rows * (period - 1)),
                jnp.zeros((local_heads, block_rows), jnp.float32),
            ],
            axis=1,
        )
        along = jnp.sum(flat.reshape(local_heads, block_rows, period), axis=1)
        window = lax.dynamic_slice_in_dim(rel_acc, row_start, period, 1) + fold_window(
            along, seq_len
        )
        return lax.dynamic_update_slice_in_dim(rel_acc, window, row_start, 1)

    def backward_block(carried, pieces):
        key_acc, value_acc, rel_acc = carried
        row_start, log_block = pieces
        scores, query_block = block_logits(row_start)
        softmax_rows = jnp.exp(scores - log_block[:, :, None])
        value_acc = value_acc + jnp.einsum(
            "hqk,qhd->khd",
            softmax_rows.astype(jnp.bfloat16),
            grad_attended,
            preferred_element_type=jnp.float32,
        )
        grad_weights = jnp.einsum(
            "qhd,khd->hqk", grad_attended, values, preferred_element_type=jnp.float32
        )
        row_dot = jnp.sum(softmax_rows * grad_weights, axis=2, keepdims=True)
        grad_scores = (softmax_rows * (grad_weights - row_dot)).astype(jnp.bfloat16)
        rel_acc = bias_gradient(rel_acc, grad_scores.astype(jnp.float32), row_start)
        key_acc = (
            key_acc
            + jnp.einsum(
                "hqk,qhd->khd", grad_scores, query_block, preferred_element_type=jnp.float32
            )
            * score_scale
        )
        grad_query = (
            jnp.einsum("hqk,khd->qhd", grad_scores, key_rows, preferred_element_type=jnp.float32)
            * score_scale
        )
        return ((key_acc, value_acc, rel_acc), grad_query)

    start_state = (
        jnp.zeros((seq_len, local_heads, HEAD_DIM), jnp.float32),
        jnp.zeros((seq_len, local_heads, HEAD_DIM), jnp.float32),
        jnp.zeros((local_heads, seq_len - 1 + period), jnp.float32),
    )
    final_state, query_grads = lax.scan(backward_block, start_state, (block_starts, log_totals))
    key_grad, value_grad, rel_total = final_state
    rel_grad = rel_total[:, seq_len - 1 : 2 * seq_len - 1]
    grad_qkv = jnp.stack(
        [query_grads.reshape(seq_len, local_heads, HEAD_DIM), key_grad, value_grad], axis=1
    )
    grad_qkv = grad_qkv.astype(jnp.bfloat16).reshape(seq_len, 3 * local_width)
    qkv_grad_part = contract_rows(normed_first, grad_qkv).reshape(model_width, 3, local_width)
    grad_normed_first = contract_cols(grad_qkv, qkv_flat)
    table_grad_part = lax.dot_general(
        bucket_hot, rel_grad, (((0,), (1,)), ((), ())), precision=highest
    )
    gain_first_part = jnp.sum(grad_normed_first * seq_units.astype(jnp.float32), axis=0)
    grad_unit_seq = grad_normed_first * gain_attn
    gain_piece = model_width // (expert_count * mp_count)
    gain_parts = (
        jnp.stack([gain_first_part, gain_second_part])
        .reshape(2, expert_count, mp_count, gain_piece)
        .transpose(2, 0, 1, 3)
    )
    grad_unit, gain_mp = (
        lax.psum_scatter(grad_unit_seq, "mp", scatter_dimension=0, tiled=True),
        lax.psum_scatter(gain_parts, "mp", scatter_dimension=0, tiled=True),
    )
    grad_input = grad_resid + scale_first * (
        grad_unit - normal_first * jnp.mean(grad_unit * normal_first, axis=1, keepdims=True)
    )
    qkv_grad, proj_grad, table_grad, gain_grads = (
        lax.psum_scatter(qkv_grad_part, "expert", scatter_dimension=0, tiled=True),
        lax.psum_scatter(proj_grad_part, "expert", scatter_dimension=1, tiled=True),
        lax.psum_scatter(table_grad_part, "expert", scatter_dimension=0, tiled=True),
        lax.psum_scatter(gain_mp, "expert", scatter_dimension=2, tiled=True),
    )
    return (
        result.astype(jnp.bfloat16),
        grad_input,
        gain_grads[0, 0, 0],
        gain_grads[0, 1, 0],
        qkv_grad,
        proj_grad,
        table_grad,
        expert_in_grad,
        expert_out_grad,
    )


def solution(mesh):
    placed = (
        P(("expert", "mp"), None),
        P(),
        P(),
        P("expert", None, "mp"),
        P("mp", "expert"),
        P(None, "mp"),
        P("expert", None, "mp"),
        P("expert", "mp", None),
        P(("expert", "mp"), None),
        P(("expert", "mp"), None),
        P(),
        P(("expert", "mp"), None),
    )
    return jax.shard_map(
        body,
        mesh=mesh,
        in_specs=placed,
        out_specs=(
            P(("expert", "mp"), None),
            P(("expert", "mp"), None),
            P(("expert", "mp")),
            P(("expert", "mp")),
            P("expert", None, "mp"),
            P("mp", "expert"),
            P("expert", "mp"),
            P("expert", None, "mp"),
            P("expert", "mp", None),
        ),
        check_vma=False,
    )
```

profile of v0, /device:TPU:0, one launch (start us, length us, event | category | flops | bytes accessed | tf_op | source)
XLA Modules:
  0.0 559.0 jit_solution(16600963385327479604)
XLA Ops:
  10.1 7.5 %copy.193 = f32[1,3,512,1024]{3,1,2,0:T(4,128)} copy(f32[1,3,512,1024]{3,2,1,0:T(8,128)S(1)} %broadcast_bitcast_fusion) | data formatting | bytes 12582912
  17.6 7.7 %slice.97 = f32[3,523776]{1,0:T(4,128)} slice(f32[3,524288]{1,0:T(4,128)} %bitcast.169), slice={[0:3], [0:523776]} | slice | bytes 12570624 | tf_op jit(solution)/shard_map/while/body/eval_jaxpr/slice | solution.py:97
  25.3 13.2 %reshape.168 = f32[3,512,1023]{2,1,0:T(8,128)} reshape(f32[3,523776]{1,0:T(4,128)} %slice.97) | data formatting | bytes 12570624 | tf_op jit(solution)/shard_map/while/body/eval_jaxpr/reshape | solution.py:98
  38.5 3.9 slice.98
  42.3 3.5 copy.190
  45.9 28.0 %all_gather.13 = bf16[768,3,192]{2,0,1:T(8,128)(2,1)} all-gather(bf16[24,3,192]{2,0,1:T(8,128)(2,1)S(1)} %copy-done.19), channel_id=1, replica_groups=mesh['expert'=32,'mp'=4] {'expert'}, dimensions={0}, use_global_device_ids=true | all-gather | bytes 912384 | tf_op jit(solution)/shard_map/all_gather | solution.py:60
  73.9 2.3 copy.150
  76.4 15.2 %all_gather.12 = bf16[512,768]{1,0:T(8,128)(2,1)S(1)} all-gather(bf16[128,768]{1,0:T(8,128)(2,1)S(1)} %fusion.53), channel_id=1, replica_groups=mesh['expert'=32,'mp'=4] {'mp'}, dimensions={0}, use_global_device_ids=true | all-gather | bytes 983040 | tf_op jit(solution)/shard_map/all_gather | solution.py:58
  91.6 2.1 convolution_convert_fusion
  96.4 24.9 %all_gather.14 = bf16[192,768]{0,1:T(8,128)(2,1)S(1)} all-gather(bf16[192,24]{0,1:T(8,128)(2,1)S(1)} %copy-done.30), channel_id=1, replica_groups=mesh['expert'=32,'mp'=4] {'expert'}, dimensions={1}, use_global_device_ids=true | all-gather | bytes 304128 | tf_op jit(solution)/shard_map/all_gather | solution.py:61
  121.3 1.6 fusion.91
  124.6 23.2 %reduce-scatter.5.cloned.1.call-done = f32[128,768]{1,0:T(8,128)} async-done(((f32[512,768]{1,0:T(8,128)}), f32[128,768]{1,0:T(8,128)}) %reduce-scatter.5.cloned.1.call-update) | async-done | bytes 393232 | tf_op jit(solution)/shard_map/reduce_scatter | solution.py:126
  150.5 2.1 broadcast_in_dim.87
  154.1 2.3 broadcast_in_dim.88
  156.4 8.8 %all-to-all-start = ((bf16[128,2,5,768]{3,1,2,0:T(2,128)(2,1)}), bf16[128,2,5,768]{3,1,2,0:T(2,128)(2,1)}, u32[]{:S(2)}, u32[]{:S(2)}) async-start(bf16[128,2,5,768]{3,1,2,0:T(2,128)(2,1)} %bitcast.170), calls=%async_computation.1 | async-start | bytes 3932160 | tf_op jit(solution)/shard_map/all_to_all | solution.py:162
  167.6 2.1 broadcast_in_dim.89
  169.8 2.3 copy.162
  172.1 21.2 %all-to-all-done = bf16[128,2,5,768]{3,1,2,0:T(2,128)(2,1)} async-done(((bf16[128,2,5,768]{3,1,2,0:T(2,128)(2,1)}), bf16[128,2,5,768]{3,1,2,0:T(2,128)(2,1)}, u32[]{:S(2)}, u32[]{:S(2)}) %all-to-all-start) | async-done | bytes 1966112 | tf_op jit(solution)/shard_map/all_to_all | solution.py:162
  193.2 3.3 broadcast_in_dim.90
  196.5 5.9 %all-to-all-start.2 = ((bf16[128,2,5,768]{3,1,2,0:T(2,128)(2,1)}), bf16[128,2,5,768]{3,1,2,0:T(2,128)(2,1)}, u32[]{:S(2)}, u32[]{:S(2)}) async-start(bf16[128,2,5,768]{3,1,2,0:T(2,128)(2,1)} %bitcast.171), calls=%async_computation.3 | async-start | bytes 3932160 | tf_op jit(solution)/shard_map/all_to_all | solution.py:194
  202.4 6.7 %copy.174 = bf16[128,2,5,768]{0,3,2,1:T(8,128)(2,1)} copy(bf16[128,2,5,768]{3,1,2,0:T(2,128)(2,1)} %all-to-all-done) | data formatting | bytes 3932160 | tf_op jit(solution)/shard_map/all_to_all | solution.py:162
  209.2 5.9 %fusion.9 = (bf16[128,2,5,768]{3,0,2,1:T(8,128)(2,1)}, f32[2,128,5,768]{3,1,2,0:T(8,128)}) fusion(bf16[128,2,5,768]{0,3,2,1:T(8,128)(2,1)} %copy.174, bf16[2,768,768]{2,1,0:T(8,128)(2,1)S(1)} %copy-done), kind=kOutput, calls=%fused_computation.16 | convolution fusion | flops 1514864640 | bytes 10223616 | tf_op jit(solution)/shard_map/sjcd,jdf->sjcf/dot_general | solution.py:165
  215.1 15.4 %all-to-all-done.2 = bf16[128,2,5,768]{3,1,2,0:T(2,128)(2,1)} async-done(((bf16[128,2,5,768]{3,1,2,0:T(2,128)(2,1)}), bf16[128,2,5,768]{3,1,2,0:T(2,128)(2,1)}, u32[]{:S(2)}, u32[]{:S(2)}) %all-to-all-start.2) | async-done | bytes 1966112 | tf_op jit(solution)/shard_map/all_to_all | solution.py:194
  230.5 5.3 fusion.5
  237.1 1.7 fusion.23
  238.8 5.0 copy.164
  243.8 5.9 %all-to-all-start.3 = ((f32[128,2,5,768]{3,1,2,0:T(2,128)}), f32[128,2,5,768]{3,1,2,0:T(2,128)}, u32[]{:S(2)}, u32[]{:S(2)}) async-start(f32[128,2,5,768]{3,1,2,0:T(2,128)} %copy.164), calls=%async_computation.4 | async-start | bytes 7864320 | tf_op jit(solution)/shard_map/all_to_all | solution.py:211
  249.8 48.7 %all-to-all-done.3 = f32[128,2,5,768]{3,1,2,0:T(2,128)} async-done(((f32[128,2,5,768]{3,1,2,0:T(2,128)}), f32[128,2,5,768]{3,1,2,0:T(2,128)}, u32[]{:S(2)}, u32[]{:S(2)}) %all-to-all-start.3) | async-done | bytes 3932192 | tf_op jit(solution)/shard_map/all_to_all | solution.py:211
  298.5 3.8 bitcast_reduce_fusion.1
  303.9 14.9 %all_gather.15 = bf16[512,768]{1,0:T(8,128)(2,1)S(1)} all-gather(bf16[128,768]{1,0:T(8,128)(2,1)S(1)} %fusion.88), channel_id=1, replica_groups=mesh['expert'=32,'mp'=4] {'mp'}, dimensions={0}, use_global_device_ids=true | all-gather | bytes 983040 | tf_op jit(solution)/shard_map/all_gather | solution.py:225
  322.9 2.0 fusion.31
  327.4 3.9 fusion.20
  331.3 4.9 copy.159
  336.2 5.8 %all-to-all-start.1 = ((f32[128,2,5,768]{3,1,2,0:T(2,128)}), f32[128,2,5,768]{3,1,2,0:T(2,128)}, u32[]{:S(2)}, u32[]{:S(2)}) async-start(f32[128,2,5,768]{3,1,2,0:T(2,128)} %copy.159), calls=%async_computation.2 | async-start | bytes 7864320 | tf_op jit(solution)/shard_map/all_to_all | solution.py:171
  342.5 6.5 %convolution_bitcast_fusion.1 = f32[2,768,768]{2,1,0:T(8,128)} fusion(bf16[128,2,5,768]{0,3,2,1:T(8,128)(2,1)} %copy.174, bf16[128,2,5,768]{3,0,2,1:T(8,128)(2,1)} %copy-done.44), kind=kOutput, calls=%fused_computation.35 | convolution fusion | flops 1509949440 | bytes 8650752 | tf_op jit(solution)/shard_map/sjcd,sjcf->jdf/dot_general | solution.py:205
  348.9 5.8 %convolution_bitcast_fusion = f32[2,768,768]{2,1,0:T(8,128)} fusion(bf16[128,2,5,768]{3,0,2,1:T(8,128)(2,1)S(1)} %copy-done.43, bf16[128,2,5,768]{3,1,2,0:T(2,128)(2,1)} %all-to-all-done.2), kind=kOutput, calls=%fused_computation.34 | convolution fusion | flops 1509949440 | bytes 8650752 | tf_op jit(solution)/shard_map/sjcf,sjcd->jfd/dot_general | solution.py:200
  354.7 1.6 copy.191
  356.3 3.5 concatenate.29.clone
  359.8 7.0 %reshape.192 = bf16[1571328]{0:T(1024)(128)(2,1)} reshape(bf16[3,512,1023]{2,1,0:T(8,128)(2,1)} %concatenate.29.clone) | data formatting | bytes 6285312
  366.8 5.6 %reshape.177 = bf16[3,523776]{1,0:T(4,128)(2,1)} reshape(bf16[1571328]{0:T(1024)(128)(2,1)} %reshape.192) | data formatting | bytes 6285312 | tf_op jit(solution)/shard_map/while/body/eval_jaxpr/reshape | solution.py:240
  374.0 6.6 %pad_convert_fusion = f32[3,524288]{1,0:T(4,128)} fusion(bf16[3,523776]{1,0:T(4,128)(2,1)} %reshape.177), kind=kLoop, calls=%fused_computation.2 | loop fusion | flops 1572864 | bytes 9434112 | tf_op jit(solution)/shard_map/while/body/eval_jaxpr/reshape | solution.py:245
  380.6 2.3 fusion.47
  382.9 7.9 %all-to-all-done.1 = f32[128,2,5,768]{3,1,2,0:T(2,128)} async-done(((f32[128,2,5,768]{3,1,2,0:T(2,128)}), f32[128,2,5,768]{3,1,2,0:T(2,128)}, u32[]{:S(2)}, u32[]{:S(2)}) %all-to-all-start.1) | async-done | bytes 3932192 | tf_op jit(solution)/shard_map/all_to_all | solution.py:171
  390.8 3.8 bitcast_reduce_fusion.2
  395.7 16.0 %all-reduce.4 = f32[4,2,32,6]{2,1,3,0:T(2,128)S(1)} all-reduce(f32[4,2,32,6]{2,1,3,0:T(2,128)S(1)} %copy.170), channel_id=4, replica_groups=mesh['expert'=32,'mp'=4] {'mp'}, use_global_device_ids=true, to_apply=%region_16.17.clone | all-reduce | flops 1536 | bytes 12288
  412.5 6.9 %bitcast_reduce_fusion = f32[3,1024]{1,0:T(4,128)S(1)} fusion(f32[1,3,512,1024]{3,1,2,0:T(4,128)} %bitcast.168), kind=kLoop, calls=%fused_computation | loop fusion | flops 1569792 | bytes 6303744 | tf_op jit(solution)/shard_map/while/body/eval_jaxpr/reduce_sum | solution.py:245
  420.6 124.0 %all-reduce.7 = (f32[1,2,32,6]{3,1,0,2:T(2,128)}, f32[32,3]{1,0:T(8,128)S(1)}) all-reduce(f32[1,2,32,6]{3,1,0,2:T(2,128)S(1)} %copy.171, f32[32,3]{1,0:T(8,128)S(1)} %fusion.70), channel_id=5, replica_groups=mesh['expert'=32,'mp'=4] {'expert'}, use_global_device_ids=true, to_apply=%region_17.18.clone | all-reduce | flops 480 | bytes 3840
  550.1 2.1 fusion.57
  (173 shorter events, 33.8 us)
Async XLA Ops:
  7.2 202.0 %copy-start = (bf16[2,768,768]{2,1,0:T(8,128)(2,1)S(1)}, bf16[2,768,768]{2,1,0:T(8,128)(2,1)}, u32[]{:S(2)}) copy-start(bf16[2,768,768]{2,1,0:T(8,128)(2,1)} %param.18) | copy-start | bytes 7077892
  7.2 140.6 %reduce-scatter.5.cloned.1.call-start = ((), (), s32[]{:S(2)}) async-start(), calls=%async_computation.8 | async-start | bytes 1966080 | tf_op jit(solution)/shard_map/reduce_scatter | solution.py:126
  42.3 3.6 copy-start.19
  45.9 30.3 %copy-start.5 = (bf16[128,768]{1,0:T(8,128)(2,1)S(1)}, bf16[128,768]{1,0:T(8,128)(2,1)}, u32[]{:S(2)}) copy-start(bf16[128,768]{1,0:T(8,128)(2,1)} %param.12) | copy-start | bytes 589828
  45.9 45.7 %copy-start.38 = (f32[768]{0:T(1024)S(1)}, f32[768]{0:T(1024)}, u32[]{:S(2)}) copy-start(f32[768]{0:T(1024)} %param.13) | copy-start | bytes 9220
  76.2 17.6 %copy-start.4 = (f32[3,512,512]{1,2,0:T(8,128)S(1)}, f32[3,512,512]{1,2,0:T(8,128)}, u32[]{:S(2)}) copy-start(f32[3,512,512]{1,2,0:T(8,128)} %copy.190) | copy-start | bytes 9437188
  76.3 17.4 %copy-start.33 = (f32[128]{0:T(128)}, f32[128]{0:T(128)S(1)}, u32[]{:S(2)}) copy-start(f32[128]{0:T(128)S(1)} %add_rsqrt_fusion.1) | copy-start | bytes 1540
  91.6 2.1 copy-start.7
  93.8 1.4 copy-start.11
  94.7 1.7 copy-start.2
  94.7 1.7 copy-start.17
  95.2 1.2 copy-start.20
  96.4 28.1 %copy-start.14 = (bf16[3,64,512]{2,1,0:T(8,128)(2,1)}, bf16[3,64,512]{2,1,0:T(8,128)(2,1)S(1)}, u32[]{:S(2)}) copy-start(bf16[3,64,512]{2,1,0:T(8,128)(2,1)S(1)} %fusion.46) | copy-start | bytes 589828
  96.4 26.5 %copy-start.37 = (s32[128,2]{0,1:T(2,128)S(1)}, s32[128,2]{0,1:T(2,128)}, u32[]{:S(2)}) copy-start(s32[128,2]{0,1:T(2,128)} %param.20) | copy-start | bytes 3076
  96.4 52.5 %copy-start.16 = (f32[768]{0:T(1024)S(1)}, f32[768]{0:T(1024)}, u32[]{:S(2)}) copy-start(f32[768]{0:T(1024)} %param.14) | copy-start | bytes 9220
  124.5 41.8 %copy-start.27 = (s32[128]{0:T(128)}, s32[128]{0:T(128)S(1)}, u32[]{:S(2)}) copy-start(s32[128]{0:T(128)S(1)} %get-tuple-element.85) | copy-start | bytes 1540
  124.5 178.4 %copy-start.22 = (s32[128]{0:T(128)}, s32[128]{0:T(128)S(1)}, u32[]{:S(2)}) copy-start(s32[128]{0:T(128)S(1)} %get-tuple-element.86) | copy-start | bytes 1540
  148.9 3.6 copy-start.24
  154.1 11.8 %copy-start.10 = (bf16[128,768]{1,0:T(8,128)(2,1)S(1)}, bf16[128,768]{1,0:T(8,128)(2,1)}, u32[]{:S(2)}) copy-start(bf16[128,768]{1,0:T(8,128)(2,1)} %param.23) | copy-start | bytes 589828
  156.4 36.9 %all-to-all-start = ((bf16[128,2,5,768]{3,1,2,0:T(2,128)(2,1)}), bf16[128,2,5,768]{3,1,2,0:T(2,128)(2,1)}, u32[]{:S(2)}, u32[]{:S(2)}) async-start(bf16[128,2,5,768]{3,1,2,0:T(2,128)(2,1)} %bitcast.170), calls=%async_computation.1 | async-start | bytes 3932160 | tf_op jit(solution)/shard_map/all_to_all | solution.py:162
  165.9 30.6 %copy-start.31 = (f32[128]{0:T(128)}, f32[128]{0:T(128)S(1)}, u32[]{:S(2)}) copy-start(f32[128]{0:T(128)S(1)} %get-tuple-element.83) | copy-start | bytes 1540
  196.5 34.0 %all-to-all-start.2 = ((bf16[128,2,5,768]{3,1,2,0:T(2,128)(2,1)}), bf16[128,2,5,768]{3,1,2,0:T(2,128)(2,1)}, u32[]{:S(2)}, u32[]{:S(2)}) async-start(bf16[128,2,5,768]{3,1,2,0:T(2,128)(2,1)} %bitcast.171), calls=%async_computation.3 | async-start | bytes 3932160 | tf_op jit(solution)/shard_map/all_to_all | solution.py:194
  235.9 1.3 copy-start.44
  243.8 5.9 %copy-start.18 = (f32[3,512]{1,0:T(4,128)S(1)}, f32[3,512]{1,0:T(4,128)}, u32[]{:S(2)}) copy-start(f32[3,512]{1,0:T(4,128)} %copy-done.17) | copy-start | bytes 18436
  243.8 6.0 %copy-start.21 = (f32[3,512]{1,0:T(4,128)S(1)}, f32[3,512]{1,0:T(4,128)}, u32[]{:S(2)}) copy-start(f32[3,512]{1,0:T(4,128)} %copy-done.20) | copy-start | bytes 18436
  243.8 54.7 %all-to-all-start.3 = ((f32[128,2,5,768]{3,1,2,0:T(2,128)}), f32[128,2,5,768]{3,1,2,0:T(2,128)}, u32[]{:S(2)}, u32[]{:S(2)}) async-start(f32[128,2,5,768]{3,1,2,0:T(2,128)} %copy.164), calls=%async_computation.4 | async-start | bytes 7864320 | tf_op jit(solution)/shard_map/all_to_all | solution.py:211
  249.7 299.2 %reduce-scatter.7.cloned.1.call-start = ((), (), s32[]{:S(2)}) async-start(), calls=%async_computation.9 | async-start | bytes 1966080 | tf_op jit(solution)/shard_map/reduce_scatter | solution.py:307
  302.9 16.3 %copy-start.3 = (f32[3,512,512]{1,2,0:T(8,128)S(1)}, f32[3,512,512]{1,2,0:T(8,128)}, u32[]{:S(2)}) copy-start(f32[3,512,512]{1,2,0:T(8,128)} %copy-done.2) | copy-start | bytes 9437188
  303.7 16.2 %copy-start.6 = (f32[128,768]{1,0:T(8,128)}, f32[128,768]{1,0:T(8,128)S(1)}, u32[]{:S(2)}) copy-start(f32[128,768]{1,0:T(8,128)S(1)} %get-tuple-element.91) | copy-start | bytes 1179652
  303.7 16.2 %copy-start.40 = (f32[128]{0:T(128)}, f32[128]{0:T(128)S(1)}, u32[]{:S(2)}) copy-start(f32[128]{0:T(128)S(1)} %broadcast_multiply_fusion.2) | copy-start | bytes 1540
  303.9 16.0 %copy-start.12 = (bf16[512,576]{0,1:T(8,128)(2,1)S(1)}, bf16[512,576]{0,1:T(8,128)(2,1)}, u32[]{:S(2)}) copy-start(bf16[512,576]{0,1:T(8,128)(2,1)} %copy-done.11) | copy-start | bytes 1769476
  321.5 1.4 copy-start.13
  321.5 1.4 copy-start.39
  336.2 54.6 %all-to-all-start.1 = ((f32[128,2,5,768]{3,1,2,0:T(2,128)}), f32[128,2,5,768]{3,1,2,0:T(2,128)}, u32[]{:S(2)}, u32[]{:S(2)}) async-start(f32[128,2,5,768]{3,1,2,0:T(2,128)} %copy.159), calls=%async_computation.2 | async-start | bytes 7864320 | tf_op jit(solution)/shard_map/all_to_all | solution.py:171
  342.0 210.3 %reduce-scatter.11.cloned.1.call-start = ((), (), s32[]{:S(2)}) async-start(), calls=%async_computation.11 | async-start | bytes 811008 | tf_op jit(solution)/shard_map/reduce_scatter | solution.py:315
  342.5 6.5 %copy-start.43 = (bf16[128,2,5,768]{3,0,2,1:T(8,128)(2,1)S(1)}, bf16[128,2,5,768]{3,0,2,1:T(8,128)(2,1)}, u32[]{:S(2)}) copy-start(bf16[128,2,5,768]{3,0,2,1:T(8,128)(2,1)} %get-tuple-element.89) | copy-start | bytes 5898244
  366.8 5.6 %copy-start.15 = (bf16[3,64,512]{2,1,0:T(8,128)(2,1)S(1)}, bf16[3,64,512]{2,1,0:T(8,128)(2,1)}, u32[]{:S(2)}) copy-start(bf16[3,64,512]{2,1,0:T(8,128)(2,1)} %copy-done.14) | copy-start | bytes 589828
  373.8 6.8 %copy-start.9 = (bf16[512,768]{1,0:T(8,128)(2,1)S(1)}, bf16[512,768]{1,0:T(8,128)(2,1)}, u32[]{:S(2)}) copy-start(bf16[512,768]{1,0:T(8,128)(2,1)} %copy-done.7) | copy-start | bytes 2359300
  373.8 178.5 %reduce-scatter.9.cloned.1.call-start = ((), (), s32[]{:S(2)}) async-start(), calls=%async_computation.10 | async-start | bytes 2433024 | tf_op jit(solution)/shard_map/reduce_scatter | solution.py:314
  412.5 7.7 %copy-start.42 = (s32[512]{0:T(512)S(1)}, s32[512]{0:T(512)}, u32[]{:S(2)}) copy-start(s32[512]{0:T(512)} %param.22) | copy-start | bytes 6148
  412.5 135.0 %copy-start.29 = (s32[128]{0:T(128)S(1)}, s32[128]{0:T(128)}, u32[]{:S(2)}) copy-start(s32[128]{0:T(128)} %copy-done.27) | copy-start | bytes 1540
  412.5 135.0 %copy-start.36 = (f32[128]{0:T(128)S(1)}, f32[128]{0:T(128)}, u32[]{:S(2)}) copy-start(f32[128]{0:T(128)} %copy-done.35) | copy-start | bytes 1540
  412.5 135.4 %copy-start.23 = (s32[128]{0:T(128)S(1)}, s32[128]{0:T(128)}, u32[]{:S(2)}) copy-start(s32[128]{0:T(128)} %copy-done.22) | copy-start | bytes 1540
  412.5 135.4 %copy-start.32 = (f32[128]{0:T(128)S(1)}, f32[128]{0:T(128)}, u32[]{:S(2)}) copy-start(f32[128]{0:T(128)} %copy-done.31) | copy-start | bytes 1540
  412.5 136.4 %copy-start.34 = (f32[128]{0:T(128)S(1)}, f32[128]{0:T(128)}, u32[]{:S(2)}) copy-start(f32[128]{0:T(128)} %copy-done.33) | copy-start | bytes 1540
  412.5 139.8 %copy-start.1 = (bf16[2,768,768]{2,1,0:T(8,128)(2,1)S(1)}, bf16[2,768,768]{2,1,0:T(8,128)(2,1)}, u32[]{:S(2)}) copy-start(bf16[2,768,768]{2,1,0:T(8,128)(2,1)} %param.18) | copy-start | bytes 7077892
  419.4 130.7 %copy-start.26 = (f32[128]{0:T(128)S(1)}, f32[128]{0:T(128)}, u32[]{:S(2)}) copy-start(f32[128]{0:T(128)} %copy-done.24) | copy-start | bytes 1540
  419.4 130.7 %copy-start.41 = (f32[128]{0:T(128)S(1)}, f32[128]{0:T(128)}, u32[]{:S(2)}) copy-start(f32[128]{0:T(128)} %copy-done.40) | copy-start | bytes 1540
  (5 other events, 4.8 us)
Sparse Core Ops, SparseCore 0:
  123.0 24.7 reduce-scatter.4
  325.0 63.7 reduce-scatter.6
  392.8 76.9 reduce-scatter.10
  473.8 78.4 reduce-scatter.8
where the time goes:
time: 565 us; the launch traced here: 559 us
  blocking collectives  223 us (39%)
  waiting for transfers between devices  117 us (21%)
  local copies, waits for them, and re-layouts  100 us (18%)
  matrix products  49.4 us (9%)
  other arithmetic  28.3 us (5%)
  starting transfers between devices  27 us (5%)
  between operations  14.7 us (3%)
    unnamed x2, blocking collectives  140 us
    all_to_all x1, waiting for transfers between devices, body(): lax.all_to_all(grad_partial, ('expert', 'mp'), split_axis=0, concat_axis=...  48.7 us
    unnamed x103, local copies, waits for them, and re-layouts  28.8 us
    all_gather x1, blocking collectives, body(): lax.all_gather(qkv_weight, 'expert', axis=0, tiled=True)  28 us
    all_gather x1, blocking collectives, body(): lax.all_gather(proj_weight, 'expert', axis=1, tiled=True)  24.9 us
    reduce_scatter x1, waiting for transfers between devices, body(): lax.psum_scatter(jnp.dot(attended, proj_full, preferred_element_type=jnp....  23.2 us
    all_to_all x1, waiting for transfers between devices, body(): lax.all_to_all(spread_rows(send_rows), ('expert', 'mp'), split_axis=0, co...  21.2 us
    all_to_all x1, waiting for transfers between devices, body(): lax.all_to_all(spread_rows(grad_send), ('expert', 'mp'), split_axis=0, co...  15.4 us
  transfers between devices with their start and end apart: 8, of which 5 were waited for; matrix products, arithmetic and copies ran while one was open for 17% of the time, Pallas kernels for 0%

commit v1 on v0

--- a/solution.py
+++ b/solution.py
@@ -1,6 +1,8 @@
 import jax
 import jax.numpy as jnp
 from jax import lax
+from jax.experimental import pallas as pl
+from jax.experimental.pallas import tpu as pltpu
 from jax.sharding import PartitionSpec as P
 
 HEAD_DIM = 64
@@ -12,6 +14,408 @@
 inv_root_two = 0.7071067811865476
 inv_root_tau = 0.3989422804014327
 highest = lax.Precision.HIGHEST
+
+
+MESH = pl.DeviceIdType.MESH
+BLOCK = 16
+HALF = 80
+PLANE = 32
+RING = 4
+PAD = PLANE * BLOCK
+ROWS = 320
+EXPERT_ROWS = 640
+f32 = jnp.float32
+bf16 = jnp.bfloat16
+
+
+def place():
+    e, z = lax.axis_index("expert"), lax.axis_index("mp")
+    return e, z, lax.rem(z + 1, RING), lax.rem(z + RING - 1, RING)
+
+
+def plane_target(e, d):
+    step = d // 8
+    dy, dx, dc = lax.rem(step * 2, 4) + step // 2, lax.rem(d // 2, 4), lax.rem(d, 2)
+    y, x, c = e // 8, lax.rem(e // 2, 4), lax.rem(e, 2)
+    return lax.rem(y + dy, 4) * 8 + lax.rem(x + dx, 4) * 2 + lax.rem(c + dc, 2)
+
+
+def plane_source(e, d):
+    step = d // 8
+    dy, dx, dc = lax.rem(step * 2, 4) + step // 2, lax.rem(d // 2, 4), lax.rem(d, 2)
+    y, x, c = e // 8, lax.rem(e // 2, 4), lax.rem(e, 2)
+    return lax.rem(y + 4 - dy, 4) * 8 + lax.rem(x + 4 - dx, 4) * 2 + lax.rem(c + dc, 2)
+
+
+def block_at(index):
+    return pl.ds(pl.multiple_of(index * BLOCK, BLOCK), BLOCK)
+
+
+def greet(plane, ring):
+    e, z, right, left = place()
+    barrier = pltpu.get_barrier_semaphore()
+    if plane:
+
+        def signal(d, carry):
+            pl.semaphore_signal(
+                barrier, inc=1, device_id=(plane_target(e, d), z), device_id_type=MESH
+            )
+            return carry
+
+        lax.fori_loop(1, PLANE, signal, 0)
+    if ring:
+        for other in (right, left):
+            pl.semaphore_signal(barrier, inc=1, device_id=(e, other), device_id_type=MESH)
+    pl.semaphore_wait(barrier, (PLANE - 1) * plane + 2 * ring)
+
+
+def drain(ref, sem):
+    pltpu.make_async_copy(ref, ref, sem).wait()
+
+
+def dot(left, right):
+    return jnp.dot(left, right, preferred_element_type=f32)
+
+
+def dot_rows(left, right):
+    return lax.dot_general(left, right, (((0,), (0,)), ((), ())), preferred_element_type=f32)
+
+
+def dot_cols(left, right):
+    return lax.dot_general(left, right, (((1,), (1,)), ((), ())), preferred_element_type=f32)
+
+
+def packer():
+    row = lax.broadcasted_iota(jnp.int32, (2 * HALF, 256), 0)
+    col = lax.broadcasted_iota(jnp.int32, (2 * HALF, 256), 1)
+    expert = (row >= HALF).astype(jnp.int32)
+    inner = row - expert * HALF
+    source = (inner * 205) // 1024
+    slot = inner - source * 5
+    return (col == source * BLOCK + expert * 5 + slot).astype(bf16)
+
+
+class Dispatch:
+    def __init__(self, send, landed, rows, sems):
+        self.send, self.landed, self.rows = send, landed, rows
+        self.plane_out, self.plane_in, self.ring_out, self.ring_in = sems
+
+    def part(self, slot, half):
+        return self.rows.at[:, pl.ds(slot * 160 + half * HALF, HALF)]
+
+    def cross(self):
+        e, z, right, left = place()
+
+        def send(d, carry):
+            other = plane_target(e, d)
+            pltpu.make_async_remote_copy(
+                self.send.at[block_at(other)],
+                self.landed.at[block_at(d)],
+                self.plane_out,
+                self.plane_in.at[d // 16],
+                device_id=(other, z),
+                device_id_type=MESH,
+            ).start()
+            return carry
+
+        lax.fori_loop(1, PLANE, send, 0)
+        self.landed[0:BLOCK] = self.send[block_at(e)]
+
+    def copy(self, index, source, target, other):
+        e = lax.axis_index("expert")
+        return pltpu.make_async_remote_copy(
+            source,
+            target,
+            self.ring_out.at[index],
+            self.ring_in.at[index],
+            device_id=(e, other),
+            device_id_type=MESH,
+        )
+
+    def copies(self):
+        e, z, right, left = place()
+        part = self.part
+        return [
+            self.copy(0, part(0, 0), part(2, 0), right),
+            self.copy(1, part(0, 1), part(2, 1), right),
+            self.copy(2, part(0, 0), part(1, 0), left),
+            self.copy(3, part(0, 1), part(1, 1), left),
+            self.copy(4, part(2, 0), part(3, 0), right),
+            self.copy(5, part(1, 1), part(3, 1), left),
+        ]
+
+    def turn(self, half, pack):
+        lo = 256 * half
+        span = self.landed.at[pl.ds(lo + (BLOCK if half == 0 else 0), 256 - (BLOCK if half == 0 else 0))]
+        drain(span, self.plane_in.at[half])
+        packed = dot(pack, self.landed[lo : lo + 256]).astype(bf16)
+        for j in range(2):
+            self.rows[j, half * HALF : half * HALF + HALF] = packed[j * HALF : j * HALF + HALF]
+        ring = self.copies()
+        ring[half].start()
+        ring[2 + half].start()
+
+    def relay(self):
+        ring = self.copies()
+        ring[0].wait_recv()
+        ring[4].start()
+        ring[3].wait_recv()
+        ring[5].start()
+        ring[1].wait_recv()
+        ring[2].wait_recv()
+
+    def last(self):
+        ring = self.copies()
+        ring[4].wait_recv()
+        ring[5].wait_recv()
+
+    def close(self):
+        for copy in self.copies():
+            copy.wait_send()
+        drain(self.send.at[pl.ds(0, (PLANE - 1) * BLOCK)], self.plane_out)
+
+
+DISPATCH_SCRATCH = [
+    pltpu.SemaphoreType.DMA,
+    pltpu.SemaphoreType.DMA((2,)),
+    pltpu.SemaphoreType.DMA((6,)),
+    pltpu.SemaphoreType.DMA((6,)),
+]
+
+
+class Return:
+    def __init__(self, partial, relayed, landed, spread, home, sems):
+        self.partial, self.relayed, self.landed = partial, relayed, landed
+        self.spread, self.home = spread, home
+        self.ring_out, self.ring_in, self.plane_out, self.plane_in = sems
+
+    def part(self, slot, half):
+        return self.partial.at[:, pl.ds(slot * 160 + half * HALF, HALF)]
+
+    def copies(self):
+        e, z, right, left = place()
+
+        def copy(index, source, other):
+            return pltpu.make_async_remote_copy(
+                source,
+                self.landed.at[index],
+                self.ring_out.at[index],
+                self.ring_in.at[index],
+                device_id=(e, other),
+                device_id_type=MESH,
+            )
+
+        part = self.part
+        return [
+            copy(0, part(3, 0), right),
+            copy(1, part(3, 1), left),
+            copy(2, part(1, 1), right),
+            copy(3, part(2, 0), left),
+            copy(4, self.relayed.at[0], right),
+            copy(5, self.relayed.at[1], left),
+        ]
+
+    def near(self):
+        ring = self.copies()
+        ring[2].start()
+        ring[3].start()
+
+    def far(self):
+        ring = self.copies()
+        ring[0].start()
+        ring[1].start()
+
+    def add_far(self):
+        ring = self.copies()
+        for index, slot, half in ((0, 1, 0), (1, 2, 1)):
+            ring[index].wait_recv()
+            self.relayed[index] = (
+                self.part(slot, half)[...].astype(f32) + self.landed[index].astype(f32)
+            ).astype(bf16)
+            ring[4 + index].start()
+
+    def finish(self, half, pack):
+        e, z, right, left = place()
+        ring = self.copies()
+        direct, summed = (3, 4) if half == 0 else (2, 5)
+        ring[direct].wait_recv()
+        ring[summed].wait_recv()
+        total = (
+            self.part(0, half)[...].astype(f32)
+            + self.landed[direct].astype(f32)
+            + self.landed[summed].astype(f32)
+        ).astype(bf16)
+        flat = jnp.concatenate([total[0], total[1]], axis=0)
+        self.spread[256 * half : 256 * half + 256] = dot_rows(pack, flat).astype(bf16)
+
+        def send(d, carry):
+            pltpu.make_async_remote_copy(
+                self.spread.at[block_at(d)],
+                self.home.at[block_at(e)],
+                self.plane_out,
+                self.plane_in,
+                device_id=(plane_source(e, d), z),
+                device_id_type=MESH,
+            ).start()
+            return carry
+
+        lax.fori_loop(max(1, 16 * half), 16 * half + 16, send, 0)
+        if half == 0:
+            self.home[block_at(e)] = self.spread[0:BLOCK]
+
+    def arrive(self):
+        drain(self.home.at[pl.ds(0, (PLANE - 1) * BLOCK)], self.plane_in)
+
+    def close(self):
+        for copy in self.copies():
+            copy.wait_send()
+        drain(self.spread.at[pl.ds(0, (PLANE - 1) * BLOCK)], self.plane_out)
+
+
+RETURN_SCRATCH = [
+    pltpu.VMEM((2, 2, HALF, 768), bf16),
+    pltpu.VMEM((6, 2, HALF, 768), bf16),
+    pltpu.VMEM((PAD, 768), bf16),
+    pltpu.VMEM((PAD, 768), bf16),
+    pltpu.SemaphoreType.DMA((6,)),
+    pltpu.SemaphoreType.DMA((6,)),
+    pltpu.SemaphoreType.DMA,
+    pltpu.SemaphoreType.DMA,
+]
+
+
+def kernel_params(collective_id):
+    return pltpu.CompilerParams(
+        collective_id=collective_id, has_side_effects=True, vmem_limit_bytes=60 * 1024 * 1024
+    )
+
+
+VMEM = pl.BlockSpec(memory_space=pltpu.VMEM)
+
+
+def spread_kernel(send, rows, landed, *sems):
+    greet(1, 1)
+    work = Dispatch(send, landed, rows, sems)
+    work.cross()
+    pack = packer()
+    work.turn(0, pack)
+    work.turn(1, pack)
+    work.relay()
+    work.last()
+    work.close()
+
+
+def spread_rows(send):
+    return pl.pallas_call(
+        spread_kernel,
+        out_shape=jax.ShapeDtypeStruct((2, EXPERT_ROWS, 768), bf16),
+        in_specs=[VMEM],
+        out_specs=VMEM,
+        scratch_shapes=[pltpu.VMEM((PAD, 768), bf16)] + DISPATCH_SCRATCH,
+        compiler_params=kernel_params(1),
+        name="spread_cotangent",
+    )(send)
+
+
+def gather_kernel(partial, out, relayed, landed, spread, home, *sems):
+    greet(1, 1)
+    work = Return(partial, relayed, landed, spread, home, sems)
+    work.near()
+    work.far()
+    pack = packer()
+    work.add_far()
+    work.finish(0, pack)
+    work.finish(1, pack)
+    work.arrive()
+    out[...] = home[...]
+    work.close()
+
+
+def gather_rows(partial):
+    return pl.pallas_call(
+        gather_kernel,
+        out_shape=jax.ShapeDtypeStruct((PAD, 768), bf16),
+        in_specs=[VMEM],
+        out_specs=VMEM,
+        scratch_shapes=RETURN_SCRATCH,
+        compiler_params=kernel_params(2),
+        name="gather_mixture",
+    )(partial)
+
+
+def expert_kernel(
+    send, grad_rows, weight_in, weight_out,
+    x_out, hidden, grad_pre, y_part, grad_home,
+    landed, held_in, held_out, grad_part, load_sems,
+    d0, d1, d2, d3, *back,
+):
+    loads = [
+        pltpu.make_async_copy(weight_in, held_in, load_sems.at[0]),
+        pltpu.make_async_copy(weight_out, held_out, load_sems.at[1]),
+    ]
+    for load in loads:
+        load.start()
+    greet(1, 1)
+    out_way = Dispatch(send, landed, x_out, (d0, d1, d2, d3))
+    home_way = Return(grad_part, back[0], back[1], back[2], back[3], back[4:])
+    out_way.cross()
+    pack = packer()
+    out_way.turn(0, pack)
+    out_way.turn(1, pack)
+    for load in loads:
+        load.wait()
+
+    def run(first, count):
+        for j in range(2):
+            span = pl.ds(first * 160, count * 160)
+            pre_act = dot(x_out[j, span], held_in[j])
+            cdf = 0.5 * (1.0 + lax.erf(pre_act * inv_root_two))
+            hidden[j, span] = (pre_act * cdf).astype(bf16)
+            slope = cdf + pre_act * jnp.exp(-0.5 * pre_act * pre_act) * inv_root_tau
+            grad_hidden = dot_cols(grad_rows[j, span], held_out[j])
+            grad_pre[j, span] = (grad_hidden * slope).astype(bf16)
+            grad_part[j, span] = dot_cols(grad_pre[j, span], held_in[j]).astype(bf16)
+
+    run(0, 1)
+    out_way.relay()
+    run(1, 2)
+    home_way.near()
+    out_way.last()
+    run(3, 1)
+    home_way.far()
+    for j in range(2):
+        y_part[j, 0:320] = dot(hidden[j, 0:320], held_out[j]).astype(bf16)
+    home_way.add_far()
+    for j in range(2):
+        y_part[j, 320:640] = dot(hidden[j, 320:640], held_out[j]).astype(bf16)
+    home_way.finish(0, pack)
+    home_way.finish(1, pack)
+    home_way.arrive()
+    grad_home[...] = home_way.home[...]
+    out_way.close()
+    home_way.close()
+
+
+def run_experts(send, grad_rows, weight_in, weight_out):
+    rows = jax.ShapeDtypeStruct((2, EXPERT_ROWS, 768), bf16)
+    anywhere = pl.BlockSpec(memory_space=pl.ANY)
+    return pl.pallas_call(
+        expert_kernel,
+        out_shape=[rows, rows, rows, rows, jax.ShapeDtypeStruct((PAD, 768), bf16)],
+        in_specs=[VMEM, VMEM, anywhere, anywhere],
+        out_specs=[VMEM] * 5,
+        scratch_shapes=[
+            pltpu.VMEM((PAD, 768), bf16),
+            pltpu.VMEM((2, 768, 768), bf16),
+            pltpu.VMEM((2, 768, 768), bf16),
+            pltpu.VMEM((2, EXPERT_ROWS, 768), bf16),
+            pltpu.SemaphoreType.DMA((2,)),
+        ]
+        + DISPATCH_SCRATCH
+        + RETURN_SCRATCH,
+        compiler_params=kernel_params(3),
+        name="experts",
+    )(send, grad_rows, weight_in, weight_out)
 
 
 def contract_rows(left, right):
@@ -139,47 +543,12 @@
     slot_index = jnp.sum((jnp.cumsum(id_hot, axis=0) - id_hot) * id_hot, axis=1).reshape(
         tok_rows, TOPK
     )
-    dest_rows = expert_ids * capacity + slot_index
-    buffer_pos = jnp.arange(all_experts * capacity, dtype=jnp.int32)
+    dest_rows = (expert_ids // local_experts) * BLOCK + lax.rem(expert_ids, 2) * capacity + slot_index
+    buffer_pos = jnp.arange(PAD, dtype=jnp.int32)
     selectors = [
         (buffer_pos[:, None] == dest_rows[None, :, route_slot]).astype(jnp.bfloat16)
         for route_slot in range(TOPK)
     ]
-
-    def spread_rows(buffer_rows):
-        shaped = buffer_rows.reshape(expert_count, 1, local_experts, capacity, model_width)
-        widened = jnp.broadcast_to(
-            shaped, (expert_count, mp_count, local_experts, capacity, model_width)
-        )
-        return widened.reshape(expert_count * mp_count, local_experts, capacity, model_width)
-
-    send_rows = sum(
-        (
-            jnp.dot(selector, normed_second, preferred_element_type=jnp.float32)
-            for selector in selectors
-        )
-    ).astype(jnp.bfloat16)
-    received = lax.all_to_all(
-        spread_rows(send_rows), ("expert", "mp"), split_axis=0, concat_axis=0, tiled=True
-    )
-    pre_act = jnp.einsum("sjcd,jdf->sjcf", received, expert_in, preferred_element_type=jnp.float32)
-    normal_cdf = 0.5 * (1.0 + lax.erf(pre_act * inv_root_two))
-    hidden = (pre_act * normal_cdf).astype(jnp.bfloat16)
-    partial_out = jnp.einsum(
-        "sjcf,jfd->sjcd", hidden, expert_out, preferred_element_type=jnp.float32
-    )
-    arrived = lax.all_to_all(partial_out, ("expert", "mp"), split_axis=0, concat_axis=0, tiled=True)
-    summed = jnp.sum(
-        arrived.reshape(expert_count, mp_count, local_experts, capacity, model_width), axis=1
-    )
-    expert_rows = summed.astype(jnp.bfloat16).reshape(all_experts * capacity, model_width)
-    mixture = sum(
-        (
-            gate_values[:, route_slot, None] * contract_rows(selectors[route_slot], expert_rows)
-            for route_slot in range(TOPK)
-        )
-    )
-    result = resid + mixture
     grad_out = cotangent.astype(jnp.float32)
     grad_send = sum(
         (
@@ -191,31 +560,24 @@
             for route_slot in range(TOPK)
         )
     ).astype(jnp.bfloat16)
-    grad_recv = lax.all_to_all(
-        spread_rows(grad_send), ("expert", "mp"), split_axis=0, concat_axis=0, tiled=True
-    )
-    grad_hidden = jnp.einsum(
-        "sjcd,jfd->sjcf", grad_recv, expert_out, preferred_element_type=jnp.float32
-    )
-    expert_out_grad = jnp.einsum(
-        "sjcf,sjcd->jfd", hidden, grad_recv, preferred_element_type=jnp.float32
-    )
-    gelu_slope = normal_cdf + pre_act * jnp.exp(-0.5 * pre_act * pre_act) * inv_root_tau
-    grad_pre = (grad_hidden * gelu_slope).astype(jnp.bfloat16)
-    expert_in_grad = jnp.einsum(
-        "sjcd,sjcf->jdf", received, grad_pre, preferred_element_type=jnp.float32
-    )
-    grad_partial = jnp.einsum(
-        "sjcf,jdf->sjcd", grad_pre, expert_in, preferred_element_type=jnp.float32
-    )
-    grad_arrived = lax.all_to_all(
-        grad_partial, ("expert", "mp"), split_axis=0, concat_axis=0, tiled=True
-    )
-    grad_summed = jnp.sum(
-        grad_arrived.reshape(expert_count, mp_count, local_experts, capacity, model_width), axis=1
-    )
-    grad_rows = grad_summed.astype(jnp.bfloat16).reshape(all_experts * capacity, model_width)
-    grad_normed = sum((contract_rows(selector, grad_rows) for selector in selectors))
+    grad_recv = spread_rows(grad_send)
+    send_rows = jnp.dot(
+        selectors[0] + selectors[1], normed_second, preferred_element_type=jnp.float32
+    ).astype(jnp.bfloat16)
+    received, hidden, grad_pre, y_part, grad_rows = run_experts(
+        send_rows, grad_recv, expert_in, expert_out
+    )
+    expert_rows = gather_rows(y_part)
+    mixture = sum(
+        (
+            gate_values[:, route_slot, None] * contract_rows(selectors[route_slot], expert_rows)
+            for route_slot in range(TOPK)
+        )
+    )
+    result = resid + mixture
+    expert_out_grad = jnp.einsum("jrf,jrd->jfd", hidden, grad_recv, preferred_element_type=jnp.float32)
+    expert_in_grad = jnp.einsum("jrd,jrf->jdf", received, grad_pre, preferred_element_type=jnp.float32)
+    grad_normed = contract_rows(selectors[0] + selectors[1], grad_rows)
     gain_second_part = jnp.sum(grad_normed * normal_second, axis=0)
     grad_unit_second = grad_normed * gain_moe
     grad_resid = grad_out + scale_second * (

time: 565 us -> 508 us (0.90)
  Pallas kernels: 0 us -> 140 us
  waiting for transfers between devices: 117 us -> 4.44 us
  local copies, waits for them, and re-layouts: 100 us -> 63.8 us
  starting transfers between devices: 27 us -> 0.38 us
  matrix products: 49.4 us -> 36.3 us
    pallas_call x0 -> x3, Pallas kernels: none -> 140 us  [the longest x1 65.6 us: run_experts(): pl.pallas_call(expert_kernel, out_shape=[rows, rows, rows, rows, jax.Shap...]
    all_to_all x4 -> x0, waiting for transfers between devices: 93.2 us -> none  [the longest x1 48.7 us: body(): lax.all_to_all(grad_partial, ('expert', 'mp'), split_axis=0, concat_axis=...]
    all_to_all x4 -> x0, starting transfers between devices: 26.3 us -> none  [the longest x1 8.77 us: body(): lax.all_to_all(spread_rows(send_rows), ('expert', 'mp'), split_axis=0, co...]
    reduce_scatter x1, waiting for transfers between devices: 23.2 us -> 0.02 us  [body(): lax.psum_scatter(jnp.dot(attended, proj_full, preferred_element_type=jnp....]
    dot_general x8 -> x3, matrix products: 30.7 us -> 12.3 us  [the longest x1 5.98 us: body(): jnp.einsum('jrf,jrd->jfd', hidden, grad_recv, preferred_element_type=jnp....]
    broadcast_in_dim x6 -> x0, local copies, waits for them, and re-layouts: 13.6 us -> none  [spread_rows(): jnp.broadcast_to(shaped, (expert_count, mp_count, local_experts, capacity...]
    transpose x2 -> x0, local copies, waits for them, and re-layouts: 9.87 us -> none  [the longest x1 4.96 us: body(): jnp.einsum('sjcf,jdf->sjcd', grad_pre, expert_in, preferred_element_type=...]
    reduce_sum x2 -> x0, other arithmetic: 7.64 us -> none  [the longest x1 3.82 us: body(): jnp.sum(arrived.reshape(expert_count, mp_count, local_experts, capacity,...]
  transfers between devices with their start and end apart: 8 -> 4, of which waited for: 5 -> 1; matrix products, arithmetic and copies ran while one was open for 17% -> 12% of each run, Pallas kernels for 0% -> 15%
where the time goes in v1:
time: 508 us; the launch traced here: 503 us
  blocking collectives  219 us (43%)
  Pallas kernels  140 us (28%)
  local copies, waits for them, and re-layouts  63.8 us (13%)
  matrix products  36.3 us (7%)
  other arithmetic  23.8 us (5%)
  between operations  14.8 us (3%)
    unnamed x2, blocking collectives  139 us
    pallas_call x1, Pallas kernels, run_experts(): pl.pallas_call(expert_kernel, out_shape=[rows, rows, rows, rows, jax.Shap...  65.6 us
    pallas_call x1, Pallas kernels, gather_rows(): pl.pallas_call(gather_kernel, out_shape=jax.ShapeDtypeStruct((PAD, 768),...  38.3 us
    pallas_call x1, Pallas kernels, spread_rows(): pl.pallas_call(spread_kernel, out_shape=jax.ShapeDtypeStruct((2, EXPERT_R...  36.2 us
    unnamed x115, local copies, waits for them, and re-layouts  31.6 us
    all_gather x1, blocking collectives, body(): lax.all_gather(proj_weight, 'expert', axis=1, tiled=True)  25.2 us
    all_gather x1, blocking collectives, body(): lax.all_gather(qkv_weight, 'expert', axis=0, tiled=True)  24.6 us
    all_gather x1, blocking collectives, body(): seq_units = lax.all_gather(unit_first, 'mp', axis=0, tiled=True)  15.7 us
  transfers between devices with their start and end apart: 4, of which 1 were waited for; matrix products, arithmetic and copies ran while one was open for 12% of the time, Pallas kernels for 15%

profile of v1, /device:TPU:0, one launch (start us, length us, event | category | flops | bytes accessed | tf_op | source)
XLA Modules:
  0.0 502.9 jit_solution(2664019287194087305)
XLA Ops:
  8.0 1.0 fusion.28
  9.1 1.0 convolution_bitcast_fusion
  10.9 1.0 fusion.23
  11.9 25.2 %all_gather.14 = bf16[192,768]{0,1:T(8,128)(2,1)S(1)} all-gather(bf16[192,24]{0,1:T(8,128)(2,1)} %param.16), channel_id=1, replica_groups=mesh['expert'=32,'mp'=4] {'expert'}, dimensions={1}, use_global_device_ids=true | all-gather | bytes 304128 | tf_op jit(solution)/shard_map/all_gather | solution.py:465
  37.1 15.7 %all_gather.12 = bf16[512,768]{1,0:T(8,128)(2,1)} all-gather(bf16[128,768]{1,0:T(8,128)(2,1)S(1)} %fusion.23), channel_id=1, replica_groups=mesh['expert'=32,'mp'=4] {'mp'}, dimensions={0}, use_global_device_ids=true | all-gather | bytes 983040 | tf_op jit(solution)/shard_map/all_gather | solution.py:462
  52.8 24.6 %all_gather.13 = bf16[768,3,192]{2,0,1:T(8,128)(2,1)S(1)} all-gather(bf16[24,3,192]{2,0,1:T(8,128)(2,1)} %param.15), channel_id=1, replica_groups=mesh['expert'=32,'mp'=4] {'expert'}, dimensions={0}, use_global_device_ids=true | all-gather | bytes 912384 | tf_op jit(solution)/shard_map/all_gather | solution.py:464
  77.4 1.5 copy.92
  78.9 3.4 broadcast_bitcast_fusion
  82.4 7.1 %copy.128 = f32[1,3,512,1024]{3,1,2,0:T(4,128)S(1)} copy(f32[1,3,512,1024]{3,2,1,0:T(8,128)} %broadcast_bitcast_fusion) | data formatting | bytes 12582912
  89.5 4.0 slice.97
  93.5 13.2 %reshape.146 = f32[3,512,1023]{2,1,0:T(8,128)} reshape(f32[3,523776]{1,0:T(4,128)} %slice.97) | data formatting | bytes 12570624 | tf_op jit(solution)/shard_map/while/body/eval_jaxpr/reshape | solution.py:502
  106.7 1.9 slice-done
  108.6 2.7 copy.122
  111.4 2.1 convolution_convert_fusion.1
  113.4 3.0 fusion.71
  118.3 1.6 fusion.72
  120.3 1.2 dynamic-slice.3
  121.6 1.2 dynamic-slice.1
  125.7 1.4 fusion.32
  127.1 1.3 add_convert_fusion.send
  128.4 36.2 %spread_cotangent.1.grad_rows = bf16[2,640,768]{2,1,0:T(8,128)(2,1)} custom-call(bf16[512,768]{1,0:T(8,128)(2,1)} %add_convert_fusion.send), custom_call_target="tpu_custom_call" | custom-call | tf_op jit(solution)/shard_map/spread_cotangent/pallas_call | solution.py:309
  164.7 1.2 multiply_reduce_fusion.3
  165.9 2.0 convolution_convert_fusion.send
  167.9 65.6 %experts.1 = (bf16[2,640,768]{2,1,0:T(8,128)(2,1)}, bf16[2,640,768]{2,1,0:T(8,128)(2,1)}, bf16[2,640,768]{2,1,0:T(8,128)(2,1)}, bf16[2,640,768]{2,1,0:T(8,128)(2,1)}, bf16[512,768]{1,0:T(8,128)(2,1)}) custom-call(bf16[512,768]{1,0:T(8,128)(2,1)} %convolution_convert_fusion.send, bf16[2,640,768]{2,1,0:T(8,128)(2,1)} %spread_cotangent.1.grad_rows, ...), custom_call_target="tpu_custom_call" | custom-call | tf_op jit(solution)/shard_map/experts/pallas_call | solution.py:402
  233.6 1.6 multiply_reduce_fusion.1
  236.1 14.4 %all_gather.15 = bf16[512,768]{1,0:T(8,128)(2,1)S(1)} all-gather(bf16[128,768]{1,0:T(8,128)(2,1)S(1)} %fusion.69), channel_id=1, replica_groups=mesh['expert'=32,'mp'=4] {'mp'}, dimensions={0}, use_global_device_ids=true | all-gather | bytes 983040 | tf_op jit(solution)/shard_map/all_gather | solution.py:587
  250.5 0.9 copy-done.4
  251.9 1.3 fusion.8
  256.4 2.7 copy.126
  259.2 2.0 fusion.3
  261.3 1.8 concatenate.29.clone
  263.1 7.5 %reshape.164 = bf16[1571328]{0:T(1024)(128)(2,1)} reshape(bf16[3,512,1023]{2,1,0:T(8,128)(2,1)S(1)} %concatenate.29.clone) | data formatting | bytes 6285312
  270.6 5.6 %reshape.151 = bf16[3,523776]{1,0:T(4,128)(2,1)} reshape(bf16[1571328]{0:T(1024)(128)(2,1)} %reshape.164) | data formatting | bytes 6285312 | tf_op jit(solution)/shard_map/while/body/eval_jaxpr/reshape | solution.py:602
  276.2 6.6 %pad_convert_fusion = f32[3,524288]{1,0:T(4,128)} fusion(bf16[3,523776]{1,0:T(4,128)(2,1)} %reshape.151), kind=kLoop, calls=%fused_computation.1 | loop fusion | flops 1572864 | bytes 9434112 | tf_op jit(solution)/shard_map/while/body/eval_jaxpr/reshape | solution.py:607
  282.9 38.3 %gather_mixture.1 = bf16[512,768]{1,0:T(8,128)(2,1)} custom-call(bf16[2,640,768]{2,1,0:T(8,128)(2,1)} %get-tuple-element.62.partial), custom_call_target="tpu_custom_call" | custom-call | tf_op jit(solution)/shard_map/gather_mixture/pallas_call | solution.py:335
  321.6 15.3 %all-reduce.4 = f32[4,2,32,6]{2,1,3,0:T(2,128)S(1)} all-reduce(f32[4,2,32,6]{2,1,3,0:T(2,128)S(1)} %copy.108), channel_id=4, replica_groups=mesh['expert'=32,'mp'=4] {'mp'}, use_global_device_ids=true, to_apply=%region_14.15.clone | all-reduce | flops 1536 | bytes 12288
  337.7 1.4 fusion.73
  339.4 6.8 %bitcast_reduce_fusion = f32[3,1024]{1,0:T(4,128)S(1)} fusion(f32[1,3,512,1024]{3,1,2,0:T(4,128)} %bitcast.105), kind=kLoop, calls=%fused_computation | loop fusion | flops 1569792 | bytes 6303744 | tf_op jit(solution)/shard_map/while/body/eval_jaxpr/reduce_sum | solution.py:607
  346.9 2.3 fusion.17
  349.6 124.2 %all-reduce.7 = (f32[1,2,32,6]{3,1,0,2:T(2,128)S(1)}, f32[32,3]{1,0:T(8,128)S(1)}) all-reduce(f32[1,2,32,6]{3,1,0,2:T(2,128)S(1)} %copy.109, f32[32,3]{1,0:T(8,128)S(1)} %fusion.42), channel_id=5, replica_groups=mesh['expert'=32,'mp'=4] {'expert'}, use_global_device_ids=true, to_apply=%region_15.16.clone | all-reduce | flops 480 | bytes 3840
  473.8 1.2 constant_dynamic-slice_fusion
  476.1 1.0 convolution_multiply_fusion.3
  477.1 1.0 fusion.15
  478.2 6.0 %fusion.75 = f32[2,768,768]{2,1,0:T(8,128)} fusion(bf16[2,640,768]{2,1,0:T(8,128)(2,1)} %get-tuple-element.66, bf16[2,640,768]{2,1,0:T(8,128)(2,1)S(1)} %copy-done.3), kind=kOutput, calls=%fused_computation.134 | convolution fusion | flops 1509949440 | bytes 8650752 | tf_op jit(solution)/shard_map/jrf,jrd->jfd/dot_general | solution.py:578
  484.2 4.3 fusion.74
  488.5 1.2 fusion.24
  489.8 2.0 fusion.27
  491.8 4.4 reduce-scatter.9.cloned.1.call-done
  (161 shorter events, 15.2 us)
Async XLA Ops:
  7.2 1.9 copy-start
  7.2 157.5 %reduce-scatter.5.cloned.1.call-start = ((), (), s32[]{:S(2)}) async-start(), calls=%async_computation.4 | async-start | bytes 1966080 | tf_op jit(solution)/shard_map/reduce_scatter | solution.py:530
  9.1 28.1 %copy-start.37 = (f32[128]{0:T(128)}, f32[128]{0:T(128)S(1)}, u32[]{:S(2)}) copy-start(f32[128]{0:T(128)S(1)} %add_rsqrt_fusion.1) | copy-start | bytes 1540
  37.1 80.5 %copy-start.10 = (bf16[192,768]{0,1:T(8,128)(2,1)}, bf16[192,768]{0,1:T(8,128)(2,1)S(1)}, u32[]{:S(2)}) copy-start(bf16[192,768]{0,1:T(8,128)(2,1)S(1)} %all_gather.14) | copy-start | bytes 884740
  108.6 2.7 copy-start.42
  113.4 3.5 copy-start.19
  117.6 2.3 copy-start.47
  117.6 8.0 %copy-start.48 = (f32[128,2]{0,1:T(2,128)S(1)}, f32[128,2]{0,1:T(2,128)}, u32[]{:S(2)}) copy-start(f32[128,2]{0,1:T(2,128)} %param.21) | copy-start | bytes 3076
  119.8 7.3 %copy-start.12 = (bf16[128,768]{1,0:T(8,128)(2,1)S(1)}, bf16[128,768]{1,0:T(8,128)(2,1)}, u32[]{:S(2)}) copy-start(bf16[128,768]{1,0:T(8,128)(2,1)} %param.23) | copy-start | bytes 589828
  119.9 368.7 %reduce-scatter.7.cloned.1.call-start = ((), (), s32[]{:S(2)}) async-start(), calls=%async_computation.5 | async-start | bytes 1966080 | tf_op jit(solution)/shard_map/reduce_scatter | solution.py:669
  125.6 40.3 %copy-start.30 = (s32[128]{0:T(128)}, s32[128]{0:T(128)S(1)}, u32[]{:S(2)}) copy-start(s32[128]{0:T(128)S(1)} %get-tuple-element.82) | copy-start | bytes 1540
  125.7 39.0 %copy-start.39 = (f32[128]{0:T(128)}, f32[128]{0:T(128)S(1)}, u32[]{:S(2)}) copy-start(f32[128]{0:T(128)S(1)} %get-tuple-element.95) | copy-start | bytes 1540
  125.7 39.0 %copy-start.26 = (f32[3,512]{1,0:T(4,128)S(1)}, f32[3,512]{1,0:T(4,128)}, u32[]{:S(2)}) copy-start(f32[3,512]{1,0:T(4,128)} %copy-done.25) | copy-start | bytes 18436
  125.7 39.0 %copy-start.29 = (f32[3,512]{1,0:T(4,128)S(1)}, f32[3,512]{1,0:T(4,128)}, u32[]{:S(2)}) copy-start(f32[3,512]{1,0:T(4,128)} %copy-done.28) | copy-start | bytes 18436
  127.1 38.8 %copy-start.27 = (f32[768]{0:T(1024)S(1)}, f32[768]{0:T(1024)}, u32[]{:S(2)}) copy-start(f32[768]{0:T(1024)} %param.14) | copy-start | bytes 9220
  165.9 69.3 %copy-start.35 = (f32[128]{0:T(128)}, f32[128]{0:T(128)S(1)}, u32[]{:S(2)}) copy-start(f32[128]{0:T(128)S(1)} %add_rsqrt_fusion) | copy-start | bytes 1540
  167.9 65.6 %copy-start.31 = (s32[128]{0:T(128)S(1)}, s32[128]{0:T(128)}, u32[]{:S(2)}) copy-start(s32[128]{0:T(128)} %copy-done.30) | copy-start | bytes 1540
  167.9 65.7 %copy-start.34 = (s32[128]{0:T(128)S(1)}, s32[128]{0:T(128)}, u32[]{:S(2)}) copy-start(s32[128]{0:T(128)} %copy-done.33) | copy-start | bytes 1540
  167.9 68.0 %copy-start.13 = (bf16[128,768]{1,0:T(8,128)(2,1)S(1)}, bf16[128,768]{1,0:T(8,128)(2,1)}, u32[]{:S(2)}) copy-start(bf16[128,768]{1,0:T(8,128)(2,1)} %param.23) | copy-start | bytes 589828
  233.6 17.9 %copy-start.11 = (bf16[192,768]{0,1:T(8,128)(2,1)S(1)}, bf16[192,768]{0,1:T(8,128)(2,1)}, u32[]{:S(2)}) copy-start(bf16[192,768]{0,1:T(8,128)(2,1)} %copy-done.10) | copy-start | bytes 884740
  235.2 18.0 %copy-start.45 = (f32[128]{0:T(128)}, f32[128]{0:T(128)S(1)}, u32[]{:S(2)}) copy-start(f32[128]{0:T(128)S(1)} %broadcast_multiply_fusion.2) | copy-start | bytes 1540
  236.1 17.0 %copy-start.20 = (bf16[512,576]{0,1:T(8,128)(2,1)S(1)}, bf16[512,576]{0,1:T(8,128)(2,1)}, u32[]{:S(2)}) copy-start(bf16[512,576]{0,1:T(8,128)(2,1)} %copy-done.19) | copy-start | bytes 1769476
  254.8 4.2 copy-start.24
  256.0 3.2 copy-start.15
  256.0 3.2 copy-start.21
  256.0 3.2 copy-start.43
  259.1 2.1 copy-start.17
  261.2 230.6 %reduce-scatter.11.cloned.1.call-start = ((), (), s32[]{:S(2)}) async-start(), calls=%async_computation.7 | async-start | bytes 811008 | tf_op jit(solution)/shard_map/reduce_scatter | solution.py:677
  282.9 54.8 %copy-start.5 = (bf16[512,768]{1,0:T(8,128)(2,1)S(1)}, bf16[512,768]{1,0:T(8,128)(2,1)}, u32[]{:S(2)}) copy-start(bf16[512,768]{1,0:T(8,128)(2,1)} %copy-done.4) | copy-start | bytes 2359300
  282.9 54.8 %copy-start.23 = (bf16[3,64,512]{2,1,0:T(8,128)(2,1)S(1)}, bf16[3,64,512]{2,1,0:T(8,128)(2,1)}, u32[]{:S(2)}) copy-start(bf16[3,64,512]{2,1,0:T(8,128)(2,1)} %copy-done.22) | copy-start | bytes 589828
  339.1 157.1 %reduce-scatter.9.cloned.1.call-start = ((), (), s32[]{:S(2)}) async-start(), calls=%async_computation.6 | async-start | bytes 2433024 | tf_op jit(solution)/shard_map/reduce_scatter | solution.py:676
  339.3 7.5 %copy-start.16 = (bf16[512,768]{1,0:T(8,128)(2,1)S(1)}, bf16[512,768]{1,0:T(8,128)(2,1)}, u32[]{:S(2)}) copy-start(bf16[512,768]{1,0:T(8,128)(2,1)} %all_gather.12) | copy-start | bytes 2359300
  339.3 7.5 %copy-start.18 = (bf16[512,3,3,64]{0,3,2,1:T(8,128)(2,1)S(1)}, bf16[512,3,3,64]{0,3,2,1:T(8,128)(2,1)}, u32[]{:S(2)}) copy-start(bf16[512,3,3,64]{0,3,2,1:T(8,128)(2,1)} %copy-done.17) | copy-start | bytes 1769476
  339.3 7.5 %copy-start.44 = (f32[768]{0:T(1024)S(1)}, f32[768]{0:T(1024)}, u32[]{:S(2)}) copy-start(f32[768]{0:T(1024)} %param.13) | copy-start | bytes 9220
  346.1 3.1 copy-start.51
  346.5 129.6 %copy-start.6 = (bf16[512,768]{1,0:T(8,128)(2,1)S(1)}, bf16[512,768]{1,0:T(8,128)(2,1)}, u32[]{:S(2)}) copy-start(bf16[512,768]{1,0:T(8,128)(2,1)} %gather_mixture.1) | copy-start | bytes 2359300
  346.9 130.3 %copy-start.32 = (s32[128]{0:T(128)S(1)}, s32[128]{0:T(128)}, u32[]{:S(2)}) copy-start(s32[128]{0:T(128)} %copy-done.30) | copy-start | bytes 1540
  346.9 130.3 %copy-start.40 = (f32[128]{0:T(128)S(1)}, f32[128]{0:T(128)}, u32[]{:S(2)}) copy-start(f32[128]{0:T(128)} %copy-done.39) | copy-start | bytes 1540
  349.1 129.0 %copy-start.3 = (bf16[2,640,768]{2,1,0:T(8,128)(2,1)S(1)}, bf16[2,640,768]{2,1,0:T(8,128)(2,1)}, u32[]{:S(2)}) copy-start(bf16[2,640,768]{2,1,0:T(8,128)(2,1)} %spread_cotangent.1.grad_rows) | copy-start | bytes 5898244
  478.2 6.0 %copy-start.49 = (bf16[2,640,768]{2,1,0:T(8,128)(2,1)S(1)}, bf16[2,640,768]{2,1,0:T(8,128)(2,1)}, u32[]{:S(2)}) copy-start(bf16[2,640,768]{2,1,0:T(8,128)(2,1)} %get-tuple-element.64) | copy-start | bytes 5898244
  478.2 6.0 %copy-start.50 = (bf16[2,640,768]{2,1,0:T(8,128)(2,1)S(1)}, bf16[2,640,768]{2,1,0:T(8,128)(2,1)}, u32[]{:S(2)}) copy-start(bf16[2,640,768]{2,1,0:T(8,128)(2,1)} %get-tuple-element.65) | copy-start | bytes 5898244
  484.1 4.4 copy-start.7
  484.1 4.4 copy-start.38
  484.1 5.6 %copy-start.9 = (f32[128,768]{1,0:T(8,128)S(1)}, f32[128,768]{1,0:T(8,128)}, u32[]{:S(2)}) copy-start(f32[128,768]{1,0:T(8,128)} %copy-done.8) | copy-start | bytes 1179652
  484.2 5.6 %copy-start.14 = (bf16[128,768]{1,0:T(8,128)(2,1)S(1)}, bf16[128,768]{1,0:T(8,128)(2,1)}, u32[]{:S(2)}) copy-start(bf16[128,768]{1,0:T(8,128)(2,1)} %param.23) | copy-start | bytes 589828
  484.2 5.6 %copy-start.36 = (f32[128]{0:T(128)S(1)}, f32[128]{0:T(128)}, u32[]{:S(2)}) copy-start(f32[128]{0:T(128)} %copy-done.35) | copy-start | bytes 1540
  484.2 5.6 %copy-start.46 = (f32[128]{0:T(128)S(1)}, f32[128]{0:T(128)}, u32[]{:S(2)}) copy-start(f32[128]{0:T(128)} %copy-done.45) | copy-start | bytes 1540
  484.2 11.9 %copy-start.1 = (f32[32,3]{0,1:T(4,128)S(1)}, f32[32,3]{0,1:T(4,128)}, u32[]{:S(2)}) copy-start(f32[32,3]{0,1:T(4,128)} %param.17) | copy-start | bytes 1156
  (9 other events, 10.1 us)
Sparse Core Ops, SparseCore 0:
  120.0 24.9 reduce-scatter.4
  261.3 25.6 reduce-scatter.6
  339.2 74.3 reduce-scatter.10
  417.6 78.5 reduce-scatter.8

commit v2 on v1

v2 whole, which is shorter than its diff:
```python
import jax
import jax.numpy as jnp
from jax import lax
from jax.experimental import pallas as pl
from jax.experimental.pallas import tpu as pltpu
from jax.sharding import PartitionSpec as P

HEAD_DIM = 64
TOPK = 2


epsilon = 1e-06
masked_value = -1e30
inv_root_two = 0.7071067811865476
inv_root_tau = 0.3989422804014327
highest = lax.Precision.HIGHEST


MESH = pl.DeviceIdType.MESH
BLOCK = 16
HALF = 80
PLANE = 32
RING = 4
PAD = PLANE * BLOCK
ROWS = 320
EXPERT_ROWS = 640
f32 = jnp.float32
bf16 = jnp.bfloat16


def place():
    e, z = lax.axis_index("expert"), lax.axis_index("mp")
    return e, z, lax.rem(z + 1, RING), lax.rem(z + RING - 1, RING)


def plane_target(e, d):
    step = d // 8
    dy, dx, dc = lax.rem(step * 2, 4) + step // 2, lax.rem(d // 2, 4), lax.rem(d, 2)
    y, x, c = e // 8, lax.rem(e // 2, 4), lax.rem(e, 2)
    return lax.rem(y + dy, 4) * 8 + lax.rem(x + dx, 4) * 2 + lax.rem(c + dc, 2)


def plane_source(e, d):
    step = d // 8
    dy, dx, dc = lax.rem(step * 2, 4) + step // 2, lax.rem(d // 2, 4), lax.rem(d, 2)
    y, x, c = e // 8, lax.rem(e // 2, 4), lax.rem(e, 2)
    return lax.rem(y + 4 - dy, 4) * 8 + lax.rem(x + 4 - dx, 4) * 2 + lax.rem(c + dc, 2)


def block_at(index):
    return pl.ds(pl.multiple_of(index * BLOCK, BLOCK), BLOCK)


def greet(plane, ring, across=0):
    e, z, right, left = place()
    barrier = pltpu.get_barrier_semaphore()
    if plane:

        def signal(d, carry):
            pl.semaphore_signal(
                barrier, inc=1, device_id=(plane_target(e, d), z), device_id_type=MESH
            )
            return carry

        lax.fori_loop(1, PLANE, signal, 0)
    if ring:
        for other in (right, left):
            pl.semaphore_signal(barrier, inc=1, device_id=(e, other), device_id_type=MESH)
    if across:
        other = lax.rem(z + 2, RING)
        pl.semaphore_signal(barrier, inc=1, device_id=(e, other), device_id_type=MESH)
    pl.semaphore_wait(barrier, (PLANE - 1) * plane + 2 * ring + across)


def drain(ref, sem):
    pltpu.make_async_copy(ref, ref, sem).wait()


def dot(left, right):
    return jnp.dot(left, right, preferred_element_type=f32)


def dot_rows(left, right):
    return lax.dot_general(left, right, (((0,), (0,)), ((), ())), preferred_element_type=f32)


def dot_cols(left, right):
    return lax.dot_general(left, right, (((1,), (1,)), ((), ())), preferred_element_type=f32)


def packer():
    row = lax.broadcasted_iota(jnp.int32, (2 * HALF, 256), 0)
    col = lax.broadcasted_iota(jnp.int32, (2 * HALF, 256), 1)
    expert = (row >= HALF).astype(jnp.int32)
    inner = row - expert * HALF
    source = (inner * 205) // 1024
    slot = inner - source * 5
    return (col == source * BLOCK + expert * 5 + slot).astype(bf16)


class Dispatch:
    def __init__(self, send, landed, rows, sems):
        self.send, self.landed, self.rows = send, landed, rows
        self.plane_out, self.plane_in, self.ring_out, self.ring_in = sems

    def part(self, slot, half):
        return self.rows.at[:, pl.ds(slot * 160 + half * HALF, HALF)]

    def cross(self):
        e, z, right, left = place()

        def send(d, carry):
            other = plane_target(e, d)
            pltpu.make_async_remote_copy(
                self.send.at[block_at(other)],
                self.landed.at[block_at(d)],
                self.plane_out,
                self.plane_in.at[d // 16],
                device_id=(other, z),
                device_id_type=MESH,
            ).start()
            return carry

        lax.fori_loop(1, PLANE, send, 0)
        self.landed[0:BLOCK] = self.send[block_at(e)]

    def copy(self, index, source, target, other):
        e = lax.axis_index("expert")
        return pltpu.make_async_remote_copy(
            source,
            target,
            self.ring_out.at[index],
            self.ring_in.at[index],
            device_id=(e, other),
            device_id_type=MESH,
        )

    def copies(self):
        e, z, right, left = place()
        part = self.part
        return [
            self.copy(0, part(0, 0), part(2, 0), right),
            self.copy(1, part(0, 1), part(2, 1), right),
            self.copy(2, part(0, 0), part(1, 0), left),
            self.copy(3, part(0, 1), part(1, 1), left),
            self.copy(4, part(2, 0), part(3, 0), right),
            self.copy(5, part(1, 1), part(3, 1), left),
        ]

    def turn(self, half, pack):
        lo = 256 * half
        span = self.landed.at[pl.ds(lo + (BLOCK if half == 0 else 0), 256 - (BLOCK if half == 0 else 0))]
        drain(span, self.plane_in.at[half])
        packed = dot(pack, self.landed[lo : lo + 256]).astype(bf16)
        for j in range(2):
            self.rows[j, half * HALF : half * HALF + HALF] = packed[j * HALF : j * HALF + HALF]
        ring = self.copies()
        ring[half].start()
        ring[2 + half].start()

    def relay(self):
        ring = self.copies()
        ring[0].wait_recv()
        ring[4].start()
        ring[3].wait_recv()
        ring[5].start()
        ring[1].wait_recv()
        ring[2].wait_recv()

    def last(self):
        ring = self.copies()
        ring[4].wait_recv()
        ring[5].wait_recv()

    def close(self):
        for copy in self.copies():
            copy.wait_send()
        drain(self.send.at[pl.ds(0, (PLANE - 1) * BLOCK)], self.plane_out)


DISPATCH_SCRATCH = [
    pltpu.SemaphoreType.DMA,
    pltpu.SemaphoreType.DMA((2,)),
    pltpu.SemaphoreType.DMA((6,)),
    pltpu.SemaphoreType.DMA((6,)),
]


class Return:
    def __init__(self, partial, relayed, landed, spread, home, sems):
        self.partial, self.relayed, self.landed = partial, relayed, landed
        self.spread, self.home = spread, home
        self.ring_out, self.ring_in, self.plane_out, self.plane_in = sems

    def part(self, slot, half):
        return self.partial.at[:, pl.ds(slot * 160 + half * HALF, HALF)]

    def copies(self):
        e, z, right, left = place()

        def copy(index, source, other):
            return pltpu.make_async_remote_copy(
                source,
                self.landed.at[index],
                self.ring_out.at[index],
                self.ring_in.at[index],
                device_id=(e, other),
                device_id_type=MESH,
            )

        part = self.part
        return [
            copy(0, part(3, 0), right),
            copy(1, part(3, 1), left),
            copy(2, part(1, 1), right),
            copy(3, part(2, 0), left),
            copy(4, self.relayed.at[0], right),
            copy(5, self.relayed.at[1], left),
        ]

    def near(self):
        ring = self.copies()
        ring[2].start()
        ring[3].start()

    def far(self):
        ring = self.copies()
        ring[0].start()
        ring[1].start()

    def add_far(self):
        ring = self.copies()
        for index, slot, half in ((0, 1, 0), (1, 2, 1)):
            ring[index].wait_recv()
            self.relayed[index] = (
                self.part(slot, half)[...].astype(f32) + self.landed[index].astype(f32)
            ).astype(bf16)
            ring[4 + index].start()

    def finish(self, half, pack):
        e, z, right, left = place()
        ring = self.copies()
        direct, summed = (3, 4) if half == 0 else (2, 5)
        ring[direct].wait_recv()
        ring[summed].wait_recv()
        total = (
            self.part(0, half)[...].astype(f32)
            + self.landed[direct].astype(f32)
            + self.landed[summed].astype(f32)
        ).astype(bf16)
        flat = jnp.concatenate([total[0], total[1]], axis=0)
        self.spread[256 * half : 256 * half + 256] = dot_rows(pack, flat).astype(bf16)

        def send(d, carry):
            pltpu.make_async_remote_copy(
                self.spread.at[block_at(d)],
                self.home.at[block_at(e)],
                self.plane_out,
                self.plane_in,
                device_id=(plane_source(e, d), z),
                device_id_type=MESH,
            ).start()
            return carry

        lax.fori_loop(max(1, 16 * half), 16 * half + 16, send, 0)
        if half == 0:
            self.home[block_at(e)] = self.spread[0:BLOCK]

    def arrive(self):
        drain(self.home.at[pl.ds(0, (PLANE - 1) * BLOCK)], self.plane_in)

    def close(self):
        for copy in self.copies():
            copy.wait_send()
        drain(self.spread.at[pl.ds(0, (PLANE - 1) * BLOCK)], self.plane_out)


RETURN_SCRATCH = [
    pltpu.VMEM((2, 2, HALF, 768), bf16),
    pltpu.VMEM((6, 2, HALF, 768), bf16),
    pltpu.VMEM((PAD, 768), bf16),
    pltpu.VMEM((PAD, 768), bf16),
    pltpu.SemaphoreType.DMA((6,)),
    pltpu.SemaphoreType.DMA((6,)),
    pltpu.SemaphoreType.DMA,
    pltpu.SemaphoreType.DMA,
]


def kernel_params(collective_id):
    return pltpu.CompilerParams(
        collective_id=collective_id, has_side_effects=True, vmem_limit_bytes=60 * 1024 * 1024
    )


VMEM = pl.BlockSpec(memory_space=pltpu.VMEM)


def expert_kernel(
    send, grad_rows, weight_in, weight_out, picked, resid, cotangent, gain_moe,
    x_out, hidden, grad_pre, y_part, grad_resid, gain_part,
    landed, held_in, held_out, grad_part, load_sems,
    d0, d1, d2, d3, *back,
):
    loads = [
        pltpu.make_async_copy(weight_in, held_in, load_sems.at[0]),
        pltpu.make_async_copy(weight_out, held_out, load_sems.at[1]),
    ]
    for load in loads:
        load.start()
    greet(1, 1)
    out_way = Dispatch(send, landed, x_out, (d0, d1, d2, d3))
    home_way = Return(grad_part, back[0], back[1], back[2], back[3], back[4:])
    out_way.cross()
    pack = packer()
    out_way.turn(0, pack)
    out_way.turn(1, pack)
    for load in loads:
        load.wait()

    def run(first, count):
        for j in range(2):
            span = pl.ds(first * 160, count * 160)
            pre_act = dot(x_out[j, span], held_in[j])
            cdf = 0.5 * (1.0 + lax.erf(pre_act * inv_root_two))
            hidden[j, span] = (pre_act * cdf).astype(bf16)
            slope = cdf + pre_act * jnp.exp(-0.5 * pre_act * pre_act) * inv_root_tau
            grad_hidden = dot_cols(grad_rows[j, span], held_out[j])
            grad_pre[j, span] = (grad_hidden * slope).astype(bf16)
            grad_part[j, span] = dot_cols(grad_pre[j, span], held_in[j]).astype(bf16)

    run(0, 1)
    out_way.relay()
    run(1, 2)
    home_way.near()
    out_way.last()
    run(3, 1)
    home_way.far()
    for j in range(2):
        y_part[j, 0:320] = dot(hidden[j, 0:320], held_out[j]).astype(bf16)
    home_way.add_far()
    for j in range(2):
        y_part[j, 320:640] = dot(hidden[j, 320:640], held_out[j]).astype(bf16)
    home_way.finish(0, pack)
    home_way.finish(1, pack)
    home_way.arrive()
    grad_normed = dot(picked[0] + picked[1], home_way.home[...])
    residual = resid[...]
    scale = rms_scale(residual)
    normal = residual * scale
    gain_part[...] = jnp.sum(grad_normed * normal, axis=0, keepdims=True)
    grad_unit = grad_normed * gain_moe[...]
    grad_resid[...] = cotangent[...].astype(f32) + scale * (
        grad_unit - normal * jnp.mean(grad_unit * normal, axis=1, keepdims=True)
    )
    out_way.close()
    home_way.close()


def run_experts(send, grad_rows, weight_in, weight_out, *local):
    rows = jax.ShapeDtypeStruct((2, EXPERT_ROWS, 768), bf16)
    anywhere = pl.BlockSpec(memory_space=pl.ANY)
    return pl.pallas_call(
        expert_kernel,
        out_shape=[
            rows,
            rows,
            rows,
            rows,
            jax.ShapeDtypeStruct((128, 768), f32),
            jax.ShapeDtypeStruct((1, 768), f32),
        ],
        in_specs=[VMEM, VMEM, anywhere, anywhere] + [VMEM] * 4,
        out_specs=[VMEM] * 6,
        scratch_shapes=[
            pltpu.VMEM((PAD, 768), bf16),
            pltpu.VMEM((2, 768, 768), bf16),
            pltpu.VMEM((2, 768, 768), bf16),
            pltpu.VMEM((2, EXPERT_ROWS, 768), bf16),
            pltpu.SemaphoreType.DMA((2,)),
        ]
        + DISPATCH_SCRATCH
        + RETURN_SCRATCH,
        compiler_params=kernel_params(3),
        name="experts",
    )(send, grad_rows, weight_in, weight_out, *local)


SEQ = 512
SIDE = 64
WIDTH = 768
HEAD_WIDTH = 192
LOCAL_HEADS = 3
score_scale = HEAD_DIM ** (-0.5)


class RingGather:
    def __init__(self, rows, sems):
        self.rows = rows
        self.out, self.arrived = sems

    def copies(self):
        e, z, right, left = place()

        def copy(index, owner, half, other):
            block = self.rows.at[pl.ds(pl.multiple_of(owner * 128 + half * SIDE, SIDE), SIDE)]
            return pltpu.make_async_remote_copy(
                block,
                block,
                self.out.at[index],
                self.arrived.at[index],
                device_id=(e, other),
                device_id_type=MESH,
            )

        def landing(index, owner, half):
            block = self.rows.at[pl.ds(pl.multiple_of(owner * 128 + half * SIDE, SIDE), SIDE)]
            return pltpu.make_async_copy(block, block, self.arrived.at[index])

        far = lax.rem(z + 2, RING)
        sends = [
            copy(0, z, 0, right),
            copy(1, z, 1, right),
            copy(2, z, 0, left),
            copy(3, z, 1, left),
            copy(4, left, 0, right),
            copy(5, right, 1, left),
        ]
        lands = [
            landing(0, left, 0),
            landing(1, left, 1),
            landing(2, right, 0),
            landing(3, right, 1),
            landing(4, far, 0),
            landing(5, far, 1),
        ]
        return sends, lands

    def start(self):
        sends, lands = self.copies()
        for index in (0, 3, 1, 2):
            sends[index].start()

    def finish(self):
        sends, lands = self.copies()
        lands[0].wait()
        sends[4].start()
        lands[3].wait()
        sends[5].start()
        for index in (1, 2, 4, 5):
            lands[index].wait()

    def close(self):
        sends, lands = self.copies()
        for send in sends:
            send.wait_send()


GATHER_SCRATCH = [pltpu.SemaphoreType.DMA((6,)), pltpu.SemaphoreType.DMA((6,))]


class RingSum:
    def __init__(self, partial, relayed, landed, sems):
        self.partial, self.relayed, self.landed = partial, relayed, landed
        self.out, self.arrived = sems

    def part(self, slot, half):
        e, z, right, left = place()
        owner = (z, right, left, lax.rem(z + 2, RING))[slot]
        return self.partial.at[pl.ds(pl.multiple_of(owner * 128 + half * SIDE, SIDE), SIDE)]

    def copies(self):
        e, z, right, left = place()

        def copy(index, source, other):
            return pltpu.make_async_remote_copy(
                source,
                self.landed.at[index],
                self.out.at[index],
                self.arrived.at[index],
                device_id=(e, other),
                device_id_type=MESH,
            )

        part = self.part
        return [
            copy(0, part(3, 0), right),
            copy(1, part(3, 1), left),
            copy(2, part(1, 1), right),
            copy(3, part(2, 0), left),
            copy(4, self.relayed.at[0], right),
            copy(5, self.relayed.at[1], left),
        ]

    def start(self):
        ring = self.copies()
        for index in range(4):
            ring[index].start()

    def add_far(self):
        ring = self.copies()
        for index, slot, half in ((0, 1, 0), (1, 2, 1)):
            ring[index].wait_recv()
            self.relayed[index] = (
                self.part(slot, half)[...].astype(f32) + self.landed[index].astype(f32)
            ).astype(bf16)
            ring[4 + index].start()

    def total(self):
        ring = self.copies()
        halves = []
        for half, direct, summed in ((0, 3, 4), (1, 2, 5)):
            ring[direct].wait_recv()
            ring[summed].wait_recv()
            halves.append(
                self.part(0, half)[...].astype(f32)
                + self.landed[direct].astype(f32)
                + self.landed[summed].astype(f32)
            )
        return jnp.concatenate(halves, axis=0)

    def close(self):
        for copy in self.copies():
            copy.wait_send()


SUM_SCRATCH = [
    pltpu.VMEM((SEQ, WIDTH), bf16),
    pltpu.VMEM((2, SIDE, WIDTH), bf16),
    pltpu.VMEM((6, SIDE, WIDTH), bf16),
    pltpu.SemaphoreType.DMA((6,)),
    pltpu.SemaphoreType.DMA((6,)),
]


def head_mask(h):
    lane = lax.broadcasted_iota(jnp.int32, (SEQ, HEAD_WIDTH), 1)
    return (lane >= h * HEAD_DIM) & (lane < (h + 1) * HEAD_DIM)


def sum_diagonals(square):
    rows = square
    for step in (32, 8, 1):
        count = rows.shape[0] // step
        rows = sum(
            pltpu.roll(rows[a * step : a * step + step], (SEQ - a * step) % SEQ, 1)
            if a
            else rows[:step]
            for a in range(count)
        )
    return rows


def bucket_hot_rows(bucket_rev):
    return (bucket_rev == lax.broadcasted_iota(jnp.int32, (32, SEQ), 0)).astype(f32)


def plane_sends(source_at, target_at, send_sem, recv_sem):
    e, z, right, left = place()

    def send(chip, carry):
        other = plane_target(e, chip * 2)
        pltpu.make_async_remote_copy(
            source_at(other // 2),
            target_at(e // 2),
            send_sem,
            recv_sem,
            device_id=(other, z),
            device_id_type=MESH,
        ).start()
        return carry

    lax.fori_loop(1, 16, send, 0)


def rms_scale(values):
    return lax.rsqrt(jnp.mean(values * values, axis=1, keepdims=True) + epsilon)


def select_rows(ids):
    expert = lax.broadcasted_iota(jnp.int32, (128, 64), 1)
    hot = [(ids[:, c : c + 1] == expert).astype(f32) for c in range(TOPK)]
    row = lax.broadcasted_iota(jnp.int32, (128, 128), 0)
    col = lax.broadcasted_iota(jnp.int32, (128, 128), 1)
    before = dot((col < row).astype(bf16), (hot[0] + hot[1]).astype(bf16))
    pos = lax.broadcasted_iota(jnp.int32, (128, PAD), 1)
    picks = []
    for c in range(TOPK):
        slot = jnp.sum(before * hot[c], axis=1, keepdims=True).astype(jnp.int32)
        own = ids[:, c : c + 1]
        first = own // 2
        picks.append((pos == first * BLOCK + (own - first * 2) * 5 + slot).astype(bf16))
    return picks


def attend_kernel(
    tokens, gain_attn, gain_moe, weights, cotangent, ids, gates, bias, bucket_rev,
    resid, units, whole, qkv, probs, attended, picked, send_rows, grad_rows,
    wall, whole32, grad_send, grad_landed, w_send, w_recv, s_send, s_recv,
    d0, d1, d2, d3, g0, g1, *ring_sum,
):
    e, z, right, left = place()
    core, chip = lax.rem(e, 2), e // 2
    greet(1, 1)
    wall[core, chip] = weights[...]
    plane_sends(
        lambda other: weights, lambda own: wall.at[core, own], w_send, w_recv
    )
    inputs = tokens[...].astype(f32)
    own_rows = pl.ds(pl.multiple_of(z * 128, 128), 128)
    units[own_rows] = (inputs * rms_scale(inputs)).astype(bf16)
    gather = RingGather(units, (g0, g1))
    gather.start()

    picks = select_rows(ids[...])
    for c in range(TOPK):
        picked[c] = picks[c]
    grad_out = cotangent[...].astype(f32)
    grad_send[...] = (
        dot_rows(picks[0], (gates[:, 0:1] * grad_out).astype(bf16))
        + dot_rows(picks[1], (gates[:, 1:2] * grad_out).astype(bf16))
    ).astype(bf16)
    grads = Dispatch(grad_send, grad_landed, grad_rows, (d0, d1, d2, d3))
    grads.cross()

    drain(wall.at[0, pl.ds(0, 15)], w_recv)
    sibling = pltpu.make_async_remote_copy(
        wall.at[core],
        wall.at[core],
        s_send,
        s_recv,
        device_id=(chip * 2 + 1 - core, z),
        device_id_type=MESH,
    )
    sibling.start()
    hot = bucket_hot_rows(bucket_rev[...])
    gather.finish()
    normed = (units[...].astype(f32) * gain_attn[...]).astype(bf16)
    pltpu.make_async_copy(wall.at[1 - core], wall.at[1 - core], s_recv).wait()
    for block in range(PLANE):
        whole32[24 * block : 24 * block + 24] = wall[block % 2, block // 2].astype(f32)[:24]
    whole[...] = whole32[...].astype(bf16)
    projected = dot(normed, whole[:, :640]).astype(bf16)
    qkv[...] = projected[:, : 3 * HEAD_WIDTH]
    queries = projected[:, :HEAD_WIDTH]
    keys = projected[:, HEAD_WIDTH : 2 * HEAD_WIDTH]
    values = projected[:, 2 * HEAD_WIDTH : 3 * HEAD_WIDTH]

    pack = packer()
    grads.turn(0, pack)
    grads.turn(1, pack)

    row = lax.broadcasted_iota(jnp.int32, (SEQ, SEQ), 0)
    col = lax.broadcasted_iota(jnp.int32, (SEQ, SEQ), 1)
    mixed = jnp.zeros((SEQ, HEAD_WIDTH), f32)
    for h in range(LOCAL_HEADS):
        mask = head_mask(h)
        rel = jnp.sum(bias[:, h : h + 1] * hot, axis=0, keepdims=True)
        shifted = pltpu.roll(jnp.broadcast_to(rel, (SEQ, SEQ)), 0, 1, stride=1, stride_axis=0)
        scores = dot_cols(jnp.where(mask, queries, jnp.zeros_like(queries)), keys) * score_scale
        scores = jnp.where(col <= row, scores + shifted, masked_value)
        raised = jnp.exp(scores - jnp.max(scores, axis=1, keepdims=True))
        weights_p = (raised / jnp.sum(raised, axis=1, keepdims=True)).astype(bf16)
        probs[h] = weights_p
        mixed = jnp.where(mask, dot(weights_p, values), mixed)
        if h == 0:
            grads.relay()
    attended[...] = mixed.astype(bf16)
    summing = RingSum(ring_sum[0], ring_sum[1], ring_sum[2], ring_sum[3:])
    ring_sum[0][...] = dot_cols(attended[...], whole[:, 3 * HEAD_WIDTH :]).astype(bf16)
    summing.start()
    summing.add_far()
    residual = inputs + summing.total()
    resid[...] = residual
    normed_m = (residual * rms_scale(residual) * gain_moe[...]).astype(bf16)
    send_rows[...] = dot_rows(picks[0] + picks[1], normed_m).astype(bf16)
    grads.last()
    gather.close()
    grads.close()
    summing.close()
    sibling.wait_send()
    drain(wall.at[0, pl.ds(0, 15)], w_send)


def attend(*operands):
    def shape(dims, kind=bf16):
        return jax.ShapeDtypeStruct(dims, kind)

    return pl.pallas_call(
        attend_kernel,
        out_shape=[
            shape((128, WIDTH), f32),
            shape((SEQ, WIDTH)),
            shape((WIDTH, WIDTH)),
            shape((SEQ, 3 * HEAD_WIDTH)),
            shape((LOCAL_HEADS, SEQ, SEQ)),
            shape((SEQ, HEAD_WIDTH)),
            shape((TOPK, 128, PAD)),
            shape((PAD, WIDTH)),
            shape((2, EXPERT_ROWS, WIDTH)),
        ],
        in_specs=[VMEM] * 9,
        out_specs=[VMEM] * 9,
        scratch_shapes=[
            pltpu.VMEM((2, 16, 32, WIDTH), bf16),
            pltpu.VMEM((WIDTH, WIDTH), f32),
            pltpu.VMEM((PAD, WIDTH), bf16),
            pltpu.VMEM((PAD, WIDTH), bf16),
            pltpu.SemaphoreType.DMA,
            pltpu.SemaphoreType.DMA,
            pltpu.SemaphoreType.DMA,
            pltpu.SemaphoreType.DMA,
        ]
        + DISPATCH_SCRATCH
        + GATHER_SCRATCH
        + SUM_SCRATCH,
        compiler_params=kernel_params(1),
        name="attend",
    )(*operands)


def attend_back_kernel(
    grad_resid, y_part, units, whole, qkv, probs, attended, tokens, resid, gates, picked,
    gain_attn, gain_moe_part, bucket_rev,
    out, grad_input, weight_grad, small,
    seq_grad, blocks, near_blocks, plane_landed, small_own, small_landed,
    s_send, s_recv, p_send, p_recv, t_send, t_recv, g0, g1, *rest,
):
    e, z, right, left = place()
    core, chip = lax.rem(e, 2), e // 2
    opposite = lax.rem(z + 2, RING)
    ring_sum, back = rest[:5], rest[5:]
    greet(1, 1, 1)
    own_rows = pl.ds(pl.multiple_of(z * 128, 128), 128)
    seq_grad[own_rows] = grad_resid[...].astype(bf16)
    gather = RingGather(seq_grad, (g0, g1))
    gather.start()
    home_way = Return(y_part, back[0], back[1], back[2], back[3], back[4:])
    hot = bucket_hot_rows(bucket_rev[...])
    proj = whole[:, 3 * HEAD_WIDTH :]
    queries = qkv[:, :HEAD_WIDTH]
    keys = qkv[:, HEAD_WIDTH : 2 * HEAD_WIDTH]
    values = qkv[:, 2 * HEAD_WIDTH :]
    gather.finish()
    home_way.far()
    home_way.near()
    grad_att = dot(seq_grad[...], proj).astype(bf16)
    proj_part = dot_rows(seq_grad[...], attended[...])
    zeros = jnp.zeros((SEQ, HEAD_WIDTH), f32)
    grad_q, grad_k, grad_v = zeros, zeros, zeros
    diagonals = []
    for h in range(LOCAL_HEADS):
        mask = head_mask(h)
        weights_p = probs[h]
        soft = weights_p.astype(f32)
        grad_w = dot_cols(jnp.where(mask, grad_att, jnp.zeros_like(grad_att)), values)
        row_dot = jnp.sum(soft * grad_w, axis=1, keepdims=True)
        grad_s = soft * (grad_w - row_dot)
        grad_scores = grad_s.astype(bf16)
        diagonals.append(sum_diagonals(grad_scores.astype(f32)))
        grad_q = jnp.where(mask, dot(grad_scores, keys), grad_q)
        grad_k = jnp.where(mask, dot_rows(grad_scores, queries), grad_k)
        grad_v = jnp.where(mask, dot_rows(weights_p, grad_att), grad_v)
        if h == 0:
            home_way.add_far()
    grad_qkv = jnp.concatenate(
        [grad_q * score_scale, grad_k * score_scale, grad_v], axis=1
    ).astype(bf16)
    grad_normed = dot_cols(grad_qkv, whole[:, : 3 * HEAD_WIDTH])
    summing = RingSum(ring_sum[0], ring_sum[1], ring_sum[2], ring_sum[3:])
    ring_sum[0][...] = grad_normed.astype(bf16)
    summing.start()
    unit_rows = units[...].astype(f32)
    gain_part = jnp.sum(grad_normed * unit_rows, axis=0, keepdims=True)
    normed = (unit_rows * gain_attn[...]).astype(bf16)
    qkv_part = dot_rows(normed, grad_qkv)
    full = jnp.concatenate([qkv_part, proj_part], axis=1)
    diagonal = jnp.concatenate(diagonals + [jnp.zeros((5, SEQ), f32)], axis=0)
    table_rows = lax.dot_general(
        diagonal, hot, (((1,), (1,)), ((), ())), precision=highest, preferred_element_type=f32
    )
    table_wide = jnp.concatenate([table_rows[:LOCAL_HEADS], jnp.zeros((3, 32), f32)], axis=0)
    table_wide = jnp.concatenate([table_wide, jnp.zeros((6, WIDTH - 32), f32)], axis=1)
    extra = jnp.concatenate([gain_part, gain_moe_part[...], table_wide], axis=0)
    for block in range(PLANE):
        blocks[block % 2, block // 2] = jnp.concatenate(
            [full[24 * block : 24 * block + 24], extra], axis=0
        ).astype(bf16)
    sibling = pltpu.make_async_remote_copy(
        blocks.at[1 - core],
        near_blocks,
        s_send,
        s_recv,
        device_id=(chip * 2 + 1 - core, z),
        device_id_type=MESH,
    )
    sibling.start()
    pack = packer()
    home_way.finish(0, pack)
    home_way.finish(1, pack)
    sibling.wait_recv()
    near_blocks[...] = (blocks[core].astype(f32) + near_blocks[...].astype(f32)).astype(bf16)
    plane_sends(
        lambda other: near_blocks.at[other], lambda own: plane_landed.at[own], p_send, p_recv
    )
    plane_landed[chip] = near_blocks[chip]
    summing.add_far()
    inputs = tokens[...].astype(f32)
    scale_first = rms_scale(inputs)
    normal_first = inputs * scale_first
    grad_unit = summing.total() * gain_attn[...]
    grad_input[...] = grad_resid[...] + scale_first * (
        grad_unit - normal_first * jnp.mean(grad_unit * normal_first, axis=1, keepdims=True)
    )
    home_way.arrive()
    home = home_way.home[...]
    out[...] = (
        resid[...] + gates[:, 0:1] * dot(picked[0], home) + gates[:, 1:2] * dot(picked[1], home)
    ).astype(bf16)
    drain(plane_landed.at[pl.ds(0, 15)], p_recv)
    total = plane_landed[0].astype(f32)
    for block in range(1, 16):
        total = total + plane_landed[block].astype(f32)
    weight_grad[...] = total[:24]
    small_own[...] = total[24:]
    shares = [
        pltpu.make_async_remote_copy(
            small_own,
            small_landed.at[index],
            t_send.at[index],
            t_recv.at[index],
            device_id=(e, other),
            device_id_type=MESH,
        )
        for index, other in enumerate((right, left, opposite))
    ]
    for share in shares:
        share.start()
    for share in shares:
        share.wait_recv()
    summed = small_own[...] + small_landed[0] + small_landed[1] + small_landed[2]
    line = lax.broadcasted_iota(jnp.int32, (8, WIDTH), 0)
    small[...] = jnp.where(line < 2, summed, small_own[...])
    for share in shares:
        share.wait_send()
    gather.close()
    home_way.close()
    summing.close()
    sibling.wait_send()
    drain(plane_landed.at[pl.ds(0, 15)], p_send)


def attend_back(*operands):
    def shape(dims, kind=f32):
        return jax.ShapeDtypeStruct(dims, kind)

    return pl.pallas_call(
        attend_back_kernel,
        out_shape=[
            shape((128, WIDTH), bf16),
            shape((128, WIDTH)),
            shape((24, WIDTH)),
            shape((8, WIDTH)),
        ],
        in_specs=[VMEM] * 14,
        out_specs=[VMEM] * 4,
        scratch_shapes=[
            pltpu.VMEM((SEQ, WIDTH), bf16),
            pltpu.VMEM((2, 16, 32, WIDTH), bf16),
            pltpu.VMEM((16, 32, WIDTH), bf16),
            pltpu.VMEM((16, 32, WIDTH), bf16),
            pltpu.VMEM((8, WIDTH), f32),
            pltpu.VMEM((3, 8, WIDTH), f32),
            pltpu.SemaphoreType.DMA,
            pltpu.SemaphoreType.DMA,
            pltpu.SemaphoreType.DMA,
            pltpu.SemaphoreType.DMA,
            pltpu.SemaphoreType.DMA((3,)),
            pltpu.SemaphoreType.DMA((3,)),
        ]
        + GATHER_SCRATCH
        + SUM_SCRATCH
        + RETURN_SCRATCH,
        compiler_params=kernel_params(2),
        name="attend_back",
    )(*operands)


def body(
    tokens,
    gain_attn,
    gain_moe,
    qkv_weight,
    proj_weight,
    bias_table,
    expert_in,
    expert_out,
    expert_ids,
    gate_values,
    bucket_table,
    cotangent,
):
    share = qkv_weight.shape[0]
    weights = jnp.concatenate([qkv_weight.reshape(share, 3 * HEAD_WIDTH), proj_weight.T], axis=1)
    weights = jnp.pad(weights, ((0, 8), (0, 0)))
    gain_first, gain_second = gain_attn[None], gain_moe[None]
    bucket_rev = jnp.concatenate([bucket_table[:1], bucket_table[:0:-1]])[None]
    resid, units, whole, qkv, probs, attended, picked, send_rows, grad_rows = attend(
        tokens, gain_first, gain_second, weights, cotangent, expert_ids, gate_values,
        bias_table, bucket_rev,
    )
    received, hidden, grad_pre, y_part, grad_resid, gain_part = run_experts(
        send_rows, grad_rows, expert_in, expert_out, picked, resid, cotangent, gain_second
    )
    out, grad_input, weight_grad, small = attend_back(
        grad_resid, y_part, units, whole, qkv, probs, attended, tokens, resid, gate_values,
        picked, gain_first, gain_part, bucket_rev,
    )
    expert_out_grad = jnp.einsum("jrf,jrd->jfd", hidden, grad_rows, preferred_element_type=f32)
    expert_in_grad = jnp.einsum("jrd,jrf->jdf", received, grad_pre, preferred_element_type=f32)
    e, z = lax.axis_index("expert"), lax.axis_index("mp")
    piece = (e * RING + z) * 6
    gains = lax.dynamic_slice_in_dim(small[:2], piece, 6, axis=1)
    table_grad = lax.dynamic_slice_in_dim(small[2 : 2 + LOCAL_HEADS], e, 1, axis=1).T
    return (
        out,
        grad_input,
        gains[0],
        gains[1],
        weight_grad[:, : 3 * HEAD_WIDTH].reshape(share, 3, HEAD_WIDTH),
        weight_grad[:, 3 * HEAD_WIDTH :].T,
        table_grad,
        expert_in_grad,
        expert_out_grad,
    )


def solution(mesh):
    placed = (
        P(("expert", "mp"), None),
        P(),
        P(),
        P("expert", None, "mp"),
        P("mp", "expert"),
        P(None, "mp"),
        P("expert", None, "mp"),
        P("expert", "mp", None),
        P(("expert", "mp"), None),
        P(("expert", "mp"), None),
        P(),
        P(("expert", "mp"), None),
    )
    return jax.shard_map(
        body,
        mesh=mesh,
        in_specs=placed,
        out_specs=(
            P(("expert", "mp"), None),
            P(("expert", "mp"), None),
            P(("expert", "mp")),
            P(("expert", "mp")),
            P("expert", None, "mp"),
            P("mp", "expert"),
            P("expert", "mp"),
            P("expert", None, "mp"),
            P("expert", "mp", None),
        ),
        check_vma=False,
    )
```

time: 508 us -> 213 us (0.42)
  blocking collectives: 219 us -> 0 us
  local copies, waits for them, and re-layouts: 63.8 us -> 16.9 us
  Pallas kernels: 140 us -> 182 us
  matrix products: 36.3 us -> 10.2 us
  other arithmetic: 23.8 us -> 2.65 us
  between operations: 14.8 us -> 0.7 us
    unnamed x2 -> x0, blocking collectives: 139 us -> none
    all_gather x4 -> x0, blocking collectives: 79.9 us -> none  [the longest x1 25.2 us: body(): lax.all_gather(proj_weight, 'expert', axis=1, tiled=True)]
    pallas_call x2, Pallas kernels: 74.5 us -> 118 us  [the longest x1 59.2 us: attend_back(): pl.pallas_call(attend_back_kernel, out_shape=[shape((128, WIDTH), bf16),...]
    dot_general x22 -> x2, matrix products: 36.3 us -> 10.2 us  [the longest x1 5.93 us: body(): jnp.einsum('jrd,jrf->jdf', received, grad_pre, preferred_element_type=f32)]
    unnamed x115 -> x19, local copies, waits for them, and re-layouts: 31.6 us -> 7.24 us
    reshape x3 -> x2, local copies, waits for them, and re-layouts: 19 us -> 0.2 us  [the longest x1 0.1 us: body(): qkv_weight.reshape(share, 3 * HEAD_WIDTH)]
    reduce_sum x6 -> x0, other arithmetic: 10.7 us -> none  [the longest x1 6.76 us: bias_gradient(): along = jnp.sum(flat.reshape(local_heads, block_rows, period), axis=1)]
    reshape x1 -> x0, other arithmetic: 6.63 us -> none  [bias_gradient(): along = jnp.sum(flat.reshape(local_heads, block_rows, period), axis=1)]
  transfers between devices with their start and end apart: 4 -> 0, of which waited for: 1 -> 0; matrix products, arithmetic and copies ran while one was open for 12% -> 0% of each run, Pallas kernels for 15% -> 0%
where the time goes in v2:
time: 213 us
  Pallas kernels  182 us (85%)
  local copies, waits for them, and re-layouts  16.9 us (8%)
  matrix products  10.2 us (5%)
  other arithmetic  2.65 us (1%)
    pallas_call x1, Pallas kernels, run_experts(): pl.pallas_call(expert_kernel, out_shape=[rows, rows, rows, rows, jax.Shap...  64.6 us
    pallas_call x1, Pallas kernels, attend_back(): pl.pallas_call(attend_back_kernel, out_shape=[shape((128, WIDTH), bf16),...  59.2 us
    pallas_call x1, Pallas kernels, attend(): pl.pallas_call(attend_kernel, out_shape=[shape((128, WIDTH), f32), shape(...  58.5 us
    unnamed x19, local copies, waits for them, and re-layouts  7.24 us
    dot_general x1, matrix products, body(): jnp.einsum('jrd,jrf->jdf', received, grad_pre, preferred_element_type=f32)  5.93 us
    dot_general x1, matrix products, body(): jnp.einsum('jrf,jrd->jfd', hidden, grad_rows, preferred_element_type=f32)  4.29 us

profile of v2, /device:TPU:0, one launch (start us, length us, event | category | flops | bytes accessed | tf_op | source)
XLA Modules:
  0.0 212.8 jit_solution(15058970799520766766)
XLA Ops:
  0.6 1.3 broadcast_in_dim.9.gain_attn
  1.9 1.3 broadcast_in_dim.10.gain_moe
  3.2 0.8 copy.29
  4.0 0.1 reshape.24
  4.1 1.4 fusion.2.weights
  5.5 1.4 copy.30.ids
  6.9 1.4 copy.31.gates
  8.3 1.4 copy.32.bias
  9.7 0.8 slice.25
  10.4 0.1 reverse
  10.5 0.1 slice.35
  10.6 1.2 slice.24
  11.8 1.2 pad_add_fusion
  13.0 58.5 %attend.1 = (f32[128,768]{1,0:T(8,128)}, bf16[512,768]{1,0:T(8,128)(2,1)}, bf16[768,768]{1,0:T(8,128)(2,1)}, bf16[512,576]{1,0:T(8,128)(2,1)}, bf16[3,512,512]{2...) custom-call(bf16[128,768]{1,0:T(8,128)(2,1)} %tokens.3, ...), custom_call_target="tpu_custom_call" | custom-call | tf_op jit(solution)/shard_map/attend/pallas_call | solution.py:689
  71.6 64.6 %experts.1 = (bf16[2,640,768]{2,1,0:T(8,128)(2,1)}, bf16[2,640,768]{2,1,0:T(8,128)(2,1)}, bf16[2,640,768]{2,1,0:T(8,128)(2,1)}, bf16[2,640,768]{2,1,0:T(8,128)(2...) custom-call(bf16[512,768]{1,0:T(8,128)(2,1)} %get-tuple-element.28.send, bf16[2,640,768]{2,1,0:T(8,128)(2,1)} %get-tuple-element.29.grad_rows, ...), custom_call_target="tpu_custom_call" | custom-call | tf_op jit(solution)/shard_map/experts/pallas_call | solution.py:363
  136.1 0.0 copy-start.4
  136.1 59.2 %attend_back.1 = (bf16[128,768]{1,0:T(8,128)(2,1)}, f32[128,768]{1,0:T(8,128)}, f32[24,768]{1,0:T(8,128)}, f32[8,768]{1,0:T(8,128)}) custom-call(f32[128,768]{1,0:T(8,128)} %get-tuple-element.32.grad_resid, bf16[2,640,768]{2,1,0:T(8,128)(2,1)} %get-tuple-element.33.y_part, bf16[512,768]{1,0:T(8,128)(2,1)} %get-tuple-element.34.units, ...), custom_call_target="tpu_custom_call" | custom-call | tf_op jit(solution)/shard_map/attend_back/pallas_call | solution.py:857
  195.4 0.7 slice.26
  196.1 0.1 constant_dynamic-slice_fusion
  196.2 0.5 slice_bitcast_fusion.1
  196.7 0.8 slice.29
  197.6 0.1 reshape.25
  197.7 0.6 copy.36
  198.3 1.4 slice_bitcast_fusion
  199.7 0.7 slice.31
  200.5 0.7 dynamic-slice_reduce_fusion
  201.2 0.0 copy-done.4
  201.2 0.0 copy-start
  201.2 0.0 copy-start.3
  201.2 5.9 %fusion.3 = f32[2,768,768]{2,1,0:T(8,128)} fusion(bf16[2,640,768]{2,1,0:T(8,128)(2,1)S(1)} %copy-done.4, bf16[2,640,768]{2,1,0:T(8,128)(2,1)} %get-tuple-element.45), kind=kOutput, calls=%fused_computation.10 | convolution fusion | flops 1509949440 | bytes 8650752 | tf_op jit(solution)/shard_map/jrd,jrf->jdf/dot_general | solution.py:920
  207.1 0.0 copy-done
  207.1 0.0 copy-done.3
  207.1 0.0 copy-start.2
  207.1 0.0 copy-start.1
  207.1 4.3 %fusion.4 = f32[2,768,768]{2,1,0:T(8,128)} fusion(bf16[2,640,768]{2,1,0:T(8,128)(2,1)S(1)} %copy-done.3, bf16[2,640,768]{2,1,0:T(8,128)(2,1)S(1)} %copy-done), kind=kOutput, calls=%fused_computation.11 | convolution fusion | flops 1509949440 | bytes 8650752 | tf_op jit(solution)/shard_map/jrf,jrd->jfd/dot_general | solution.py:919
  211.4 0.0 copy-done.2
  211.4 0.7 copy.41
  212.1 0.0 copy-done.1
  212.1 0.7 copy.42
Async XLA Ops:
  136.1 65.0 %copy-start.4 = (bf16[2,640,768]{2,1,0:T(8,128)(2,1)S(1)}, bf16[2,640,768]{2,1,0:T(8,128)(2,1)}, u32[]{:S(2)}) copy-start(bf16[2,640,768]{2,1,0:T(8,128)(2,1)} %get-tuple-element.44) | copy-start | bytes 5898244
  201.2 5.9 %copy-start = (bf16[2,640,768]{2,1,0:T(8,128)(2,1)S(1)}, bf16[2,640,768]{2,1,0:T(8,128)(2,1)}, u32[]{:S(2)}) copy-start(bf16[2,640,768]{2,1,0:T(8,128)(2,1)} %get-tuple-element.29.grad_rows) | copy-start | bytes 5898244
  201.2 5.9 %copy-start.3 = (bf16[2,640,768]{2,1,0:T(8,128)(2,1)S(1)}, bf16[2,640,768]{2,1,0:T(8,128)(2,1)}, u32[]{:S(2)}) copy-start(bf16[2,640,768]{2,1,0:T(8,128)(2,1)} %get-tuple-element.46) | copy-start | bytes 5898244
  207.1 4.3 %copy-start.2 = (bf16[128,768]{1,0:T(8,128)(2,1)S(1)}, bf16[128,768]{1,0:T(8,128)(2,1)}, u32[]{:S(2)}) copy-start(bf16[128,768]{1,0:T(8,128)(2,1)} %get-tuple-element.76) | copy-start | bytes 589828
  207.1 5.0 %copy-start.1 = (f32[128,768]{1,0:T(8,128)S(1)}, f32[128,768]{1,0:T(8,128)}, u32[]{:S(2)}) copy-start(f32[128,768]{1,0:T(8,128)} %get-tuple-element.77) | copy-start | bytes 1179652

commit v3 on v2

--- a/solution.py
+++ b/solution.py
@@ -106,7 +106,7 @@
     def part(self, slot, half):
         return self.rows.at[:, pl.ds(slot * 160 + half * HALF, HALF)]
 
-    def cross(self):
+    def cross(self, half):
         e, z, right, left = place()
 
         def send(d, carry):
@@ -114,15 +114,19 @@
             pltpu.make_async_remote_copy(
                 self.send.at[block_at(other)],
                 self.landed.at[block_at(d)],
-                self.plane_out,
-                self.plane_in.at[d // 16],
+                self.plane_out.at[half],
+                self.plane_in.at[half],
                 device_id=(other, z),
                 device_id_type=MESH,
             ).start()
             return carry
 
-        lax.fori_loop(1, PLANE, send, 0)
-        self.landed[0:BLOCK] = self.send[block_at(e)]
+        lax.fori_loop(max(1, 16 * half), 16 * half + 16, send, 0)
+        if half == 0:
+            self.landed[0:BLOCK] = self.send[block_at(e)]
+
+    def crossed(self, half):
+        drain(self.send.at[pl.ds(0, (15 + half) * BLOCK)], self.plane_out.at[half])
 
     def copy(self, index, source, target, other):
         e = lax.axis_index("expert")
@@ -175,11 +179,10 @@
     def close(self):
         for copy in self.copies():
             copy.wait_send()
-        drain(self.send.at[pl.ds(0, (PLANE - 1) * BLOCK)], self.plane_out)
 
 
 DISPATCH_SCRATCH = [
-    pltpu.SemaphoreType.DMA,
+    pltpu.SemaphoreType.DMA((2,)),
     pltpu.SemaphoreType.DMA((2,)),
     pltpu.SemaphoreType.DMA((6,)),
     pltpu.SemaphoreType.DMA((6,)),
@@ -294,96 +297,6 @@
 
 
 VMEM = pl.BlockSpec(memory_space=pltpu.VMEM)
-
-
-def expert_kernel(
-    send, grad_rows, weight_in, weight_out, picked, resid, cotangent, gain_moe,
-    x_out, hidden, grad_pre, y_part, grad_resid, gain_part,
-    landed, held_in, held_out, grad_part, load_sems,
-    d0, d1, d2, d3, *back,
-):
-    loads = [
-        pltpu.make_async_copy(weight_in, held_in, load_sems.at[0]),
-        pltpu.make_async_copy(weight_out, held_out, load_sems.at[1]),
-    ]
-    for load in loads:
-        load.start()
-    greet(1, 1)
-    out_way = Dispatch(send, landed, x_out, (d0, d1, d2, d3))
-    home_way = Return(grad_part, back[0], back[1], back[2], back[3], back[4:])
-    out_way.cross()
-    pack = packer()
-    out_way.turn(0, pack)
-    out_way.turn(1, pack)
-    for load in loads:
-        load.wait()
-
-    def run(first, count):
-        for j in range(2):
-            span = pl.ds(first * 160, count * 160)
-            pre_act = dot(x_out[j, span], held_in[j])
-            cdf = 0.5 * (1.0 + lax.erf(pre_act * inv_root_two))
-            hidden[j, span] = (pre_act * cdf).astype(bf16)
-            slope = cdf + pre_act * jnp.exp(-0.5 * pre_act * pre_act) * inv_root_tau
-            grad_hidden = dot_cols(grad_rows[j, span], held_out[j])
-            grad_pre[j, span] = (grad_hidden * slope).astype(bf16)
-            grad_part[j, span] = dot_cols(grad_pre[j, span], held_in[j]).astype(bf16)
-
-    run(0, 1)
-    out_way.relay()
-    run(1, 2)
-    home_way.near()
-    out_way.last()
-    run(3, 1)
-    home_way.far()
-    for j in range(2):
-        y_part[j, 0:320] = dot(hidden[j, 0:320], held_out[j]).astype(bf16)
-    home_way.add_far()
-    for j in range(2):
-        y_part[j, 320:640] = dot(hidden[j, 320:640], held_out[j]).astype(bf16)
-    home_way.finish(0, pack)
-    home_way.finish(1, pack)
-    home_way.arrive()
-    grad_normed = dot(picked[0] + picked[1], home_way.home[...])
-    residual = resid[...]
-    scale = rms_scale(residual)
-    normal = residual * scale
-    gain_part[...] = jnp.sum(grad_normed * normal, axis=0, keepdims=True)
-    grad_unit = grad_normed * gain_moe[...]
-    grad_resid[...] = cotangent[...].astype(f32) + scale * (
-        grad_unit - normal * jnp.mean(grad_unit * normal, axis=1, keepdims=True)
-    )
-    out_way.close()
-    home_way.close()
-
-
-def run_experts(send, grad_rows, weight_in, weight_out, *local):
-    rows = jax.ShapeDtypeStruct((2, EXPERT_ROWS, 768), bf16)
-    anywhere = pl.BlockSpec(memory_space=pl.ANY)
-    return pl.pallas_call(
-        expert_kernel,
-        out_shape=[
-            rows,
-            rows,
-            rows,
-            rows,
-            jax.ShapeDtypeStruct((128, 768), f32),
-            jax.ShapeDtypeStruct((1, 768), f32),
-        ],
-        in_specs=[VMEM, VMEM, anywhere, anywhere] + [VMEM] * 4,
-        out_specs=[VMEM] * 6,
-        scratch_shapes=[
-            pltpu.VMEM((PAD, 768), bf16),
-            pltpu.VMEM((2, 768, 768), bf16),
-            pltpu.VMEM((2, 768, 768), bf16),
-            pltpu.VMEM((2, EXPERT_ROWS, 768), bf16),
-            pltpu.SemaphoreType.DMA((2,)),
-        ]
-        + DISPATCH_SCRATCH
-        + RETURN_SCRATCH,
-        compiler_params=kernel_params(3),
-        name="experts",
-    )(send, grad_rows, weight_in, weight_out, *local)
 
 
 SEQ = 512
@@ -555,7 +468,7 @@
     return (bucket_rev == lax.broadcasted_iota(jnp.int32, (32, SEQ), 0)).astype(f32)
 
 
-def plane_sends(source_at, target_at, send_sem, recv_sem):
+def plane_sends(source_at, target_at, send_sem, recv_sem_at):
     e, z, right, left = place()
 
     def send(chip, carry):
@@ -564,7 +477,7 @@
             source_at(other // 2),
             target_at(e // 2),
             send_sem,
-            recv_sem,
+            recv_sem_at(e // 2),
             device_id=(other, z),
             device_id_type=MESH,
         ).start()
@@ -593,159 +506,204 @@
     return picks
 
 
-def attend_kernel(
-    tokens, gain_attn, gain_moe, weights, cotangent, ids, gates, bias, bucket_rev,
-    resid, units, whole, qkv, probs, attended, picked, send_rows, grad_rows,
-    wall, whole32, grad_send, grad_landed, w_send, w_recv, s_send, s_recv,
-    d0, d1, d2, d3, g0, g1, *ring_sum,
+def as_column(row):
+    n = row.shape[1]
+    same = lax.broadcasted_iota(jnp.int32, (n, n), 0) == lax.broadcasted_iota(jnp.int32, (n, n), 1)
+    return jnp.sum(jnp.where(same, row, 0.0), axis=1, keepdims=True)
+
+
+def as_row(rows):
+    return jnp.concatenate([rows[i : i + 1] for i in range(rows.shape[0])], axis=1)
+
+
+def layer_kernel(
+    tokens, gain_attn, gain_moe, qkv_weight, proj_weight, bias, weight_in, weight_out,
+    ids, gates, buckets, cotangent,
+    out, grad_input, qkv_grad, proj_grad, gain_first, gain_second, table_out,
+    rows_hbm, hidden_hbm, grad_pre_hbm, grad_rows_hbm,
+    units, whole, probs, picked, resid, mine, wall, whole32,
+    x_send, x_landed, x_rows, g_send, g_landed, g_rows,
+    held_in, held_out, hidden, grad_pre, grad_part, y_part,
+    seq_grad, blocks, near_blocks, plane_landed, small_own, small_landed,
+    load_sems, save_sems, w_send, w_recv, s_send, s_recv, v_send, v_recv,
+    p_send, p_recv, t_send, t_recv, *rest,
 ):
+    x_sems, g_sems, rest = rest[:4], rest[4:8], rest[8:]
+    unit_sems, grad_sems, rest = rest[:2], rest[2:4], rest[4:]
+    sum_a, sum_b, rest = rest[:5], rest[5:10], rest[10:]
+    back_x, back_y = rest[:8], rest[8:]
     e, z, right, left = place()
     core, chip = lax.rem(e, 2), e // 2
-    greet(1, 1)
-    wall[core, chip] = weights[...]
-    plane_sends(
-        lambda other: weights, lambda own: wall.at[core, own], w_send, w_recv
-    )
+    twin = chip * 2 + 1 - core
+    opposite = lax.rem(z + 2, RING)
+    loads = [
+        pltpu.make_async_copy(weight_in, held_in, load_sems.at[0]),
+        pltpu.make_async_copy(weight_out, held_out, load_sems.at[1]),
+    ]
+    for load in loads:
+        load.start()
+    greet(1, 1, 1)
+
+    mine[...] = jnp.concatenate(
+        [qkv_weight[i].astype(f32) for i in range(3)] + [proj_weight[...].astype(f32)], axis=1
+    ).astype(bf16)
+    plane_sends(lambda other: mine, lambda own: wall.at[core, own], w_send, w_recv.at.__getitem__)
     inputs = tokens[...].astype(f32)
     own_rows = pl.ds(pl.multiple_of(z * 128, 128), 128)
     units[own_rows] = (inputs * rms_scale(inputs)).astype(bf16)
-    gather = RingGather(units, (g0, g1))
-    gather.start()
-
-    picks = select_rows(ids[...])
+    unit_ring = RingGather(units, unit_sems)
+    unit_ring.start()
+    wall[core, chip] = mine[...]
+
+    gain_a, gain_m = as_row(gain_attn[...]), as_row(gain_moe[...])
+    id_columns = jnp.concatenate(
+        [as_column(ids[c : c + 1].astype(f32)) for c in range(TOPK)], axis=1
+    ).astype(jnp.int32)
+    gate_columns = [as_column(gates[c : c + 1]) for c in range(TOPK)]
+    picks = select_rows(id_columns)
     for c in range(TOPK):
         picked[c] = picks[c]
     grad_out = cotangent[...].astype(f32)
-    grad_send[...] = (
-        dot_rows(picks[0], (gates[:, 0:1] * grad_out).astype(bf16))
-        + dot_rows(picks[1], (gates[:, 1:2] * grad_out).astype(bf16))
+    g_send[...] = (
+        dot_rows(picks[0], (gate_columns[0] * grad_out).astype(bf16))
+        + dot_rows(picks[1], (gate_columns[1] * grad_out).astype(bf16))
     ).astype(bf16)
-    grads = Dispatch(grad_send, grad_landed, grad_rows, (d0, d1, d2, d3))
-    grads.cross()
-
-    drain(wall.at[0, pl.ds(0, 15)], w_recv)
-    sibling = pltpu.make_async_remote_copy(
-        wall.at[core],
-        wall.at[core],
-        s_send,
-        s_recv,
-        device_id=(chip * 2 + 1 - core, z),
-        device_id_type=MESH,
-    )
-    sibling.start()
-    hot = bucket_hot_rows(bucket_rev[...])
-    gather.finish()
-    normed = (units[...].astype(f32) * gain_attn[...]).astype(bf16)
-    pltpu.make_async_copy(wall.at[1 - core], wall.at[1 - core], s_recv).wait()
+    grads = Dispatch(g_send, g_landed, g_rows, g_sems)
+    far_row = lax.broadcasted_iota(jnp.int32, (SEQ, SEQ), 0)
+    far_col = lax.broadcasted_iota(jnp.int32, (SEQ, SEQ), 1)
+    mirror = (far_row + far_col == jnp.where(far_col == 0, 0, SEQ)).astype(bf16)
+    hot = dot(bucket_hot_rows(as_row(buckets[...])).astype(bf16), mirror)
+    pack = packer()
+    unit_ring.finish()
+    unit_rows = units[...].astype(f32)
+    normed = (unit_rows * gain_a).astype(bf16)
+
+    def pass_on(source):
+        return pltpu.make_async_remote_copy(
+            wall.at[core, source],
+            wall.at[core, source],
+            s_send,
+            s_recv,
+            device_id=(twin, z),
+            device_id_type=MESH,
+        )
+
+    pass_on(chip).start()
+
+    def forward(step, carry):
+        source = plane_source(e, step * 2) // 2
+        pltpu.make_async_copy(wall.at[core, source], wall.at[core, source], w_recv.at[source]).wait()
+        pass_on(source).start()
+        return carry
+
+    lax.fori_loop(1, 16, forward, 0)
+    drain(wall.at[0, pl.ds(0, 15)], w_send)
+    grads.cross(0)
+    grads.cross(1)
+    drain(wall.at[1 - core], s_recv)
     for block in range(PLANE):
-        whole32[24 * block : 24 * block + 24] = wall[block % 2, block // 2].astype(f32)[:24]
+        whole32[24 * block : 24 * block + 24] = wall[block % 2, block // 2].astype(f32)
     whole[...] = whole32[...].astype(bf16)
+
     projected = dot(normed, whole[:, :640]).astype(bf16)
-    qkv[...] = projected[:, : 3 * HEAD_WIDTH]
     queries = projected[:, :HEAD_WIDTH]
     keys = projected[:, HEAD_WIDTH : 2 * HEAD_WIDTH]
     values = projected[:, 2 * HEAD_WIDTH : 3 * HEAD_WIDTH]
-
-    pack = packer()
-    grads.turn(0, pack)
-    grads.turn(1, pack)
-
-    row = lax.broadcasted_iota(jnp.int32, (SEQ, SEQ), 0)
-    col = lax.broadcasted_iota(jnp.int32, (SEQ, SEQ), 1)
     mixed = jnp.zeros((SEQ, HEAD_WIDTH), f32)
     for h in range(LOCAL_HEADS):
         mask = head_mask(h)
-        rel = jnp.sum(bias[:, h : h + 1] * hot, axis=0, keepdims=True)
+        rel = jnp.sum(as_column(bias[h : h + 1]) * hot, axis=0, keepdims=True)
         shifted = pltpu.roll(jnp.broadcast_to(rel, (SEQ, SEQ)), 0, 1, stride=1, stride_axis=0)
         scores = dot_cols(jnp.where(mask, queries, jnp.zeros_like(queries)), keys) * score_scale
-        scores = jnp.where(col <= row, scores + shifted, masked_value)
+        scores = jnp.where(far_col <= far_row, scores + shifted, masked_value)
         raised = jnp.exp(scores - jnp.max(scores, axis=1, keepdims=True))
         weights_p = (raised / jnp.sum(raised, axis=1, keepdims=True)).astype(bf16)
         probs[h] = weights_p
         mixed = jnp.where(mask, dot(weights_p, values), mixed)
-        if h == 0:
-            grads.relay()
-    attended[...] = mixed.astype(bf16)
-    summing = RingSum(ring_sum[0], ring_sum[1], ring_sum[2], ring_sum[3:])
-    ring_sum[0][...] = dot_cols(attended[...], whole[:, 3 * HEAD_WIDTH :]).astype(bf16)
-    summing.start()
-    summing.add_far()
-    residual = inputs + summing.total()
+    attended = mixed.astype(bf16)
+    proj = whole[:, 3 * HEAD_WIDTH :]
+    sum_a[0][...] = dot_cols(attended, proj).astype(bf16)
+    attn_sum = RingSum(sum_a[0], sum_a[1], sum_a[2], sum_a[3:])
+    attn_sum.start()
+    attn_sum.add_far()
+    residual = inputs + attn_sum.total()
     resid[...] = residual
-    normed_m = (residual * rms_scale(residual) * gain_moe[...]).astype(bf16)
-    send_rows[...] = dot_rows(picks[0] + picks[1], normed_m).astype(bf16)
+    scale_m = rms_scale(residual)
+    normal_m = residual * scale_m
+    x_send[...] = dot_rows(picks[0] + picks[1], (normal_m * gain_m).astype(bf16)).astype(bf16)
+
+    out_way = Dispatch(x_send, x_landed, x_rows, x_sems)
+    home_way = Return(grad_part, back_x[0], back_x[1], back_x[2], back_x[3], back_x[4:])
+    out_way.cross(0)
+    grads.turn(0, pack)
+    grads.turn(1, pack)
+    out_way.crossed(0)
+    out_way.cross(1)
+    out_way.turn(0, pack)
+    out_way.turn(1, pack)
+    for load in loads:
+        load.wait()
+
+    def run(first, count):
+        for j in range(2):
+            span = pl.ds(first * 160, count * 160)
+            pre_act = dot(x_rows[j, span], held_in[j])
+            cdf = 0.5 * (1.0 + lax.erf(pre_act * inv_root_two))
+            hidden[j, span] = (pre_act * cdf).astype(bf16)
+            slope = cdf + pre_act * jnp.exp(-0.5 * pre_act * pre_act) * inv_root_tau
+            grad_hidden = dot_cols(g_rows[j, span], held_out[j])
+            grad_pre[j, span] = (grad_hidden * slope).astype(bf16)
+            grad_part[j, span] = dot_cols(grad_pre[j, span], held_in[j]).astype(bf16)
+
+    run(0, 1)
+    grads.relay()
+    out_way.relay()
+    run(1, 2)
+    home_way.near()
     grads.last()
-    gather.close()
-    grads.close()
-    summing.close()
-    sibling.wait_send()
-    drain(wall.at[0, pl.ds(0, 15)], w_send)
-
-
-def attend(*operands):
-    def shape(dims, kind=bf16):
-        return jax.ShapeDtypeStruct(dims, kind)
-
-    return pl.pallas_call(
-        attend_kernel,
-        out_shape=[
-            shape((128, WIDTH), f32),
-            shape((SEQ, WIDTH)),
-            shape((WIDTH, WIDTH)),
-            shape((SEQ, 3 * HEAD_WIDTH)),
-            shape((LOCAL_HEADS, SEQ, SEQ)),
-            shape((SEQ, HEAD_WIDTH)),
-            shape((TOPK, 128, PAD)),
-            shape((PAD, WIDTH)),
-            shape((2, EXPERT_ROWS, WIDTH)),
-        ],
-        in_specs=[VMEM] * 9,
-        out_specs=[VMEM] * 9,
-        scratch_shapes=[
-            pltpu.VMEM((2, 16, 32, WIDTH), bf16),
-            pltpu.VMEM((WIDTH, WIDTH), f32),
-            pltpu.VMEM((PAD, WIDTH), bf16),
-            pltpu.VMEM((PAD, WIDTH), bf16),
-            pltpu.SemaphoreType.DMA,
-            pltpu.SemaphoreType.DMA,
-            pltpu.SemaphoreType.DMA,
-            pltpu.SemaphoreType.DMA,
-        ]
-        + DISPATCH_SCRATCH
-        + GATHER_SCRATCH
-        + SUM_SCRATCH,
-        compiler_params=kernel_params(1),
-        name="attend",
-    )(*operands)
-
-
-def attend_back_kernel(
-    grad_resid, y_part, units, whole, qkv, probs, attended, tokens, resid, gates, picked,
-    gain_attn, gain_moe_part, bucket_rev,
-    out, grad_input, weight_grad, small,
-    seq_grad, blocks, near_blocks, plane_landed, small_own, small_landed,
-    s_send, s_recv, p_send, p_recv, t_send, t_recv, g0, g1, *rest,
-):
-    e, z, right, left = place()
-    core, chip = lax.rem(e, 2), e // 2
-    opposite = lax.rem(z + 2, RING)
-    ring_sum, back = rest[:5], rest[5:]
-    greet(1, 1, 1)
-    own_rows = pl.ds(pl.multiple_of(z * 128, 128), 128)
-    seq_grad[own_rows] = grad_resid[...].astype(bf16)
-    gather = RingGather(seq_grad, (g0, g1))
-    gather.start()
-    home_way = Return(y_part, back[0], back[1], back[2], back[3], back[4:])
-    hot = bucket_hot_rows(bucket_rev[...])
-    proj = whole[:, 3 * HEAD_WIDTH :]
-    queries = qkv[:, :HEAD_WIDTH]
-    keys = qkv[:, HEAD_WIDTH : 2 * HEAD_WIDTH]
-    values = qkv[:, 2 * HEAD_WIDTH :]
-    gather.finish()
+    out_way.last()
+    run(3, 1)
     home_way.far()
-    home_way.near()
+    saves = [
+        pltpu.make_async_copy(source, target, save_sems.at[index])
+        for index, (source, target) in enumerate(
+            (
+                (x_rows, rows_hbm),
+                (hidden, hidden_hbm),
+                (grad_pre, grad_pre_hbm),
+                (g_rows, grad_rows_hbm),
+            )
+        )
+    ]
+    for save in saves:
+        save.start()
+    for j in range(2):
+        y_part[j, 0:320] = dot(hidden[j, 0:320], held_out[j]).astype(bf16)
+    home_way.add_far()
+    for j in range(2):
+        y_part[j, 320:640] = dot(hidden[j, 320:640], held_out[j]).astype(bf16)
+    home_way.finish(0, pack)
+    home_way.finish(1, pack)
+    y_way = Return(y_part, back_y[0], back_y[1], back_y[2], back_y[3], back_y[4:])
+    y_way.far()
+    y_way.near()
+    y_way.add_far()
+    home_way.arrive()
+    grad_normed = dot(picked[0] + picked[1], home_way.home[...])
+    gain_m_part = jnp.sum(grad_normed * normal_m, axis=0, keepdims=True)
+    grad_unit_m = grad_normed * gain_m
+    grad_resid = grad_out + scale_m * (
+        grad_unit_m - normal_m * jnp.mean(grad_unit_m * normal_m, axis=1, keepdims=True)
+    )
+
+    seq_grad[own_rows] = grad_resid.astype(bf16)
+    grad_ring = RingGather(seq_grad, grad_sems)
+    grad_ring.start()
+    grad_ring.finish()
     grad_att = dot(seq_grad[...], proj).astype(bf16)
-    proj_part = dot_rows(seq_grad[...], attended[...])
+    proj_part = dot_rows(seq_grad[...], attended)
+    y_way.finish(0, pack)
+    y_way.finish(1, pack)
     zeros = jnp.zeros((SEQ, HEAD_WIDTH), f32)
     grad_q, grad_k, grad_v = zeros, zeros, zeros
     diagonals = []
@@ -755,33 +713,27 @@
         soft = weights_p.astype(f32)
         grad_w = dot_cols(jnp.where(mask, grad_att, jnp.zeros_like(grad_att)), values)
         row_dot = jnp.sum(soft * grad_w, axis=1, keepdims=True)
-        grad_s = soft * (grad_w - row_dot)
-        grad_scores = grad_s.astype(bf16)
+        grad_scores = (soft * (grad_w - row_dot)).astype(bf16)
         diagonals.append(sum_diagonals(grad_scores.astype(f32)))
         grad_q = jnp.where(mask, dot(grad_scores, keys), grad_q)
         grad_k = jnp.where(mask, dot_rows(grad_scores, queries), grad_k)
         grad_v = jnp.where(mask, dot_rows(weights_p, grad_att), grad_v)
-        if h == 0:
-            home_way.add_far()
     grad_qkv = jnp.concatenate(
         [grad_q * score_scale, grad_k * score_scale, grad_v], axis=1
     ).astype(bf16)
-    grad_normed = dot_cols(grad_qkv, whole[:, : 3 * HEAD_WIDTH])
-    summing = RingSum(ring_sum[0], ring_sum[1], ring_sum[2], ring_sum[3:])
-    ring_sum[0][...] = grad_normed.astype(bf16)
-    summing.start()
-    unit_rows = units[...].astype(f32)
-    gain_part = jnp.sum(grad_normed * unit_rows, axis=0, keepdims=True)
-    normed = (unit_rows * gain_attn[...]).astype(bf16)
-    qkv_part = dot_rows(normed, grad_qkv)
-    full = jnp.concatenate([qkv_part, proj_part], axis=1)
+    grad_normed_a = dot_cols(grad_qkv, whole[:, : 3 * HEAD_WIDTH])
+    sum_b[0][...] = grad_normed_a.astype(bf16)
+    input_sum = RingSum(sum_b[0], sum_b[1], sum_b[2], sum_b[3:])
+    input_sum.start()
+    gain_part = jnp.sum(grad_normed_a * unit_rows, axis=0, keepdims=True)
+    full = jnp.concatenate([dot_rows(normed, grad_qkv), proj_part], axis=1)
     diagonal = jnp.concatenate(diagonals + [jnp.zeros((5, SEQ), f32)], axis=0)
     table_rows = lax.dot_general(
         diagonal, hot, (((1,), (1,)), ((), ())), precision=highest, preferred_element_type=f32
     )
     table_wide = jnp.concatenate([table_rows[:LOCAL_HEADS], jnp.zeros((3, 32), f32)], axis=0)
     table_wide = jnp.concatenate([table_wide, jnp.zeros((6, WIDTH - 32), f32)], axis=1)
-    extra = jnp.concatenate([gain_part, gain_moe_part[...], table_wide], axis=0)
+    extra = jnp.concatenate([gain_part, gain_m_part, table_wide], axis=0)
     for block in range(PLANE):
         blocks[block % 2, block // 2] = jnp.concatenate(
             [full[24 * block : 24 * block + 24], extra], axis=0
@@ -789,39 +741,37 @@
     sibling = pltpu.make_async_remote_copy(
         blocks.at[1 - core],
         near_blocks,
-        s_send,
-        s_recv,
-        device_id=(chip * 2 + 1 - core, z),
+        v_send,
+        v_recv,
+        device_id=(twin, z),
         device_id_type=MESH,
     )
     sibling.start()
-    pack = packer()
-    home_way.finish(0, pack)
-    home_way.finish(1, pack)
+    input_sum.add_far()
     sibling.wait_recv()
     near_blocks[...] = (blocks[core].astype(f32) + near_blocks[...].astype(f32)).astype(bf16)
     plane_sends(
-        lambda other: near_blocks.at[other], lambda own: plane_landed.at[own], p_send, p_recv
+        lambda other: near_blocks.at[other],
+        lambda own: plane_landed.at[own],
+        p_send,
+        lambda own: p_recv,
     )
     plane_landed[chip] = near_blocks[chip]
-    summing.add_far()
-    inputs = tokens[...].astype(f32)
+    y_way.arrive()
+    home = y_way.home[...]
+    out[...] = (
+        resid[...] + gate_columns[0] * dot(picked[0], home) + gate_columns[1] * dot(picked[1], home)
+    ).astype(bf16)
     scale_first = rms_scale(inputs)
     normal_first = inputs * scale_first
-    grad_unit = summing.total() * gain_attn[...]
-    grad_input[...] = grad_resid[...] + scale_first * (
+    grad_unit = input_sum.total() * gain_a
+    grad_input[...] = grad_resid + scale_first * (
         grad_unit - normal_first * jnp.mean(grad_unit * normal_first, axis=1, keepdims=True)
     )
-    home_way.arrive()
-    home = home_way.home[...]
-    out[...] = (
-        resid[...] + gates[:, 0:1] * dot(picked[0], home) + gates[:, 1:2] * dot(picked[1], home)
-    ).astype(bf16)
     drain(plane_landed.at[pl.ds(0, 15)], p_recv)
     total = plane_landed[0].astype(f32)
     for block in range(1, 16):
         total = total + plane_landed[block].astype(f32)
-    weight_grad[...] = total[:24]
     small_own[...] = total[24:]
     shares = [
         pltpu.make_async_remote_copy(
@@ -836,54 +786,138 @@
     ]
     for share in shares:
         share.start()
+    for i in range(3):
+        qkv_grad[i] = total[:24, i * HEAD_WIDTH : (i + 1) * HEAD_WIDTH]
+    proj_grad[...] = total[:24, 3 * HEAD_WIDTH :]
+    column = lax.broadcasted_iota(jnp.int32, (8, WIDTH), 1)
+    table_own = jnp.sum(jnp.where(column == e, total[24:], 0.0), axis=1, keepdims=True)
+    table_out[...] = table_own[2 : 2 + LOCAL_HEADS]
     for share in shares:
         share.wait_recv()
     summed = small_own[...] + small_landed[0] + small_landed[1] + small_landed[2]
-    line = lax.broadcasted_iota(jnp.int32, (8, WIDTH), 0)
-    small[...] = jnp.where(line < 2, summed, small_own[...])
+    feature = lax.broadcasted_iota(jnp.int32, (WIDTH, 128), 0)
+    lane = lax.broadcasted_iota(jnp.int32, (WIDTH, 128), 1)
+    taken = (feature == (e * RING + z) * 6 + lane).astype(f32)
+    gains = jnp.dot(summed, taken, precision=highest, preferred_element_type=f32)
+    gain_first[...] = gains[0:1, :6]
+    gain_second[...] = gains[1:2, :6]
+
     for share in shares:
         share.wait_send()
-    gather.close()
+    for save in saves:
+        save.wait()
+    for way in (grads, out_way):
+        way.close()
+        way.crossed(1)
+    grads.crossed(0)
     home_way.close()
-    summing.close()
+    y_way.close()
+    unit_ring.close()
+    grad_ring.close()
+    attn_sum.close()
+    input_sum.close()
     sibling.wait_send()
+    drain(wall.at[0], s_send)
     drain(plane_landed.at[pl.ds(0, 15)], p_send)
 
 
-def attend_back(*operands):
+def run_layer(*operands):
     def shape(dims, kind=f32):
         return jax.ShapeDtypeStruct(dims, kind)
 
+    anywhere = pl.BlockSpec(memory_space=pl.ANY)
+    rows = (2, EXPERT_ROWS, WIDTH)
+    dma = pltpu.SemaphoreType.DMA
     return pl.pallas_call(
-        attend_back_kernel,
+        layer_kernel,
         out_shape=[
             shape((128, WIDTH), bf16),
             shape((128, WIDTH)),
-            shape((24, WIDTH)),
-            shape((8, WIDTH)),
-        ],
-        in_specs=[VMEM] * 14,
-        out_specs=[VMEM] * 4,
+            shape((3, 24, HEAD_WIDTH)),
+            shape((24, HEAD_WIDTH)),
+            shape((1, 6)),
+            shape((1, 6)),
+            shape((LOCAL_HEADS, 1)),
+        ]
+        + [shape(rows, bf16)] * 4,
+        in_specs=[VMEM] * 6 + [anywhere] * 2 + [VMEM] * 4,
+        out_specs=[VMEM] * 7 + [anywhere] * 4,
         scratch_shapes=[
+            pltpu.VMEM((SEQ, WIDTH), bf16),
+            pltpu.VMEM((WIDTH, WIDTH), bf16),
+            pltpu.VMEM((LOCAL_HEADS, SEQ, SEQ), bf16),
+            pltpu.VMEM((TOPK, 128, PAD), bf16),
+            pltpu.VMEM((128, WIDTH), f32),
+            pltpu.VMEM((24, WIDTH), bf16),
+            pltpu.VMEM((2, 16, 24, WIDTH), bf16),
+            pltpu.VMEM((WIDTH, WIDTH), f32),
+        ]
+        + [pltpu.VMEM((PAD, WIDTH), bf16), pltpu.VMEM((PAD, WIDTH), bf16), pltpu.VMEM(rows, bf16)] * 2
+        + [pltpu.VMEM((2, WIDTH, WIDTH), bf16)] * 2
+        + [pltpu.VMEM(rows, bf16)] * 4
+        + [
             pltpu.VMEM((SEQ, WIDTH), bf16),
             pltpu.VMEM((2, 16, 32, WIDTH), bf16),
             pltpu.VMEM((16, 32, WIDTH), bf16),
             pltpu.VMEM((16, 32, WIDTH), bf16),
             pltpu.VMEM((8, WIDTH), f32),
             pltpu.VMEM((3, 8, WIDTH), f32),
-            pltpu.SemaphoreType.DMA,
-            pltpu.SemaphoreType.DMA,
-            pltpu.SemaphoreType.DMA,
-            pltpu.SemaphoreType.DMA,
-            pltpu.SemaphoreType.DMA((3,)),
-            pltpu.SemaphoreType.DMA((3,)),
+            dma((2,)),
+            dma((4,)),
+            dma,
+            dma((16,)),
+            dma,
+            dma,
+            dma,
+            dma,
+            dma,
+            dma,
+            dma((3,)),
+            dma((3,)),
         ]
-        + GATHER_SCRATCH
-        + SUM_SCRATCH
-        + RETURN_SCRATCH,
-        compiler_params=kernel_params(2),
-        name="attend_back",
+        + DISPATCH_SCRATCH * 2
+        + GATHER_SCRATCH * 2
+        + SUM_SCRATCH * 2
+        + RETURN_SCRATCH * 2,
+        compiler_params=kernel_params(1),
+        name="layer",
     )(*operands)
+
+
+def expert_grad_kernel(rows, grad_pre, hidden, grad_rows, *refs):
+    grad_in, grad_out = refs[-2:]
+    passed = refs[:-2]
+    grad_in[0] = dot_rows(rows[0], grad_pre[0])
+    grad_out[0] = dot_rows(hidden[0], grad_rows[0])
+
+    @pl.when((pl.program_id(0) == 0) & (pl.program_id(1) == 0))
+    def _():
+        for source, target in zip(passed[: len(passed) // 2], passed[len(passed) // 2 :]):
+            target[...] = source[...]
+
+
+def expert_grads(rows, grad_pre, hidden, grad_rows, *small):
+    half = WIDTH // 2
+    whole_rows = pl.BlockSpec((1, EXPERT_ROWS, WIDTH), lambda j, n: (j, 0, 0))
+    half_rows = pl.BlockSpec((1, EXPERT_ROWS, half), lambda j, n: (j, 0, n))
+
+    def still(array):
+        return pl.BlockSpec(array.shape, lambda j, n, rank=array.ndim: (0,) * rank)
+
+    grads = jax.ShapeDtypeStruct((2, WIDTH, WIDTH), f32)
+    return pl.pallas_call(
+        expert_grad_kernel,
+        grid=(2, 2),
+        out_shape=[jax.ShapeDtypeStruct(a.shape, a.dtype) for a in small] + [grads, grads],
+        in_specs=[whole_rows, half_rows, half_rows, whole_rows] + [still(a) for a in small],
+        out_specs=[still(a) for a in small]
+        + [
+            pl.BlockSpec((1, WIDTH, half), lambda j, n: (j, 0, n)),
+            pl.BlockSpec((1, half, WIDTH), lambda j, n: (j, n, 0)),
+        ],
+        compiler_params=pltpu.CompilerParams(vmem_limit_bytes=48 * 1024 * 1024),
+        name="expert_grads",
+    )(rows, grad_pre, hidden, grad_rows, *small)
 
 
 def body(
@@ -900,38 +934,34 @@
     bucket_table,
     cotangent,
 ):
-    share = qkv_weight.shape[0]
-    weights = jnp.concatenate([qkv_weight.reshape(share, 3 * HEAD_WIDTH), proj_weight.T], axis=1)
-    weights = jnp.pad(weights, ((0, 8), (0, 0)))
-    gain_first, gain_second = gain_attn[None], gain_moe[None]
-    bucket_rev = jnp.concatenate([bucket_table[:1], bucket_table[:0:-1]])[None]
-    resid, units, whole, qkv, probs, attended, picked, send_rows, grad_rows = attend(
-        tokens, gain_first, gain_second, weights, cotangent, expert_ids, gate_values,
-        bias_table, bucket_rev,
-    )
-    received, hidden, grad_pre, y_part, grad_resid, gain_part = run_experts(
-        send_rows, grad_rows, expert_in, expert_out, picked, resid, cotangent, gain_second
-    )
-    out, grad_input, weight_grad, small = attend_back(
-        grad_resid, y_part, units, whole, qkv, probs, attended, tokens, resid, gate_values,
-        picked, gain_first, gain_part, bucket_rev,
-    )
-    expert_out_grad = jnp.einsum("jrf,jrd->jfd", hidden, grad_rows, preferred_element_type=f32)
-    expert_in_grad = jnp.einsum("jrd,jrf->jdf", received, grad_pre, preferred_element_type=f32)
-    e, z = lax.axis_index("expert"), lax.axis_index("mp")
-    piece = (e * RING + z) * 6
-    gains = lax.dynamic_slice_in_dim(small[:2], piece, 6, axis=1)
-    table_grad = lax.dynamic_slice_in_dim(small[2 : 2 + LOCAL_HEADS], e, 1, axis=1).T
+    results = run_layer(
+        tokens,
+        gain_attn.reshape(6, 128),
+        gain_moe.reshape(6, 128),
+        qkv_weight.transpose(1, 0, 2),
+        proj_weight.T,
+        bias_table.T,
+        expert_in,
+        expert_out,
+        expert_ids.T,
+        gate_values.T,
+        bucket_table.reshape(4, 128),
+        cotangent,
+    )
+    rows, hidden, grad_pre, grad_rows = results[7:]
+    out, grad_input, qkv_grad, proj_grad, gain_first, gain_second, table, grad_in, grad_out = (
+        expert_grads(rows, grad_pre, hidden, grad_rows, *results[:7])
+    )
     return (
         out,
         grad_input,
-        gains[0],
-        gains[1],
-        weight_grad[:, : 3 * HEAD_WIDTH].reshape(share, 3, HEAD_WIDTH),
-        weight_grad[:, 3 * HEAD_WIDTH :].T,
-        table_grad,
-        expert_in_grad,
-        expert_out_grad,
+        gain_first[0],
+        gain_second[0],
+        qkv_grad.transpose(1, 0, 2),
+        proj_grad.T,
+        table.T,
+        grad_in,
+        grad_out,
     )
 
 

time: 213 us -> 157 us (0.74)
  Pallas kernels: 182 us -> 147 us
  matrix products: 10.2 us -> 0 us
  local copies, waits for them, and re-layouts: 16.9 us -> 8.62 us
    pallas_call x3 -> x2, Pallas kernels: 182 us -> 147 us  [the longest x1 138 us: run_layer(): pl.pallas_call(layer_kernel, out_shape=[shape((128, WIDTH), bf16), shape(...]
    dot_general x2 -> x0, matrix products: 10.2 us -> none  [the longest x1 5.93 us: body(): jnp.einsum('jrd,jrf->jdf', received, grad_pre, preferred_element_type=f32)]
    slice x5 -> x0, local copies, waits for them, and re-layouts: 4.26 us -> none  [the longest x2 1.94 us: body(): bucket_rev = jnp.concatenate([bucket_table[:1], bucket_table[:0:-1]])[None]]
    concatenate x2 -> x0, other arithmetic: 2.65 us -> none  [the longest x1 1.4 us: body(): jnp.concatenate([qkv_weight.reshape(share, 3 * HEAD_WIDTH), proj_weight.T...]
    broadcast_in_dim x2 -> x0, local copies, waits for them, and re-layouts: 2.53 us -> none  [body(): gain_first, gain_second = (gain_attn[None], gain_moe[None])]
    unnamed x19 -> x18, local copies, waits for them, and re-layouts: 7.24 us -> 8.62 us
where the time goes in v3:
time: 157 us
  Pallas kernels  147 us (94%)
  local copies, waits for them, and re-layouts  8.62 us (5%)
    pallas_call x1, Pallas kernels, run_layer(): pl.pallas_call(layer_kernel, out_shape=[shape((128, WIDTH), bf16), shape(...  138 us
    pallas_call x1, Pallas kernels, expert_grads(): pl.pallas_call(expert_grad_kernel, grid=(2, 2), out_shape=[jax.ShapeDtype...  9.08 us
    unnamed x18, local copies, waits for them, and re-layouts  8.62 us

profile of v3, /device:TPU:0, one launch (start us, length us, event | category | flops | bytes accessed | tf_op | source)
XLA Modules:
  0.0 156.7 jit_solution(12187192431763428373)
XLA Ops:
  0.6 137.7 %layer.1 = (bf16[128,768]{1,0:T(8,128)(2,1)}, f32[128,768]{1,0:T(8,128)}, f32[3,24,192]{2,1,0:T(8,128)}, f32[24,192]{1,0:T(8,128)}, f32[1,6]{1,0:T(1,128)}, /*in...) custom-call(bf16[128,768]{1,0:T(8,128)(2,1)} %tokens.1, ...), custom_call_target="tpu_custom_call" | custom-call | tf_op jit(solution)/shard_map/layer/pallas_call | solution.py:831
  138.3 0.0 copy-start
  138.3 1.5 copy-done
  139.9 0.0 copy-start.1
  139.9 1.5 copy-done.1
  141.4 0.0 copy-start.2
  141.4 1.0 copy-done.2
  142.4 0.0 copy-start.3
  142.4 0.9 copy-done.3
  143.3 0.0 copy-start.4
  143.3 0.9 copy-done.4
  144.2 0.0 copy-start.5
  144.2 0.7 copy-done.5
  145.0 0.0 copy-start.6
  145.0 0.7 copy-done.6
  145.6 0.0 copy-start.7
  145.6 0.7 copy-done.7
  146.3 0.0 copy-start.8
  146.3 0.7 copy-done.8
  147.0 9.1 %expert_grads.1 = (bf16[128,768]{1,0:T(8,128)(2,1)}, f32[128,768]{1,0:T(8,128)}, f32[3,24,192]{2,1,0:T(8,128)}, f32[24,192]{1,0:T(8,128)}, f32[1,6]{1,0:T(1,128)...) custom-call(bf16[2,640,768]{2,1,0:T(8,128)(2,1)S(1)} %copy-done, ...), custom_call_target="tpu_custom_call" | custom-call | tf_op jit(solution)/shard_map/expert_grads/pallas_call | solution.py:908
  156.0 0.6 reduce
Async XLA Ops:
  138.3 1.5 copy-start
  139.9 1.5 copy-start.1
  141.4 1.0 copy-start.2
  142.4 0.9 copy-start.3
  143.3 0.9 copy-start.4
  144.2 0.7 copy-start.5
  145.0 0.7 copy-start.6
  145.6 0.7 copy-start.7
  146.3 0.7 copy-start.8

commit v4 on v3

--- a/solution.py
+++ b/solution.py
@@ -69,7 +69,7 @@
     if across:
         other = lax.rem(z + 2, RING)
         pl.semaphore_signal(barrier, inc=1, device_id=(e, other), device_id_type=MESH)
-    pl.semaphore_wait(barrier, (PLANE - 1) * plane + 2 * ring + across)
+    return (PLANE - 1) * plane + 2 * ring + across
 
 
 def drain(ref, sem):
@@ -105,6 +105,9 @@
 
     def part(self, slot, half):
         return self.rows.at[:, pl.ds(slot * 160 + half * HALF, HALF)]
+
+    def one(self, expert, slot, half):
+        return self.rows.at[expert, pl.ds(slot * 160 + half * HALF, HALF)]
 
     def cross(self, half):
         e, z, right, left = place()
@@ -147,8 +150,10 @@
             self.copy(1, part(0, 1), part(2, 1), right),
             self.copy(2, part(0, 0), part(1, 0), left),
             self.copy(3, part(0, 1), part(1, 1), left),
-            self.copy(4, part(2, 0), part(3, 0), right),
-            self.copy(5, part(1, 1), part(3, 1), left),
+            self.copy(4, self.one(0, 2, 0), self.one(0, 3, 0), right),
+            self.copy(5, self.one(1, 1, 0), self.one(1, 3, 0), left),
+            self.copy(6, self.one(0, 2, 1), self.one(0, 3, 1), right),
+            self.copy(7, self.one(1, 1, 1), self.one(1, 3, 1), left),
         ]
 
     def turn(self, half, pack):
@@ -164,17 +169,14 @@
 
     def relay(self):
         ring = self.copies()
-        ring[0].wait_recv()
-        ring[4].start()
-        ring[3].wait_recv()
-        ring[5].start()
-        ring[1].wait_recv()
-        ring[2].wait_recv()
+        for near, far in ((0, 4), (2, 5), (1, 6), (3, 7)):
+            ring[near].wait_recv()
+            ring[far].start()
 
     def last(self):
         ring = self.copies()
-        ring[4].wait_recv()
-        ring[5].wait_recv()
+        for far in range(4, 8):
+            ring[far].wait_recv()
 
     def close(self):
         for copy in self.copies():
@@ -184,8 +186,8 @@
 DISPATCH_SCRATCH = [
     pltpu.SemaphoreType.DMA((2,)),
     pltpu.SemaphoreType.DMA((2,)),
-    pltpu.SemaphoreType.DMA((6,)),
-    pltpu.SemaphoreType.DMA((6,)),
+    pltpu.SemaphoreType.DMA((8,)),
+    pltpu.SemaphoreType.DMA((8,)),
 ]
 
 
@@ -195,13 +197,14 @@
         self.spread, self.home = spread, home
         self.ring_out, self.ring_in, self.plane_out, self.plane_in = sems
 
-    def part(self, slot, half):
-        return self.partial.at[:, pl.ds(slot * 160 + half * HALF, HALF)]
-
-    def copies(self):
+    def one(self, expert, slot, half):
+        return self.partial.at[expert, pl.ds(slot * 160 + half * HALF, HALF)]
+
+    def copies(self, half):
         e, z, right, left = place()
 
         def copy(index, source, other):
+            index = half * 6 + index
             return pltpu.make_async_remote_copy(
                 source,
                 self.landed.at[index],
@@ -211,46 +214,48 @@
                 device_id_type=MESH,
             )
 
-        part = self.part
+        one = self.one
         return [
-            copy(0, part(3, 0), right),
-            copy(1, part(3, 1), left),
-            copy(2, part(1, 1), right),
-            copy(3, part(2, 0), left),
-            copy(4, self.relayed.at[0], right),
-            copy(5, self.relayed.at[1], left),
+            copy(0, one(0, 3, half), right),
+            copy(1, one(1, 3, half), left),
+            copy(2, one(1, 1, half), right),
+            copy(3, one(0, 2, half), left),
+            copy(4, self.relayed.at[half, 0], right),
+            copy(5, self.relayed.at[half, 1], left),
         ]
 
-    def near(self):
-        ring = self.copies()
+    def near(self, half):
+        ring = self.copies(half)
         ring[2].start()
         ring[3].start()
 
-    def far(self):
-        ring = self.copies()
-        ring[0].start()
-        ring[1].start()
-
-    def add_far(self):
-        ring = self.copies()
-        for index, slot, half in ((0, 1, 0), (1, 2, 1)):
+    def far(self, half, index):
+        self.copies(half)[index].start()
+
+    def add_far(self, half):
+        ring = self.copies(half)
+        for index, expert, slot in ((0, 0, 1), (1, 1, 2)):
             ring[index].wait_recv()
-            self.relayed[index] = (
-                self.part(slot, half)[...].astype(f32) + self.landed[index].astype(f32)
+            self.relayed[half, index] = (
+                self.one(expert, slot, half)[...].astype(f32)
+                + self.landed[half * 6 + index].astype(f32)
             ).astype(bf16)
             ring[4 + index].start()
 
     def finish(self, half, pack):
         e, z, right, left = place()
-        ring = self.copies()
-        direct, summed = (3, 4) if half == 0 else (2, 5)
-        ring[direct].wait_recv()
-        ring[summed].wait_recv()
-        total = (
-            self.part(0, half)[...].astype(f32)
-            + self.landed[direct].astype(f32)
-            + self.landed[summed].astype(f32)
-        ).astype(bf16)
+        ring = self.copies(half)
+        total = []
+        for expert, direct, summed in ((0, 3, 4), (1, 2, 5)):
+            ring[direct].wait_recv()
+            ring[summed].wait_recv()
+            total.append(
+                (
+                    self.one(expert, 0, half)[...].astype(f32)
+                    + self.landed[half * 6 + direct].astype(f32)
+                    + self.landed[half * 6 + summed].astype(f32)
+                ).astype(bf16)
+            )
         flat = jnp.concatenate([total[0], total[1]], axis=0)
         self.spread[256 * half : 256 * half + 256] = dot_rows(pack, flat).astype(bf16)
 
@@ -273,18 +278,18 @@
         drain(self.home.at[pl.ds(0, (PLANE - 1) * BLOCK)], self.plane_in)
 
     def close(self):
-        for copy in self.copies():
+        for copy in self.copies(0) + self.copies(1):
             copy.wait_send()
         drain(self.spread.at[pl.ds(0, (PLANE - 1) * BLOCK)], self.plane_out)
 
 
 RETURN_SCRATCH = [
     pltpu.VMEM((2, 2, HALF, 768), bf16),
-    pltpu.VMEM((6, 2, HALF, 768), bf16),
+    pltpu.VMEM((12, HALF, 768), bf16),
     pltpu.VMEM((PAD, 768), bf16),
     pltpu.VMEM((PAD, 768), bf16),
-    pltpu.SemaphoreType.DMA((6,)),
-    pltpu.SemaphoreType.DMA((6,)),
+    pltpu.SemaphoreType.DMA((12,)),
+    pltpu.SemaphoreType.DMA((12,)),
     pltpu.SemaphoreType.DMA,
     pltpu.SemaphoreType.DMA,
 ]
@@ -354,14 +359,21 @@
         for index in (0, 3, 1, 2):
             sends[index].start()
 
-    def finish(self):
+    def relay(self):
         sends, lands = self.copies()
         lands[0].wait()
         sends[4].start()
         lands[3].wait()
         sends[5].start()
+
+    def land(self, index):
+        sends, lands = self.copies()
+        lands[index].wait()
+
+    def finish(self):
+        self.relay()
         for index in (1, 2, 4, 5):
-            lands[index].wait()
+            self.land(index)
 
     def close(self):
         sends, lands = self.copies()
@@ -405,10 +417,8 @@
             copy(5, self.relayed.at[1], left),
         ]
 
-    def start(self):
-        ring = self.copies()
-        for index in range(4):
-            ring[index].start()
+    def send(self, index):
+        self.copies()[index].start()
 
     def add_far(self):
         ring = self.copies()
@@ -447,7 +457,7 @@
 
 
 def head_mask(h):
-    lane = lax.broadcasted_iota(jnp.int32, (SEQ, HEAD_WIDTH), 1)
+    lane = lax.broadcasted_iota(jnp.int32, (1, HEAD_WIDTH), 1)
     return (lane >= h * HEAD_DIM) & (lane < (h + 1) * HEAD_DIM)
 
 
@@ -520,13 +530,13 @@
     tokens, gain_attn, gain_moe, qkv_weight, proj_weight, bias, weight_in, weight_out,
     ids, gates, buckets, cotangent,
     out, grad_input, qkv_grad, proj_grad, gain_first, gain_second, table_out,
-    rows_hbm, hidden_hbm, grad_pre_hbm, grad_rows_hbm,
-    units, whole, probs, picked, resid, mine, wall, whole32,
+    grads_hbm,
+    units, whole, qkv, attended, probs, picked, resid, mine, wall, whole32,
     x_send, x_landed, x_rows, g_send, g_landed, g_rows,
-    held_in, held_out, hidden, grad_pre, grad_part, y_part,
-    seq_grad, blocks, near_blocks, plane_landed, small_own, small_landed,
+    held_in, held_out, hidden, grad_pre, grad_part, y_part, expert_grads,
+    seq_grad, grad_qkv, blocks, near_blocks, plane_landed, small_own, small_landed, small_sum, small_plane,
     load_sems, save_sems, w_send, w_recv, s_send, s_recv, v_send, v_recv,
-    p_send, p_recv, t_send, t_recv, *rest,
+    p_send, p_recv, t_send, t_recv, q_send, q_recv, *rest,
 ):
     x_sems, g_sems, rest = rest[:4], rest[4:8], rest[8:]
     unit_sems, grad_sems, rest = rest[:2], rest[2:4], rest[4:]
@@ -542,19 +552,31 @@
     ]
     for load in loads:
         load.start()
-    greet(1, 1, 1)
+    arrivals = greet(1, 1, 1)
 
     mine[...] = jnp.concatenate(
         [qkv_weight[i].astype(f32) for i in range(3)] + [proj_weight[...].astype(f32)], axis=1
     ).astype(bf16)
-    plane_sends(lambda other: mine, lambda own: wall.at[core, own], w_send, w_recv.at.__getitem__)
     inputs = tokens[...].astype(f32)
     own_rows = pl.ds(pl.multiple_of(z * 128, 128), 128)
     units[own_rows] = (inputs * rms_scale(inputs)).astype(bf16)
+    pl.semaphore_wait(pltpu.get_barrier_semaphore(), arrivals)
+    plane_sends(lambda other: mine, lambda own: wall.at[core, own], w_send, w_recv.at.__getitem__)
     unit_ring = RingGather(units, unit_sems)
     unit_ring.start()
     wall[core, chip] = mine[...]
 
+    def pass_on(source):
+        return pltpu.make_async_remote_copy(
+            wall.at[core, source],
+            wall.at[core, source],
+            s_send,
+            s_recv,
+            device_id=(twin, z),
+            device_id_type=MESH,
+        )
+
+    pass_on(chip).start()
     gain_a, gain_m = as_row(gain_attn[...]), as_row(gain_moe[...])
     id_columns = jnp.concatenate(
         [as_column(ids[c : c + 1].astype(f32)) for c in range(TOPK)], axis=1
@@ -569,26 +591,16 @@
         + dot_rows(picks[1], (gate_columns[1] * grad_out).astype(bf16))
     ).astype(bf16)
     grads = Dispatch(g_send, g_landed, g_rows, g_sems)
+    unit_ring.relay()
     far_row = lax.broadcasted_iota(jnp.int32, (SEQ, SEQ), 0)
     far_col = lax.broadcasted_iota(jnp.int32, (SEQ, SEQ), 1)
     mirror = (far_row + far_col == jnp.where(far_col == 0, 0, SEQ)).astype(bf16)
     hot = dot(bucket_hot_rows(as_row(buckets[...])).astype(bf16), mirror)
+    rels = [
+        jnp.sum(as_column(bias[h : h + 1]) * hot, axis=0, keepdims=True)
+        for h in range(LOCAL_HEADS)
+    ]
     pack = packer()
-    unit_ring.finish()
-    unit_rows = units[...].astype(f32)
-    normed = (unit_rows * gain_a).astype(bf16)
-
-    def pass_on(source):
-        return pltpu.make_async_remote_copy(
-            wall.at[core, source],
-            wall.at[core, source],
-            s_send,
-            s_recv,
-            device_id=(twin, z),
-            device_id_type=MESH,
-        )
-
-    pass_on(chip).start()
 
     def forward(step, carry):
         source = plane_source(e, step * 2) // 2
@@ -597,35 +609,62 @@
         return carry
 
     lax.fori_loop(1, 16, forward, 0)
+    for index in (1, 2, 4, 5):
+        unit_ring.land(index)
     drain(wall.at[0, pl.ds(0, 15)], w_send)
     grads.cross(0)
     grads.cross(1)
+    unit_rows = units[...].astype(f32)
+    normed = (unit_rows * gain_a).astype(bf16)
     drain(wall.at[1 - core], s_recv)
     for block in range(PLANE):
         whole32[24 * block : 24 * block + 24] = wall[block % 2, block // 2].astype(f32)
     whole[...] = whole32[...].astype(bf16)
 
-    projected = dot(normed, whole[:, :640]).astype(bf16)
-    queries = projected[:, :HEAD_WIDTH]
-    keys = projected[:, HEAD_WIDTH : 2 * HEAD_WIDTH]
-    values = projected[:, 2 * HEAD_WIDTH : 3 * HEAD_WIDTH]
-    mixed = jnp.zeros((SEQ, HEAD_WIDTH), f32)
-    for h in range(LOCAL_HEADS):
-        mask = head_mask(h)
-        rel = jnp.sum(as_column(bias[h : h + 1]) * hot, axis=0, keepdims=True)
-        shifted = pltpu.roll(jnp.broadcast_to(rel, (SEQ, SEQ)), 0, 1, stride=1, stride_axis=0)
-        scores = dot_cols(jnp.where(mask, queries, jnp.zeros_like(queries)), keys) * score_scale
-        scores = jnp.where(far_col <= far_row, scores + shifted, masked_value)
-        raised = jnp.exp(scores - jnp.max(scores, axis=1, keepdims=True))
-        weights_p = (raised / jnp.sum(raised, axis=1, keepdims=True)).astype(bf16)
-        probs[h] = weights_p
-        mixed = jnp.where(mask, dot(weights_p, values), mixed)
-    attended = mixed.astype(bf16)
+    qkv[...] = dot(normed, whole[:, :640]).astype(bf16)[:, : 3 * HEAD_WIDTH]
+    keys = qkv[:, HEAD_WIDTH : 2 * HEAD_WIDTH]
+    values = qkv[:, 2 * HEAD_WIDTH :]
     proj = whole[:, 3 * HEAD_WIDTH :]
-    sum_a[0][...] = dot_cols(attended, proj).astype(bf16)
     attn_sum = RingSum(sum_a[0], sum_a[1], sum_a[2], sum_a[3:])
-    attn_sum.start()
+    owners = (z, right, left, opposite)
+    query_row = lax.broadcasted_iota(jnp.int32, (128, SEQ), 0)
+    key_col = lax.broadcasted_iota(jnp.int32, (128, SEQ), 1)
+
+    def rows_of(slot):
+        return pl.ds(pl.multiple_of(owners[slot] * 128, 128), 128)
+
+    def attend(slot):
+        rows = rows_of(slot)
+        first = owners[slot] * 128
+        queries = qkv[rows, :HEAD_WIDTH]
+        mixed = jnp.zeros((128, HEAD_WIDTH), f32)
+        for h in range(LOCAL_HEADS):
+            mask = head_mask(h)
+            turned = pltpu.roll(rels[h], first, 1)
+            shifted = pltpu.roll(
+                jnp.broadcast_to(turned, (128, SEQ)), 0, 1, stride=1, stride_axis=0
+            )
+            scores = dot_cols(jnp.where(mask, queries, jnp.zeros_like(queries)), keys) * score_scale
+            scores = jnp.where(key_col <= query_row + first, scores + shifted, masked_value)
+            raised = jnp.exp(scores - jnp.max(scores, axis=1, keepdims=True))
+            weights_p = (raised / jnp.sum(raised, axis=1, keepdims=True)).astype(bf16)
+            probs[h, rows] = weights_p
+            mixed = jnp.where(mask, dot(weights_p, values), mixed)
+        mixed = mixed.astype(bf16)
+        attended[rows] = mixed
+        sum_a[0][rows] = dot_cols(mixed, proj).astype(bf16)
+
+    attend(3)
+    attn_sum.send(0)
+    attn_sum.send(1)
+    attend(1)
+    attn_sum.send(2)
+    attend(2)
+    attn_sum.send(3)
+    attend(0)
     attn_sum.add_far()
+    grads.turn(0, pack)
+    grads.turn(1, pack)
     residual = inputs + attn_sum.total()
     resid[...] = residual
     scale_m = rms_scale(residual)
@@ -635,8 +674,6 @@
     out_way = Dispatch(x_send, x_landed, x_rows, x_sems)
     home_way = Return(grad_part, back_x[0], back_x[1], back_x[2], back_x[3], back_x[4:])
     out_way.cross(0)
-    grads.turn(0, pack)
-    grads.turn(1, pack)
     out_way.crossed(0)
     out_way.cross(1)
     out_way.turn(0, pack)
@@ -644,8 +681,8 @@
     for load in loads:
         load.wait()
 
-    def run(first, count):
-        for j in range(2):
+    def run(first, count, experts=(0, 1)):
+        for j in experts:
             span = pl.ds(first * 160, count * 160)
             pre_act = dot(x_rows[j, span], held_in[j])
             cdf = 0.5 * (1.0 + lax.erf(pre_act * inv_root_two))
@@ -659,35 +696,35 @@
     grads.relay()
     out_way.relay()
     run(1, 2)
-    home_way.near()
+    home_way.near(0)
+    home_way.near(1)
     grads.last()
     out_way.last()
-    run(3, 1)
-    home_way.far()
-    saves = [
-        pltpu.make_async_copy(source, target, save_sems.at[index])
-        for index, (source, target) in enumerate(
-            (
-                (x_rows, rows_hbm),
-                (hidden, hidden_hbm),
-                (grad_pre, grad_pre_hbm),
-                (g_rows, grad_rows_hbm),
-            )
-        )
-    ]
-    for save in saves:
-        save.start()
     for j in range(2):
-        y_part[j, 0:320] = dot(hidden[j, 0:320], held_out[j]).astype(bf16)
-    home_way.add_far()
+        run(3, 1, (j,))
+        home_way.far(0, j)
+        home_way.far(1, j)
+    y_way = Return(y_part, back_y[0], back_y[1], back_y[2], back_y[3], back_y[4:])
     for j in range(2):
-        y_part[j, 320:640] = dot(hidden[j, 320:640], held_out[j]).astype(bf16)
+        y_part[j] = dot(hidden[j], held_out[j]).astype(bf16)
+    home_way.add_far(0)
+    home_way.add_far(1)
+    for half in range(2):
+        y_way.far(half, 0)
+        y_way.far(half, 1)
+        y_way.near(half)
     home_way.finish(0, pack)
     home_way.finish(1, pack)
-    y_way = Return(y_part, back_y[0], back_y[1], back_y[2], back_y[3], back_y[4:])
-    y_way.far()
-    y_way.near()
-    y_way.add_far()
+    saves = []
+    for j in range(2):
+        expert_grads[j] = dot_rows(x_rows[j], grad_pre[j]).astype(bf16)
+        expert_grads[2 + j] = dot_rows(hidden[j], g_rows[j]).astype(bf16)
+        y_way.add_far(j)
+    for index in range(4):
+        saves.append(
+            pltpu.make_async_copy(expert_grads.at[index], grads_hbm.at[index], save_sems.at[index])
+        )
+        saves[index].start()
     home_way.arrive()
     grad_normed = dot(picked[0] + picked[1], home_way.home[...])
     gain_m_part = jnp.sum(grad_normed * normal_m, axis=0, keepdims=True)
@@ -699,45 +736,53 @@
     seq_grad[own_rows] = grad_resid.astype(bf16)
     grad_ring = RingGather(seq_grad, grad_sems)
     grad_ring.start()
-    grad_ring.finish()
-    grad_att = dot(seq_grad[...], proj).astype(bf16)
-    proj_part = dot_rows(seq_grad[...], attended)
+    zeros = jnp.zeros((SEQ, HEAD_WIDTH), f32)
+    carried = [zeros, zeros, jnp.zeros((WIDTH, HEAD_WIDTH), f32)]
+    diagonals = [jnp.zeros((1, SEQ), f32)] * LOCAL_HEADS
+
+    def attend_back(slot):
+        rows = rows_of(slot)
+        queries = qkv[rows, :HEAD_WIDTH]
+        grad_rows = seq_grad[rows]
+        grad_att = dot(grad_rows, proj).astype(bf16)
+        carried[2] = carried[2] + dot_rows(grad_rows, attended[rows])
+        grad_q = jnp.zeros((128, HEAD_WIDTH), f32)
+        for h in range(LOCAL_HEADS):
+            mask = head_mask(h)
+            weights_p = probs[h, rows]
+            soft = weights_p.astype(f32)
+            own_att = jnp.where(mask, grad_att, jnp.zeros_like(grad_att))
+            own_queries = jnp.where(mask, queries, jnp.zeros_like(queries))
+            grad_w = dot_cols(own_att, values)
+            row_dot = jnp.sum(soft * grad_w, axis=1, keepdims=True)
+            grad_scores = (soft * (grad_w - row_dot)).astype(bf16)
+            turn = lax.rem(SEQ - owners[slot] * 128, SEQ)
+            diagonals[h] = diagonals[h] + pltpu.roll(
+                sum_diagonals(grad_scores.astype(f32)), turn, 1
+            )
+            grad_q = jnp.where(mask, dot(grad_scores, keys), grad_q)
+            carried[0] = carried[0] + dot_rows(grad_scores, own_queries)
+            carried[1] = carried[1] + dot_rows(weights_p, own_att)
+        grad_qkv[rows, :HEAD_WIDTH] = (grad_q * score_scale).astype(bf16)
+
+    attend_back(0)
+    grad_ring.relay()
+    grad_ring.land(2)
+    attend_back(1)
     y_way.finish(0, pack)
+    grad_ring.land(1)
+    attend_back(2)
     y_way.finish(1, pack)
-    zeros = jnp.zeros((SEQ, HEAD_WIDTH), f32)
-    grad_q, grad_k, grad_v = zeros, zeros, zeros
-    diagonals = []
-    for h in range(LOCAL_HEADS):
-        mask = head_mask(h)
-        weights_p = probs[h]
-        soft = weights_p.astype(f32)
-        grad_w = dot_cols(jnp.where(mask, grad_att, jnp.zeros_like(grad_att)), values)
-        row_dot = jnp.sum(soft * grad_w, axis=1, keepdims=True)
-        grad_scores = (soft * (grad_w - row_dot)).astype(bf16)
-        diagonals.append(sum_diagonals(grad_scores.astype(f32)))
-        grad_q = jnp.where(mask, dot(grad_scores, keys), grad_q)
-        grad_k = jnp.where(mask, dot_rows(grad_scores, queries), grad_k)
-        grad_v = jnp.where(mask, dot_rows(weights_p, grad_att), grad_v)
-    grad_qkv = jnp.concatenate(
-        [grad_q * score_scale, grad_k * score_scale, grad_v], axis=1
+    grad_ring.land(4)
+    grad_ring.land(5)
+    attend_back(3)
+    grad_qkv[:, HEAD_WIDTH:] = jnp.concatenate(
+        [carried[0] * score_scale, carried[1]], axis=1
     ).astype(bf16)
-    grad_normed_a = dot_cols(grad_qkv, whole[:, : 3 * HEAD_WIDTH])
-    sum_b[0][...] = grad_normed_a.astype(bf16)
-    input_sum = RingSum(sum_b[0], sum_b[1], sum_b[2], sum_b[3:])
-    input_sum.start()
-    gain_part = jnp.sum(grad_normed_a * unit_rows, axis=0, keepdims=True)
-    full = jnp.concatenate([dot_rows(normed, grad_qkv), proj_part], axis=1)
-    diagonal = jnp.concatenate(diagonals + [jnp.zeros((5, SEQ), f32)], axis=0)
-    table_rows = lax.dot_general(
-        diagonal, hot, (((1,), (1,)), ((), ())), precision=highest, preferred_element_type=f32
-    )
-    table_wide = jnp.concatenate([table_rows[:LOCAL_HEADS], jnp.zeros((3, 32), f32)], axis=0)
-    table_wide = jnp.concatenate([table_wide, jnp.zeros((6, WIDTH - 32), f32)], axis=1)
-    extra = jnp.concatenate([gain_part, gain_m_part, table_wide], axis=0)
+    proj_part = carried[2]
+    full = jnp.concatenate([dot_rows(normed, grad_qkv[...]), proj_part], axis=1)
     for block in range(PLANE):
-        blocks[block % 2, block // 2] = jnp.concatenate(
-            [full[24 * block : 24 * block + 24], extra], axis=0
-        ).astype(bf16)
+        blocks[block % 2, block // 2] = full[24 * block : 24 * block + 24].astype(bf16)
     sibling = pltpu.make_async_remote_copy(
         blocks.at[1 - core],
         near_blocks,
@@ -747,32 +792,23 @@
         device_id_type=MESH,
     )
     sibling.start()
-    input_sum.add_far()
-    sibling.wait_recv()
-    near_blocks[...] = (blocks[core].astype(f32) + near_blocks[...].astype(f32)).astype(bf16)
-    plane_sends(
-        lambda other: near_blocks.at[other],
-        lambda own: plane_landed.at[own],
-        p_send,
-        lambda own: p_recv,
-    )
-    plane_landed[chip] = near_blocks[chip]
-    y_way.arrive()
-    home = y_way.home[...]
-    out[...] = (
-        resid[...] + gate_columns[0] * dot(picked[0], home) + gate_columns[1] * dot(picked[1], home)
-    ).astype(bf16)
-    scale_first = rms_scale(inputs)
-    normal_first = inputs * scale_first
-    grad_unit = input_sum.total() * gain_a
-    grad_input[...] = grad_resid + scale_first * (
-        grad_unit - normal_first * jnp.mean(grad_unit * normal_first, axis=1, keepdims=True)
-    )
-    drain(plane_landed.at[pl.ds(0, 15)], p_recv)
-    total = plane_landed[0].astype(f32)
-    for block in range(1, 16):
-        total = total + plane_landed[block].astype(f32)
-    small_own[...] = total[24:]
+    grad_normed_a = dot_cols(grad_qkv[...], whole[:, : 3 * HEAD_WIDTH])
+    sum_b[0][...] = grad_normed_a.astype(bf16)
+    input_sum = RingSum(sum_b[0], sum_b[1], sum_b[2], sum_b[3:])
+    for index in range(4):
+        input_sum.send(index)
+    gain_part = jnp.sum(grad_normed_a * unit_rows, axis=0, keepdims=True)
+    diagonal = jnp.concatenate(diagonals + [jnp.zeros((5, SEQ), f32)], axis=0)
+    table_rows = lax.dot_general(
+        diagonal, hot, (((1,), (1,)), ((), ())), precision=highest, preferred_element_type=f32
+    )
+    pieces = [
+        part[:, 128 * i : 128 * i + 128] for part in (gain_part, gain_m_part) for i in range(6)
+    ]
+    small_own[...] = jnp.concatenate(
+        pieces + [jnp.zeros((4, 128), f32)], axis=0
+    )
+    small_own[12 : 12 + LOCAL_HEADS, :32] = table_rows[:LOCAL_HEADS]
     shares = [
         pltpu.make_async_remote_copy(
             small_own,
@@ -786,22 +822,72 @@
     ]
     for share in shares:
         share.start()
-    for i in range(3):
-        qkv_grad[i] = total[:24, i * HEAD_WIDTH : (i + 1) * HEAD_WIDTH]
-    proj_grad[...] = total[:24, 3 * HEAD_WIDTH :]
-    column = lax.broadcasted_iota(jnp.int32, (8, WIDTH), 1)
-    table_own = jnp.sum(jnp.where(column == e, total[24:], 0.0), axis=1, keepdims=True)
-    table_out[...] = table_own[2 : 2 + LOCAL_HEADS]
+    input_sum.add_far()
+    sibling.wait_recv()
+    near_blocks[...] = (blocks[core].astype(f32) + near_blocks[...].astype(f32)).astype(bf16)
+    plane_sends(
+        lambda other: near_blocks.at[other],
+        lambda own: plane_landed.at[own],
+        p_send,
+        lambda own: p_recv,
+    )
+    plane_landed[chip] = near_blocks[chip]
     for share in shares:
         share.wait_recv()
-    summed = small_own[...] + small_landed[0] + small_landed[1] + small_landed[2]
+    own_small = small_own[...]
+    line = lax.broadcasted_iota(jnp.int32, (16, 128), 0)
+    small_sum[...] = jnp.where(
+        line < 12, own_small + small_landed[0] + small_landed[1] + small_landed[2], own_small
+    )
+
+    def spread_small(d, carry):
+        pltpu.make_async_remote_copy(
+            small_sum,
+            small_plane.at[d],
+            q_send,
+            q_recv,
+            device_id=(plane_target(e, d), z),
+            device_id_type=MESH,
+        ).start()
+        return carry
+
+    lax.fori_loop(1, PLANE, spread_small, 0)
+    small_plane[0] = small_sum[...]
+    y_way.arrive()
+    home = y_way.home[...]
+    out[...] = (
+        resid[...] + gate_columns[0] * dot(picked[0], home) + gate_columns[1] * dot(picked[1], home)
+    ).astype(bf16)
+    scale_first = rms_scale(inputs)
+    normal_first = inputs * scale_first
+    grad_unit = input_sum.total() * gain_a
+    grad_input[...] = grad_resid + scale_first * (
+        grad_unit - normal_first * jnp.mean(grad_unit * normal_first, axis=1, keepdims=True)
+    )
+    drain(plane_landed.at[pl.ds(0, 15)], p_recv)
+    total = plane_landed[0].astype(f32)
+    for block in range(1, 16):
+        total = total + plane_landed[block].astype(f32)
+    for i in range(3):
+        qkv_grad[i] = total[:, i * HEAD_WIDTH : (i + 1) * HEAD_WIDTH]
+    proj_grad[...] = total[:, 3 * HEAD_WIDTH :]
+    drain(small_plane.at[pl.ds(1, PLANE - 1)], q_recv)
+    summed = jnp.sum(small_plane[...], axis=0)
+    column = lax.broadcasted_iota(jnp.int32, (16, 128), 1)
+    table_own = jnp.sum(jnp.where(column == e, summed, 0.0), axis=1, keepdims=True)
+    table_out[...] = jnp.concatenate(
+        [table_own[12 + h : 13 + h] for h in range(LOCAL_HEADS)], axis=1
+    )
+    wide = jnp.concatenate([as_row(summed[0:6]), as_row(summed[6:12])], axis=0)
+    wide = jnp.concatenate([wide, jnp.zeros((6, WIDTH), f32)], axis=0)
     feature = lax.broadcasted_iota(jnp.int32, (WIDTH, 128), 0)
     lane = lax.broadcasted_iota(jnp.int32, (WIDTH, 128), 1)
     taken = (feature == (e * RING + z) * 6 + lane).astype(f32)
-    gains = jnp.dot(summed, taken, precision=highest, preferred_element_type=f32)
+    gains = jnp.dot(wide, taken, precision=highest, preferred_element_type=f32)
     gain_first[...] = gains[0:1, :6]
     gain_second[...] = gains[1:2, :6]
 
+    drain(small_plane.at[pl.ds(1, PLANE - 1)], q_send)
     for share in shares:
         share.wait_send()
     for save in saves:
@@ -837,14 +923,16 @@
             shape((24, HEAD_WIDTH)),
             shape((1, 6)),
             shape((1, 6)),
-            shape((LOCAL_HEADS, 1)),
+            shape((1, LOCAL_HEADS)),
         ]
-        + [shape(rows, bf16)] * 4,
+        + [shape((4, WIDTH, WIDTH), bf16)],
         in_specs=[VMEM] * 6 + [anywhere] * 2 + [VMEM] * 4,
-        out_specs=[VMEM] * 7 + [anywhere] * 4,
+        out_specs=[VMEM] * 7 + [anywhere],
         scratch_shapes=[
             pltpu.VMEM((SEQ, WIDTH), bf16),
             pltpu.VMEM((WIDTH, WIDTH), bf16),
+            pltpu.VMEM((SEQ, 3 * HEAD_WIDTH), bf16),
+            pltpu.VMEM((SEQ, HEAD_WIDTH), bf16),
             pltpu.VMEM((LOCAL_HEADS, SEQ, SEQ), bf16),
             pltpu.VMEM((TOPK, 128, PAD), bf16),
             pltpu.VMEM((128, WIDTH), f32),
@@ -856,12 +944,16 @@
         + [pltpu.VMEM((2, WIDTH, WIDTH), bf16)] * 2
         + [pltpu.VMEM(rows, bf16)] * 4
         + [
+            pltpu.VMEM((4, WIDTH, WIDTH), bf16),
             pltpu.VMEM((SEQ, WIDTH), bf16),
-            pltpu.VMEM((2, 16, 32, WIDTH), bf16),
-            pltpu.VMEM((16, 32, WIDTH), bf16),
-            pltpu.VMEM((16, 32, WIDTH), bf16),
-            pltpu.VMEM((8, WIDTH), f32),
-            pltpu.VMEM((3, 8, WIDTH), f32),
+            pltpu.VMEM((SEQ, 3 * HEAD_WIDTH), bf16),
+            pltpu.VMEM((2, 16, 24, WIDTH), bf16),
+            pltpu.VMEM((16, 24, WIDTH), bf16),
+            pltpu.VMEM((16, 24, WIDTH), bf16),
+            pltpu.VMEM((16, 128), f32),
+            pltpu.VMEM((3, 16, 128), f32),
+            pltpu.VMEM((16, 128), f32),
+            pltpu.VMEM((PLANE, 16, 128), f32),
             dma((2,)),
             dma((4,)),
             dma,
@@ -874,6 +966,8 @@
             dma,
             dma((3,)),
             dma((3,)),
+            dma,
+            dma,
         ]
         + DISPATCH_SCRATCH * 2
         + GATHER_SCRATCH * 2
@@ -884,40 +978,45 @@
     )(*operands)
 
 
-def expert_grad_kernel(rows, grad_pre, hidden, grad_rows, *refs):
-    grad_in, grad_out = refs[-2:]
-    passed = refs[:-2]
-    grad_in[0] = dot_rows(rows[0], grad_pre[0])
-    grad_out[0] = dot_rows(hidden[0], grad_rows[0])
-
-    @pl.when((pl.program_id(0) == 0) & (pl.program_id(1) == 0))
-    def _():
-        for source, target in zip(passed[: len(passed) // 2], passed[len(passed) // 2 :]):
-            target[...] = source[...]
-
-
-def expert_grads(rows, grad_pre, hidden, grad_rows, *small):
-    half = WIDTH // 2
-    whole_rows = pl.BlockSpec((1, EXPERT_ROWS, WIDTH), lambda j, n: (j, 0, 0))
-    half_rows = pl.BlockSpec((1, EXPERT_ROWS, half), lambda j, n: (j, 0, n))
-
-    def still(array):
-        return pl.BlockSpec(array.shape, lambda j, n, rank=array.ndim: (0,) * rank)
-
+def widen_kernel(narrow, *refs):
+    small = (len(refs) - 6) // 2
+    passed, results = refs[:small], refs[small : 2 * small]
+    wide_in, wide_out, held, wide, loads, saves = refs[2 * small :]
+    reads = [
+        pltpu.make_async_copy(narrow.at[i], held.at[i], loads.at[i]) for i in range(4)
+    ]
+    for read in reads:
+        read.start()
+    for source, target in zip(passed, results):
+        target[...] = source[...]
+    writes = []
+    for i in range(4):
+        reads[i].wait()
+        wide[i] = held[i].astype(f32)
+        target = (wide_in, wide_out)[i // 2].at[i % 2]
+        writes.append(pltpu.make_async_copy(wide.at[i], target, saves.at[i]))
+        writes[i].start()
+    for write in writes:
+        write.wait()
+
+
+def widen(narrow, *small):
+    anywhere = pl.BlockSpec(memory_space=pl.ANY)
     grads = jax.ShapeDtypeStruct((2, WIDTH, WIDTH), f32)
     return pl.pallas_call(
-        expert_grad_kernel,
-        grid=(2, 2),
+        widen_kernel,
         out_shape=[jax.ShapeDtypeStruct(a.shape, a.dtype) for a in small] + [grads, grads],
-        in_specs=[whole_rows, half_rows, half_rows, whole_rows] + [still(a) for a in small],
-        out_specs=[still(a) for a in small]
-        + [
-            pl.BlockSpec((1, WIDTH, half), lambda j, n: (j, 0, n)),
-            pl.BlockSpec((1, half, WIDTH), lambda j, n: (j, n, 0)),
+        in_specs=[anywhere] + [VMEM] * len(small),
+        out_specs=[VMEM] * len(small) + [anywhere] * 2,
+        scratch_shapes=[
+            pltpu.VMEM((4, WIDTH, WIDTH), bf16),
+            pltpu.VMEM((4, WIDTH, WIDTH), f32),
+            pltpu.SemaphoreType.DMA((4,)),
+            pltpu.SemaphoreType.DMA((4,)),
         ],
-        compiler_params=pltpu.CompilerParams(vmem_limit_bytes=48 * 1024 * 1024),
-        name="expert_grads",
-    )(rows, grad_pre, hidden, grad_rows, *small)
+        compiler_params=pltpu.CompilerParams(vmem_limit_bytes=60 * 1024 * 1024),
+        name="widen",
+    )(narrow, *small)
 
 
 def body(
@@ -948,9 +1047,8 @@
         bucket_table.reshape(4, 128),
         cotangent,
     )
-    rows, hidden, grad_pre, grad_rows = results[7:]
-    out, grad_input, qkv_grad, proj_grad, gain_first, gain_second, table, grad_in, grad_out = (
-        expert_grads(rows, grad_pre, hidden, grad_rows, *results[:7])
+    out, grad_input, qkv_grad, proj_grad, gain_first, gain_second, table, grad_in, grad_out = widen(
+        results[7], *results[:7]
     )
     return (
         out,
@@ -959,7 +1057,7 @@
         gain_second[0],
         qkv_grad.transpose(1, 0, 2),
         proj_grad.T,
-        table.T,
+        table,
         grad_in,
         grad_out,
     )

time: 157 us -> 139 us (0.89)
  Pallas kernels: 147 us -> 137 us
  local copies, waits for them, and re-layouts: 8.62 us -> 0 us
    unnamed x18 -> x0, local copies, waits for them, and re-layouts: 8.62 us -> none
    pallas_call x1, Pallas kernels: 138 us -> 130 us  [run_layer(): pl.pallas_call(layer_kernel, out_shape=[shape((128, WIDTH), bf16), shape(...]
    pallas_call x1, Pallas kernels: 9.08 us -> 7.13 us  [widen(): pl.pallas_call(widen_kernel, out_shape=[jax.ShapeDtypeStruct(a.shape, a.d...]
where the time goes in v4:
time: 139 us; the launch traced here: 138 us
  Pallas kernels  137 us (99%)
    pallas_call x1, Pallas kernels, run_layer(): pl.pallas_call(layer_kernel, out_shape=[shape((128, WIDTH), bf16), shape(...  130 us
    pallas_call x1, Pallas kernels, widen(): pl.pallas_call(widen_kernel, out_shape=[jax.ShapeDtypeStruct(a.shape, a.d...  7.13 us

profile of v4, /device:TPU:0, one launch (start us, length us, event | category | flops | bytes accessed | tf_op | source)
XLA Modules:
  0.0 137.6 jit_solution(9806596750460761608)
XLA Ops:
  0.6 129.6 %layer.1 = (bf16[128,768]{1,0:T(8,128)(2,1)}, f32[128,768]{1,0:T(8,128)}, f32[3,24,192]{2,1,0:T(8,128)}, f32[24,192]{1,0:T(8,128)}, f32[1,6]{1,0:T(1,128)}, /*in...) custom-call(bf16[128,768]{1,0:T(8,128)(2,1)} %tokens.1, f32[6,128]{1,0:T(8,128)} %bitcast.14, ...), custom_call_target="tpu_custom_call" | custom-call | tf_op jit(solution)/shard_map/layer/pallas_call | solution.py:917
  130.2 7.1 %widen.1 = (bf16[128,768]{1,0:T(8,128)(2,1)}, f32[128,768]{1,0:T(8,128)}, f32[3,24,192]{2,1,0:T(8,128)}, f32[24,192]{1,0:T(8,128)}, f32[1,6]{1,0:T(1,128)}, /*in...) custom-call(bf16[4,768,768]{2,1,0:T(8,128)(2,1)} %get-tuple-element.26.narrow, ...), custom_call_target="tpu_custom_call" | custom-call | tf_op jit(solution)/shard_map/widen/pallas_call | solution.py:1006

commit v5 on v4

--- a/solution.py
+++ b/solution.py
@@ -17,11 +17,13 @@
 
 
 MESH = pl.DeviceIdType.MESH
-BLOCK = 16
+BLOCK = 24
+NARROW = 384
 HALF = 80
 PLANE = 32
 RING = 4
 PAD = PLANE * BLOCK
+BLOCKS = (PLANE, BLOCK, NARROW)
 ROWS = 320
 EXPERT_ROWS = 640
 f32 = jnp.float32
@@ -47,8 +49,21 @@
     return lax.rem(y + 4 - dy, 4) * 8 + lax.rem(x + 4 - dx, 4) * 2 + lax.rem(c + dc, 2)
 
 
-def block_at(index):
-    return pl.ds(pl.multiple_of(index * BLOCK, BLOCK), BLOCK)
+def fold(rows):
+    return jnp.concatenate([rows[:, :NARROW], rows[:, NARROW:]], axis=0)
+
+
+def unfold(rows):
+    half = rows.shape[0] // 2
+    return jnp.concatenate([rows[:half], rows[half:]], axis=1)
+
+
+def as_blocks(rows):
+    return rows.reshape(rows.shape[0] // BLOCK, BLOCK, NARROW).astype(bf16)
+
+
+def from_blocks(blocks):
+    return blocks.astype(f32).reshape(blocks.shape[0] * BLOCK, NARROW).astype(bf16)
 
 
 def greet(plane, ring, across=0):
@@ -89,13 +104,15 @@
 
 
 def packer():
-    row = lax.broadcasted_iota(jnp.int32, (2 * HALF, 256), 0)
-    col = lax.broadcasted_iota(jnp.int32, (2 * HALF, 256), 1)
-    expert = (row >= HALF).astype(jnp.int32)
-    inner = row - expert * HALF
+    row = lax.broadcasted_iota(jnp.int32, (4 * HALF, 16 * BLOCK), 0)
+    col = lax.broadcasted_iota(jnp.int32, (4 * HALF, 16 * BLOCK), 1)
+    side = (row >= 2 * HALF).astype(jnp.int32)
+    rest = row - side * 2 * HALF
+    expert = (rest >= HALF).astype(jnp.int32)
+    inner = rest - expert * HALF
     source = (inner * 205) // 1024
     slot = inner - source * 5
-    return (col == source * BLOCK + expert * 5 + slot).astype(bf16)
+    return (col == source * BLOCK + side * 10 + expert * 5 + slot).astype(bf16)
 
 
 class Dispatch:
@@ -115,8 +132,8 @@
         def send(d, carry):
             other = plane_target(e, d)
             pltpu.make_async_remote_copy(
-                self.send.at[block_at(other)],
-                self.landed.at[block_at(d)],
+                self.send.at[other],
+                self.landed.at[d],
                 self.plane_out.at[half],
                 self.plane_in.at[half],
                 device_id=(other, z),
@@ -126,10 +143,10 @@
 
         lax.fori_loop(max(1, 16 * half), 16 * half + 16, send, 0)
         if half == 0:
-            self.landed[0:BLOCK] = self.send[block_at(e)]
+            self.landed[0] = self.send[e]
 
     def crossed(self, half):
-        drain(self.send.at[pl.ds(0, (15 + half) * BLOCK)], self.plane_out.at[half])
+        drain(self.send.at[pl.ds(0, 15 + half)], self.plane_out.at[half])
 
     def copy(self, index, source, target, other):
         e = lax.axis_index("expert")
@@ -157,10 +174,8 @@
         ]
 
     def turn(self, half, pack):
-        lo = 256 * half
-        span = self.landed.at[pl.ds(lo + (BLOCK if half == 0 else 0), 256 - (BLOCK if half == 0 else 0))]
-        drain(span, self.plane_in.at[half])
-        packed = dot(pack, self.landed[lo : lo + 256]).astype(bf16)
+        drain(self.landed.at[pl.ds(15 * half + 1, 15 + half)], self.plane_in.at[half])
+        packed = unfold(dot(pack, from_blocks(self.landed[16 * half : 16 * half + 16]))).astype(bf16)
         for j in range(2):
             self.rows[j, half * HALF : half * HALF + HALF] = packed[j * HALF : j * HALF + HALF]
         ring = self.copies()
@@ -257,12 +272,12 @@
                 ).astype(bf16)
             )
         flat = jnp.concatenate([total[0], total[1]], axis=0)
-        self.spread[256 * half : 256 * half + 256] = dot_rows(pack, flat).astype(bf16)
+        self.spread[16 * half : 16 * half + 16] = as_blocks(dot_rows(pack, fold(flat)))
 
         def send(d, carry):
             pltpu.make_async_remote_copy(
-                self.spread.at[block_at(d)],
-                self.home.at[block_at(e)],
+                self.spread.at[d],
+                self.home.at[e],
                 self.plane_out,
                 self.plane_in,
                 device_id=(plane_source(e, d), z),
@@ -272,22 +287,22 @@
 
         lax.fori_loop(max(1, 16 * half), 16 * half + 16, send, 0)
         if half == 0:
-            self.home[block_at(e)] = self.spread[0:BLOCK]
+            self.home[e] = self.spread[0]
 
     def arrive(self):
-        drain(self.home.at[pl.ds(0, (PLANE - 1) * BLOCK)], self.plane_in)
+        drain(self.home.at[pl.ds(0, PLANE - 1)], self.plane_in)
 
     def close(self):
         for copy in self.copies(0) + self.copies(1):
             copy.wait_send()
-        drain(self.spread.at[pl.ds(0, (PLANE - 1) * BLOCK)], self.plane_out)
+        drain(self.spread.at[pl.ds(0, PLANE - 1)], self.plane_out)
 
 
 RETURN_SCRATCH = [
     pltpu.VMEM((2, 2, HALF, 768), bf16),
     pltpu.VMEM((12, HALF, 768), bf16),
-    pltpu.VMEM((PAD, 768), bf16),
-    pltpu.VMEM((PAD, 768), bf16),
+    pltpu.VMEM(BLOCKS, bf16),
+    pltpu.VMEM(BLOCKS, bf16),
     pltpu.SemaphoreType.DMA((12,)),
     pltpu.SemaphoreType.DMA((12,)),
     pltpu.SemaphoreType.DMA,
@@ -512,7 +527,10 @@
         slot = jnp.sum(before * hot[c], axis=1, keepdims=True).astype(jnp.int32)
         own = ids[:, c : c + 1]
         first = own // 2
-        picks.append((pos == first * BLOCK + (own - first * 2) * 5 + slot).astype(bf16))
+        base = first * BLOCK + (own - first * 2) * 5 + slot
+        picks.append(
+            jnp.concatenate([(pos == base).astype(bf16), (pos == base + 10).astype(bf16)], axis=0)
+        )
     return picks
 
 
@@ -586,10 +604,10 @@
     for c in range(TOPK):
         picked[c] = picks[c]
     grad_out = cotangent[...].astype(f32)
-    g_send[...] = (
-        dot_rows(picks[0], (gate_columns[0] * grad_out).astype(bf16))
-        + dot_rows(picks[1], (gate_columns[1] * grad_out).astype(bf16))
-    ).astype(bf16)
+    g_send[...] = as_blocks(
+        dot_rows(picks[0], fold((gate_columns[0] * grad_out).astype(bf16)))
+        + dot_rows(picks[1], fold((gate_columns[1] * grad_out).astype(bf16)))
+    )
     grads = Dispatch(g_send, g_landed, g_rows, g_sems)
     unit_ring.relay()
     far_row = lax.broadcasted_iota(jnp.int32, (SEQ, SEQ), 0)
@@ -669,7 +687,9 @@
     resid[...] = residual
     scale_m = rms_scale(residual)
     normal_m = residual * scale_m
-    x_send[...] = dot_rows(picks[0] + picks[1], (normal_m * gain_m).astype(bf16)).astype(bf16)
+    x_send[...] = as_blocks(
+        dot_rows(picks[0] + picks[1], fold((normal_m * gain_m).astype(bf16)))
+    )
 
     out_way = Dispatch(x_send, x_landed, x_rows, x_sems)
     home_way = Return(grad_part, back_x[0], back_x[1], back_x[2], back_x[3], back_x[4:])
@@ -726,7 +746,7 @@
         )
         saves[index].start()
     home_way.arrive()
-    grad_normed = dot(picked[0] + picked[1], home_way.home[...])
+    grad_normed = unfold(dot(picked[0] + picked[1], from_blocks(home_way.home[...])))
     gain_m_part = jnp.sum(grad_normed * normal_m, axis=0, keepdims=True)
     grad_unit_m = grad_normed * gain_m
     grad_resid = grad_out + scale_m * (
@@ -822,7 +842,6 @@
     ]
     for share in shares:
         share.start()
-    input_sum.add_far()
     sibling.wait_recv()
     near_blocks[...] = (blocks[core].astype(f32) + near_blocks[...].astype(f32)).astype(bf16)
     plane_sends(
@@ -832,6 +851,7 @@
         lambda own: p_recv,
     )
     plane_landed[chip] = near_blocks[chip]
+    input_sum.add_far()
     for share in shares:
         share.wait_recv()
     own_small = small_own[...]
@@ -854,9 +874,11 @@
     lax.fori_loop(1, PLANE, spread_small, 0)
     small_plane[0] = small_sum[...]
     y_way.arrive()
-    home = y_way.home[...]
+    home = from_blocks(y_way.home[...])
     out[...] = (
-        resid[...] + gate_columns[0] * dot(picked[0], home) + gate_columns[1] * dot(picked[1], home)
+        resid[...]
+        + gate_columns[0] * unfold(dot(picked[0], home))
+        + gate_columns[1] * unfold(dot(picked[1], home))
     ).astype(bf16)
     scale_first = rms_scale(inputs)
     normal_first = inputs * scale_first
@@ -934,13 +956,13 @@
             pltpu.VMEM((SEQ, 3 * HEAD_WIDTH), bf16),
             pltpu.VMEM((SEQ, HEAD_WIDTH), bf16),
             pltpu.VMEM((LOCAL_HEADS, SEQ, SEQ), bf16),
-            pltpu.VMEM((TOPK, 128, PAD), bf16),
+            pltpu.VMEM((TOPK, 256, PAD), bf16),
             pltpu.VMEM((128, WIDTH), f32),
             pltpu.VMEM((24, WIDTH), bf16),
             pltpu.VMEM((2, 16, 24, WIDTH), bf16),
             pltpu.VMEM((WIDTH, WIDTH), f32),
         ]
-        + [pltpu.VMEM((PAD, WIDTH), bf16), pltpu.VMEM((PAD, WIDTH), bf16), pltpu.VMEM(rows, bf16)] * 2
+        + [pltpu.VMEM(BLOCKS, bf16), pltpu.VMEM(BLOCKS, bf16), pltpu.VMEM(rows, bf16)] * 2
         + [pltpu.VMEM((2, WIDTH, WIDTH), bf16)] * 2
         + [pltpu.VMEM(rows, bf16)] * 4
         + [
@@ -979,16 +1001,21 @@
 
 
 def widen_kernel(narrow, *refs):
-    small = (len(refs) - 6) // 2
-    passed, results = refs[:small], refs[small : 2 * small]
-    wide_in, wide_out, held, wide, loads, saves = refs[2 * small :]
-    reads = [
-        pltpu.make_async_copy(narrow.at[i], held.at[i], loads.at[i]) for i in range(4)
-    ]
+    count = (len(refs) - 8) // 3
+    passed, results = refs[:count], refs[count : 2 * count]
+    wide_in, wide_out, held, wide, loads, saves, ins, outs = refs[2 * count : 2 * count + 8]
+    bounced = refs[2 * count + 8 :]
+    reads = [pltpu.make_async_copy(narrow.at[i], held.at[i], loads.at[i]) for i in range(4)]
     for read in reads:
         read.start()
-    for source, target in zip(passed, results):
-        target[...] = source[...]
+    arrive = [
+        pltpu.make_async_copy(passed[i], bounced[i], ins.at[i]) for i in range(count)
+    ]
+    leave = [
+        pltpu.make_async_copy(bounced[i], results[i], outs.at[i]) for i in range(count)
+    ]
+    for copy in arrive:
+        copy.start()
     writes = []
     for i in range(4):
         reads[i].wait()
@@ -996,7 +1023,11 @@
         target = (wide_in, wide_out)[i // 2].at[i % 2]
         writes.append(pltpu.make_async_copy(wide.at[i], target, saves.at[i]))
         writes[i].start()
-    for write in writes:
+        if i == 0:
+            for one, other in zip(arrive, leave):
+                one.wait()
+                other.start()
+    for write in writes + leave:
         write.wait()
 
 
@@ -1006,14 +1037,17 @@
     return pl.pallas_call(
         widen_kernel,
         out_shape=[jax.ShapeDtypeStruct(a.shape, a.dtype) for a in small] + [grads, grads],
-        in_specs=[anywhere] + [VMEM] * len(small),
-        out_specs=[VMEM] * len(small) + [anywhere] * 2,
+        in_specs=[anywhere] * (1 + len(small)),
+        out_specs=[anywhere] * (len(small) + 2),
         scratch_shapes=[
             pltpu.VMEM((4, WIDTH, WIDTH), bf16),
             pltpu.VMEM((4, WIDTH, WIDTH), f32),
             pltpu.SemaphoreType.DMA((4,)),
             pltpu.SemaphoreType.DMA((4,)),
-        ],
+            pltpu.SemaphoreType.DMA((len(small),)),
+            pltpu.SemaphoreType.DMA((len(small),)),
+        ]
+        + [pltpu.VMEM(a.shape, a.dtype) for a in small],
         compiler_params=pltpu.CompilerParams(vmem_limit_bytes=60 * 1024 * 1024),
         name="widen",
     )(narrow, *small)

time: 139 us -> 134 us (0.964)
  Pallas kernels: 137 us -> 132 us
    pallas_call x1, Pallas kernels: 130 us -> 126 us  [run_layer(): pl.pallas_call(layer_kernel, out_shape=[shape((128, WIDTH), bf16), shape(...]
where the time goes in v5:
time: 134 us; the launch traced here: 133 us
  Pallas kernels  132 us (99%)
    pallas_call x1, Pallas kernels, run_layer(): pl.pallas_call(layer_kernel, out_shape=[shape((128, WIDTH), bf16), shape(...  126 us
    pallas_call x1, Pallas kernels, widen(): pl.pallas_call(widen_kernel, out_shape=[jax.ShapeDtypeStruct(a.shape, a.d...  6.01 us

profile of v5, /device:TPU:0, one launch (start us, length us, event | category | flops | bytes accessed | tf_op | source)
XLA Modules:
  0.0 133.2 jit_solution(17161719633198279701)
XLA Ops:
  0.6 126.4 %layer.1 = (bf16[128,768]{1,0:T(8,128)(2,1)}, f32[128,768]{1,0:T(8,128)}, f32[3,24,192]{2,1,0:T(8,128)}, f32[24,192]{1,0:T(8,128)}, f32[1,6]{1,0:T(1,128)}, /*in...) custom-call(bf16[128,768]{1,0:T(8,128)(2,1)} %tokens.1, f32[6,128]{1,0:T(8,128)} %bitcast.14, ...), custom_call_target="tpu_custom_call" | custom-call | tf_op jit(solution)/shard_map/layer/pallas_call | solution.py:939
  127.0 6.0 %widen.1 = (bf16[128,768]{1,0:T(8,128)(2,1)}, f32[128,768]{1,0:T(8,128)}, f32[3,24,192]{2,1,0:T(8,128)}, f32[24,192]{1,0:T(8,128)}, f32[1,6]{1,0:T(1,128)}, /*in...) custom-call(bf16[4,768,768]{2,1,0:T(8,128)(2,1)} %get-tuple-element.26.narrow, ...), custom_call_target="tpu_custom_call" | custom-call | tf_op jit(solution)/shard_map/widen/pallas_call | solution.py:1037

commit v6 on v5

--- a/solution.py
+++ b/solution.py
@@ -545,10 +545,12 @@
 
 
 def layer_kernel(
-    tokens, gain_attn, gain_moe, qkv_weight, proj_weight, bias, weight_in, weight_out,
-    ids, gates, buckets, cotangent,
+    tokens_hbm, qkv_hbm, proj_hbm, gain_attn_hbm, gain_moe_hbm, bias_hbm,
+    ids_hbm, gates_hbm, buckets_hbm, cotangent_hbm, weight_in, weight_out,
     out, grad_input, qkv_grad, proj_grad, gain_first, gain_second, table_out,
     grads_hbm,
+    tokens, qkv_weight, proj_weight, gain_attn, gain_moe, bias,
+    ids, gates, buckets, cotangent, input_sems,
     units, whole, qkv, attended, probs, picked, resid, mine, wall, whole32,
     x_send, x_landed, x_rows, g_send, g_landed, g_rows,
     held_in, held_out, hidden, grad_pre, grad_part, y_part, expert_grads,
@@ -564,13 +566,32 @@
     core, chip = lax.rem(e, 2), e // 2
     twin = chip * 2 + 1 - core
     opposite = lax.rem(z + 2, RING)
+    inputs_in = [
+        pltpu.make_async_copy(source, target, input_sems.at[index])
+        for index, (source, target) in enumerate(
+            (
+                (tokens_hbm, tokens),
+                (qkv_hbm, qkv_weight),
+                (proj_hbm, proj_weight),
+                (gain_attn_hbm, gain_attn),
+                (gain_moe_hbm, gain_moe),
+                (bias_hbm, bias),
+                (ids_hbm, ids),
+                (gates_hbm, gates),
+                (buckets_hbm, buckets),
+                (cotangent_hbm, cotangent),
+            )
+        )
+    ]
     loads = [
         pltpu.make_async_copy(weight_in, held_in, load_sems.at[0]),
         pltpu.make_async_copy(weight_out, held_out, load_sems.at[1]),
     ]
-    for load in loads:
+    arrivals = greet(1, 1, 1)
+    for load in inputs_in + loads:
         load.start()
-    arrivals = greet(1, 1, 1)
+    for load in inputs_in[:3]:
+        load.wait()
 
     mine[...] = jnp.concatenate(
         [qkv_weight[i].astype(f32) for i in range(3)] + [proj_weight[...].astype(f32)], axis=1
@@ -595,6 +616,8 @@
         )
 
     pass_on(chip).start()
+    for load in inputs_in[3:]:
+        load.wait()
     gain_a, gain_m = as_row(gain_attn[...]), as_row(gain_moe[...])
     id_columns = jnp.concatenate(
         [as_column(ids[c : c + 1].astype(f32)) for c in range(TOPK)], axis=1
@@ -796,27 +819,40 @@
     grad_ring.land(4)
     grad_ring.land(5)
     attend_back(3)
+    def pair(side, full):
+        for block in range(PLANE):
+            blocks[side, block % 2, block // 2] = full[24 * block : 24 * block + 24].astype(bf16)
+        exchange = pltpu.make_async_remote_copy(
+            blocks.at[side, 1 - core],
+            near_blocks.at[side],
+            v_send.at[side],
+            v_recv.at[side],
+            device_id=(twin, z),
+            device_id_type=MESH,
+        )
+        exchange.start()
+        return exchange
+
+    def spread_pair(side, exchange):
+        exchange.wait_recv()
+        near_blocks[side] = (
+            blocks[side, core].astype(f32) + near_blocks[side].astype(f32)
+        ).astype(bf16)
+        plane_sends(
+            lambda other: near_blocks.at[side, other],
+            lambda own: plane_landed.at[side, own],
+            p_send.at[side],
+            lambda own: p_recv.at[side],
+        )
+        plane_landed[side, chip] = near_blocks[side, chip]
+
+    query_part = dot_rows(normed, grad_qkv[:, :HEAD_WIDTH])
+    pairs = [pair(0, jnp.concatenate([query_part, carried[2]], axis=1))]
     grad_qkv[:, HEAD_WIDTH:] = jnp.concatenate(
         [carried[0] * score_scale, carried[1]], axis=1
     ).astype(bf16)
-    proj_part = carried[2]
-    full = jnp.concatenate([dot_rows(normed, grad_qkv[...]), proj_part], axis=1)
-    for block in range(PLANE):
-        blocks[block % 2, block // 2] = full[24 * block : 24 * block + 24].astype(bf16)
-    sibling = pltpu.make_async_remote_copy(
-        blocks.at[1 - core],
-        near_blocks,
-        v_send,
-        v_recv,
-        device_id=(twin, z),
-        device_id_type=MESH,
-    )
-    sibling.start()
+    pairs.append(pair(1, dot_rows(normed, grad_qkv[:, HEAD_WIDTH:])))
     grad_normed_a = dot_cols(grad_qkv[...], whole[:, : 3 * HEAD_WIDTH])
-    sum_b[0][...] = grad_normed_a.astype(bf16)
-    input_sum = RingSum(sum_b[0], sum_b[1], sum_b[2], sum_b[3:])
-    for index in range(4):
-        input_sum.send(index)
     gain_part = jnp.sum(grad_normed_a * unit_rows, axis=0, keepdims=True)
     diagonal = jnp.concatenate(diagonals + [jnp.zeros((5, SEQ), f32)], axis=0)
     table_rows = lax.dot_general(
@@ -842,15 +878,12 @@
     ]
     for share in shares:
         share.start()
-    sibling.wait_recv()
-    near_blocks[...] = (blocks[core].astype(f32) + near_blocks[...].astype(f32)).astype(bf16)
-    plane_sends(
-        lambda other: near_blocks.at[other],
-        lambda own: plane_landed.at[own],
-        p_send,
-        lambda own: p_recv,
-    )
-    plane_landed[chip] = near_blocks[chip]
+    sum_b[0][...] = grad_normed_a.astype(bf16)
+    input_sum = RingSum(sum_b[0], sum_b[1], sum_b[2], sum_b[3:])
+    for index in range(4):
+        input_sum.send(index)
+    spread_pair(0, pairs[0])
+    spread_pair(1, pairs[1])
     input_sum.add_far()
     for share in shares:
         share.wait_recv()
@@ -886,13 +919,17 @@
     grad_input[...] = grad_resid + scale_first * (
         grad_unit - normal_first * jnp.mean(grad_unit * normal_first, axis=1, keepdims=True)
     )
-    drain(plane_landed.at[pl.ds(0, 15)], p_recv)
-    total = plane_landed[0].astype(f32)
-    for block in range(1, 16):
-        total = total + plane_landed[block].astype(f32)
-    for i in range(3):
-        qkv_grad[i] = total[:, i * HEAD_WIDTH : (i + 1) * HEAD_WIDTH]
-    proj_grad[...] = total[:, 3 * HEAD_WIDTH :]
+    totals = []
+    for side in range(2):
+        drain(plane_landed.at[side, pl.ds(0, 15)], p_recv.at[side])
+        total = plane_landed[side, 0].astype(f32)
+        for block in range(1, 16):
+            total = total + plane_landed[side, block].astype(f32)
+        totals.append(total)
+    qkv_grad[0] = totals[0][:, :HEAD_WIDTH]
+    proj_grad[...] = totals[0][:, HEAD_WIDTH:]
+    qkv_grad[1] = totals[1][:, :HEAD_WIDTH]
+    qkv_grad[2] = totals[1][:, HEAD_WIDTH:]
     drain(small_plane.at[pl.ds(1, PLANE - 1)], q_recv)
     summed = jnp.sum(small_plane[...], axis=0)
     column = lax.broadcasted_iota(jnp.int32, (16, 128), 1)
@@ -924,9 +961,11 @@
     grad_ring.close()
     attn_sum.close()
     input_sum.close()
-    sibling.wait_send()
+    for exchange in pairs:
+        exchange.wait_send()
     drain(wall.at[0], s_send)
-    drain(plane_landed.at[pl.ds(0, 15)], p_send)
+    for side in range(2):
+        drain(plane_landed.at[side, pl.ds(0, 15)], p_send.at[side])
 
 
 def run_layer(*operands):
@@ -948,9 +987,11 @@
             shape((1, LOCAL_HEADS)),
         ]
         + [shape((4, WIDTH, WIDTH), bf16)],
-        in_specs=[VMEM] * 6 + [anywhere] * 2 + [VMEM] * 4,
+        in_specs=[anywhere] * 12,
         out_specs=[VMEM] * 7 + [anywhere],
-        scratch_shapes=[
+        scratch_shapes=[pltpu.VMEM(a.shape, a.dtype) for a in operands[:10]]
+        + [
+            dma((10,)),
             pltpu.VMEM((SEQ, WIDTH), bf16),
             pltpu.VMEM((WIDTH, WIDTH), bf16),
             pltpu.VMEM((SEQ, 3 * HEAD_WIDTH), bf16),
@@ -969,9 +1010,9 @@
             pltpu.VMEM((4, WIDTH, WIDTH), bf16),
             pltpu.VMEM((SEQ, WIDTH), bf16),
             pltpu.VMEM((SEQ, 3 * HEAD_WIDTH), bf16),
-            pltpu.VMEM((2, 16, 24, WIDTH), bf16),
-            pltpu.VMEM((16, 24, WIDTH), bf16),
-            pltpu.VMEM((16, 24, WIDTH), bf16),
+            pltpu.VMEM((2, 2, 16, 24, NARROW), bf16),
+            pltpu.VMEM((2, 16, 24, NARROW), bf16),
+            pltpu.VMEM((2, 16, 24, NARROW), bf16),
             pltpu.VMEM((16, 128), f32),
             pltpu.VMEM((3, 16, 128), f32),
             pltpu.VMEM((16, 128), f32),
@@ -982,10 +1023,10 @@
             dma((16,)),
             dma,
             dma,
-            dma,
-            dma,
-            dma,
-            dma,
+            dma((2,)),
+            dma((2,)),
+            dma((2,)),
+            dma((2,)),
             dma((3,)),
             dma((3,)),
             dma,
@@ -1069,17 +1110,17 @@
 ):
     results = run_layer(
         tokens,
+        qkv_weight.transpose(1, 0, 2),
+        proj_weight.T,
         gain_attn.reshape(6, 128),
         gain_moe.reshape(6, 128),
-        qkv_weight.transpose(1, 0, 2),
-        proj_weight.T,
         bias_table.T,
-        expert_in,
-        expert_out,
         expert_ids.T,
         gate_values.T,
         bucket_table.reshape(4, 128),
         cotangent,
+        expert_in,
+        expert_out,
     )
     out, grad_input, qkv_grad, proj_grad, gain_first, gain_second, table, grad_in, grad_out = widen(
         results[7], *results[:7]

time: 134 us -> 133 us (level)
    pallas_call x1, Pallas kernels: 126 us -> 125 us  [run_layer(): pl.pallas_call(layer_kernel, out_shape=[shape((128, WIDTH), bf16), shape(...]
where the time goes in v6:
time: 133 us; the launch traced here: 132 us
  Pallas kernels  131 us (98%)
    pallas_call x1, Pallas kernels, run_layer(): pl.pallas_call(layer_kernel, out_shape=[shape((128, WIDTH), bf16), shape(...  125 us
    pallas_call x1, Pallas kernels, widen(): pl.pallas_call(widen_kernel, out_shape=[jax.ShapeDtypeStruct(a.shape, a.d...  6.01 us

profile of v6, /device:TPU:0, one launch (start us, length us, event | category | flops | bytes accessed | tf_op | source)
XLA Modules:
  0.0 131.6 jit_solution(17619781526047834850)
XLA Ops:
  0.6 124.8 %layer.1 = (bf16[128,768]{1,0:T(8,128)(2,1)}, f32[128,768]{1,0:T(8,128)}, f32[3,24,192]{2,1,0:T(8,128)}, f32[24,192]{1,0:T(8,128)}, f32[1,6]{1,0:T(1,128)}, /*in...) custom-call(bf16[128,768]{1,0:T(8,128)(2,1)} %tokens_hbm.1, bf16[3,24,192]{2,1,0:T(8,128)(2,1)} %bitcast.12, ...), custom_call_target="tpu_custom_call" | custom-call | tf_op jit(solution)/shard_map/layer/pallas_call | solution.py:978
  125.4 6.0 %widen.1 = (bf16[128,768]{1,0:T(8,128)(2,1)}, f32[128,768]{1,0:T(8,128)}, f32[3,24,192]{2,1,0:T(8,128)}, f32[24,192]{1,0:T(8,128)}, f32[1,6]{1,0:T(1,128)}, /*in...) custom-call(bf16[4,768,768]{2,1,0:T(8,128)(2,1)} %get-tuple-element.26.narrow, ...), custom_call_target="tpu_custom_call" | custom-call | tf_op jit(solution)/shard_map/widen/pallas_call | solution.py:1078
